TPU v7x, 256 devices: a whole 4x4x8 slice. The times are simulated.
256 devices in a mesh: row: 32 (over z_lo, y, core), col: 8 (over x, z_hi).
Axes of the slice: x: 4, y: 4, z: 8 (z_hi: 2, z_lo: 4; z = z_hi * 4 + z_lo), core: 2. Of those that a mesh axis runs over, the one named last changes fastest.
Arguments:
- queries: bfloat16 [32768, 128], P(('col', 'row')), may hold values from -4 to 4
- keys: bfloat16 [61440, 128], P(('row', 'col')), may hold values from -4 to 4
- values: bfloat16 [61440, 128], P(('row', 'col')), may hold values from -6 to 6
- outputs: bfloat16 [32768, 128], P(('col', 'row')), may hold values from -6 to 6
- out_grad: bfloat16 [32768, 128], P(('col', 'row')), may hold values from -96 to 96
- lse: float32 [32768], P(('col', 'row')), as said below
Outputs:
- grad_queries: float32 [32768, 128], P(('col', 'row'))
- grad_keys: float32 [61440, 128], P(('row', 'col'))
- grad_values: float32 [61440, 128], P(('row', 'col'))
Inputs may be any that keep to these rules, and one draw needn't show every extreme that they name: `lse`: each value is the natural logarithm of 61440 plus a number between 0.05 and 0.9.
All inputs are finite; a program needn't handle non-finite values.
Results may differ from a plain program's by a relative error of at most 0.0029.
Values may be sent and summed in bfloat16 or wider, within the bound.
No kernel may reach another device: no remote copies, remote signals or barrier semaphores. Data moves between devices by JAX's collectives and lax.ppermute only.
A program may use at most 64 MiB of HBM per device.

v0:
```python
import math

import jax
import jax.numpy as jnp
from jax import lax
from jax.experimental import pallas as pl
from jax.experimental.pallas import tpu as pltpu
from jax.sharding import Mesh, PartitionSpec as P

W = 128
T = 240
QP = 2 * W + 16
BF, F32 = jnp.bfloat16, jnp.float32
FACTOR = 1.0 / math.sqrt(W)
LOG2E = math.log2(math.e)
NT = (((1,), (1,)), ((), ()))
NN = (((1,), (0,)), ((), ()))
TN = (((0,), (0,)), ((), ()))
VM = pl.BlockSpec(memory_space=pltpu.VMEM)
ANY = pl.BlockSpec(memory_space=pl.ANY)


def dot(a, b, dims):
    return lax.dot_general(a, b, dims, preferred_element_type=F32)


def call(kernel, name, outs, args, flops=0, aliases=None, spaces=None, scratch=(), vmem=40):
    nbytes = sum(math.prod(a.shape) * a.dtype.itemsize for a in list(outs) + list(args))
    return pl.pallas_call(
        kernel,
        name=name,
        out_shape=outs,
        in_specs=spaces or [VM] * len(args),
        out_specs=tuple([VM] * len(outs)),
        input_output_aliases=aliases or {},
        scratch_shapes=list(scratch),
        compiler_params=pltpu.CompilerParams(vmem_limit_bytes=vmem * 2**20),
        cost_estimate=pl.CostEstimate(flops=flops, bytes_accessed=nbytes, transcendentals=0),
    )(*args)


def sds(shape, dtype):
    return jax.ShapeDtypeStruct(shape, dtype)


def pack_kernel(q, g, o, lse, k, v, qp, kv, obuf, lbuf, sems):
    copies = [
        pltpu.make_async_copy(src, dst, sems.at[n])
        for n, (src, dst) in enumerate(
            (
                (g, qp.at[pl.ds(W, W), :]),
                (o, obuf),
                (lse, lbuf),
                (q, qp.at[pl.ds(0, W), :]),
                (k, kv.at[pl.ds(0, T), :]),
                (v, kv.at[pl.ds(T, T), :]),
            )
        )
    ]
    for copy in copies:
        copy.start()
    for copy in copies:
        copy.wait()
    prod = qp[W : 2 * W, :].astype(F32) * obuf[...].astype(F32)
    delta = jnp.sum(prod.T, axis=0, keepdims=True)
    rows = []
    for x in (lbuf[...] * LOG2E, delta):
        for _ in range(3):
            part = x.astype(BF).astype(F32)
            rows.append(part)
            x = x - part
    rows.append(jnp.zeros((10, W), F32))
    qp[2 * W :, :] = jnp.concatenate(rows, axis=0).astype(BF)


SHARDS = (
    [(0, i) for i in range(4)],
    [(1, i) for i in range(4)],
    [(2, i) for i in range(4)],
    [(1, 4), (1, 5), (2, 4), (2, 5)],
)


def chunk_kernel(first, chip, mine, sib, kv, *rest):
    if first:
        out, gc, gm, gs = rest
        acc_in = None
    else:
        acc_in, (out, gc, gm, gs) = rest[:3], rest[-4:]
    qrefs, accs = (chip, mine, sib), (gc, gm, gs)
    ks = jnp.concatenate([kv[i, 0:T, :] for i in range(4)], axis=0)
    vs = jnp.concatenate([kv[i, T:, :] for i in range(4)], axis=0)
    gk = gv = None
    for mem in SHARDS:
        q = jnp.concatenate([qrefs[r][i, 0:W, :] for r, i in mem], axis=0)
        g = jnp.concatenate([qrefs[r][i, W : 2 * W, :] for r, i in mem], axis=0)
        stat = jnp.concatenate([qrefs[r][i, 2 * W :, :].astype(F32) for r, i in mem], axis=1)
        l2 = stat[0:1] + stat[1:2] + stat[2:3]
        delta = stat[3:4] + stat[4:5] + stat[5:6]
        p = jnp.exp2(dot(ks, q, NT) * (FACTOR * LOG2E) - l2)
        ds = (p * (dot(vs, g, NT) - delta)).astype(BF)
        dv = dot(p.astype(BF), g, NN)
        dk = dot(ds, q, NN)
        gv = dv if gv is None else gv + dv
        gk = dk if gk is None else gk + dk
        u = dot(ks, ds, TN)
        for n, (r, i) in enumerate(mem):
            part = u[:, n * W : (n + 1) * W]
            accs[r][i] = part if first else acc_in[r][i] + part
    for i in range(4):
        rows = slice(i * T, (i + 1) * T)
        out[i, 0:T, :] = gk[rows].astype(out.dtype)
        out[i, T:, :] = gv[rows].astype(out.dtype)


def chunk(name, chip, mine, sib, kv, acc, dtype, after=()):
    outs = (sds((4, 2 * T, W), dtype), sds((4, W, W), F32), sds((6, W, W), F32), sds((6, W, W), F32))
    args = (chip, mine, sib, kv)
    aliases = {}
    if acc is not None:
        args += acc
        aliases = {4: 1, 5: 2, 6: 3}
    spaces = [VM] * len(args) + [ANY] * len(after)

    def kernel(*refs):
        chunk_kernel(acc is None, *refs)

    out = call(kernel, name, outs, args + tuple(after), 10 * 960 * 2048 * W, aliases, spaces)
    return out[0], tuple(out[1:])


def merge_kernel(own, b1, b2, b3, *outs):
    for r in range(4):
        total = own[r]
        for other in (b1, b2, b3):
            total = total + other[r].astype(F32)
        outs[r][...] = total.astype(outs[r].dtype)


def halves_kernel(gm, rs, after, m1, m2):
    m1[...] = (gm[0:4] + rs[0:4]).astype(BF)
    m2[...] = (gm[4:6] + rs[4:6]).astype(BF)


def rows_kernel(gc, u1, u2, own, other):
    own[...] = gc[0:2] + u1[0:2].astype(F32) + u2[...].astype(F32)
    other[...] = gc[2:4] + u1[2:4].astype(F32)


def pair_kernel(own, got, near, far):
    near[...] = own[0] + got[0]
    far[...] = own[1] + got[1]


def last_kernel(near, far, own, f1, f2, f3, gq, gk, gv):
    gq[...] = (near[...] + far[...]).T * FACTOR
    total = own[...] + f1[...].astype(F32) + f2[...].astype(F32) + f3[...].astype(F32)
    gk[...] = total[0:T] * FACTOR
    gv[...] = total[T:]


SWAP = [(0, 1), (1, 0)]
FAR = [(0, 1), (1, 0)]


def swap_cores(x):
    return lax.ppermute(x, "core", SWAP)


def swap_halves(x):
    return lax.ppermute(x, "zh", FAR)


def send_z(x, s):
    index = lambda z, c: (z % 4) * 4 + c * 2 + z // 4
    pairs = [
        (index(z, c), index((z + (s if c == 0 else -s)) % 8, c)) for z in range(8) for c in range(2)
    ]
    return lax.ppermute(x, ("zl", "core", "zh"), pairs)


def send_plane(x, s, core_on_x):
    pairs = []
    for y in range(4):
        for c in range(2):
            for i in range(4):
                to_y, to_x = (y, (i + s) % 4) if c == core_on_x else ((y + s) % 4, i)
                pairs.append(((y * 2 + c) * 4 + i, (to_y * 2 + c) * 4 + to_x))
    return lax.ppermute(x, ("y", "core", "x"), pairs)


def local(queries, keys, values, outputs, out_grad, lse):
    qp, kv = call(
        pack_kernel,
        "pack",
        (sds((QP, W), BF), sds((2 * T, W), BF)),
        (queries, out_grad, outputs, lse.reshape(1, W), keys, values),
        spaces=[ANY] * 6,
        scratch=(pltpu.VMEM((W, W), BF), pltpu.VMEM((1, W), F32), pltpu.SemaphoreType.DMA((6,))),
        vmem=60,
    )
    pair = jnp.stack([qp, swap_halves(qp)])
    chip = jnp.concatenate([pair, swap_cores(pair)])
    mine = jnp.concatenate([send_z(chip, 1), send_z(pair, 2)])
    sib = swap_cores(mine)
    kv0 = jnp.stack([kv] + [send_plane(kv, r, 0) for r in (1, 2, 3)])
    kvs = {s: send_plane(kv0, s, 1) for s in (1, 3, 2)}

    out1, acc = chunk("chunk1", chip, mine, sib, kvs[1], None, BF)
    back1 = send_plane(out1, -1, 1)
    out3, acc = chunk("chunk3", chip, mine, sib, kvs[3], acc, BF)
    back3 = send_plane(out3, -3, 1)
    out2, acc = chunk("chunk2", chip, mine, sib, kvs[2], acc, BF, (back1,))
    back2 = send_plane(out2, -2, 1)
    out0, (gc, gm, gs) = chunk("chunk0", chip, mine, sib, kv0, acc, F32, (back3,))

    rs = swap_cores(gs)
    part0, *parts = call(
        merge_kernel,
        "merge",
        (sds((2 * T, W), F32),) + (sds((2 * T, W), BF),) * 3,
        (out0, back1, back2, back3),
    )
    f1, f2, f3 = (send_plane(parts[r - 1], -r, 0) for r in (1, 2, 3))
    m1, m2 = call(
        halves_kernel,
        "halves",
        (sds((4, W, W), BF), sds((2, W, W), BF)),
        (gm, rs, part0),
        spaces=[VM, VM, ANY],
    )
    u1, u2 = send_z(m1, -1), send_z(m2, -2)
    own, other = call(rows_kernel, "rows", (sds((2, W, W), F32),) * 2, (gc, u1, u2))
    near, far = call(pair_kernel, "pair", (sds((W, W), F32),) * 2, (own, swap_cores(other)))
    return call(
        last_kernel,
        "last",
        (sds((W, W), F32), sds((T, W), F32), sds((T, W), F32)),
        (near, swap_halves(far), part0, f1, f2, f3),
    )


def solution(mesh):
    fine = Mesh(mesh.devices.reshape(4, 4, 2, 4, 2), ("zl", "y", "core", "x", "zh"))
    qs, ks = ("x", "zh", "zl", "y", "core"), ("zl", "y", "core", "x", "zh")
    return jax.shard_map(
        local,
        mesh=fine,
        in_specs=(P(qs, None), P(ks, None), P(ks, None), P(qs, None), P(qs, None), P(qs)),
        out_specs=(P(qs, None), P(ks, None), P(ks, None)),
        check_vma=False,
    )
```

profile of v0, /device:TPU:65, one launch (start us, length us, event | category | flops | bytes accessed | tf_op | source)
XLA Modules:
  0.0 94.5 jit_solution(3339602352413212792)
XLA Ops:
  0.6 1.7 %pack.1 = (bf16[272,128]{1,0:T(8,128)(2,1)}, bf16[480,128]{1,0:T(8,128)(2,1)}) custom-call(bf16[128,128]{1,0:T(8,128)(2,1)} %q.1, bf16[128,128]{1,0:T(8,128)(2,1)} %g.1, bf16[128,128]{1,0:T(8,128)(2,1)} %o.1, f32[1,128]{1,0:T(1,128)} %bitcast.15, bf16[240,128]{1,0:T(8,128)(2,1)} %k.1, bf16[240,128]{1,0:T(8,128)(2,1)} %v.1), custom_call_target="tpu_custom_call" | custom-call | bytes 414208 | tf_op jit(solution)/shard_map/pack/pallas_call | solution.py:29
  2.4 5.2 %collective-permute-start = (bf16[272,128]{1,0:T(8,128)(2,1)}, bf16[272,128]{1,0:T(8,128)(2,1)S(1)}, u32[]{:S(2)}, u32[]{:S(2)}) collective-permute-start(bf16[272,128]{1,0:T(8,128)(2,1)} %get-tuple-element.31), channel_id=1, source_target_pairs={{0,1},{1,0},{2,3},{3,2},{4,5},{5,4},{6,7},{7,6},{8,9},{9,8},{10,11... | collective-permute-start | bytes 208904 | tf_op jit(solution)/shard_map/ppermute | solution.py:171
  7.6 2.9 %collective-permute-done = bf16[272,128]{1,0:T(8,128)(2,1)S(1)} collective-permute-done((bf16[272,128]{1,0:T(8,128)(2,1)}, bf16[272,128]{1,0:T(8,128)(2,1)S(1)}, u32[]{:S(2)}, u32[]{:S(2)}) %collective-permute-start) | collective-permute-done | bytes 69664 | tf_op jit(solution)/shard_map/ppermute | solution.py:171
  10.5 1.0 %pad_maximum_fusion.2 = bf16[2,272,128]{2,1,0:T(8,128)(2,1)S(1)} fusion(bf16[1,272,128]{2,1,0:T(8,128)(2,1)S(1)} %bitcast.9, bf16[1,272,128]{2,1,0:T(8,128)(2,1)} %bitcast.7), kind=kLoop, calls=%fused_computation.2 | loop fusion | flops 69632 | bytes 278528 | tf_op jit(solution)/shard_map/stack | solution.py:202
  11.5 0.0 copy-start.1
  11.5 2.4 %collective-permute-start.1 = (bf16[2,272,128]{2,1,0:T(8,128)(2,1)S(1)}, bf16[2,272,128]{2,1,0:T(8,128)(2,1)S(1)}, u32[]{:S(2)}, u32[]{:S(2)}) collective-permute-start(bf16[2,272,128]{2,1,0:T(8,128)(2,1)S(1)} %pad_maximum_fusion.2), channel_id=1, source_target_pairs={{0,8},{8,0},{1,9},{9,1},{2,10},{10,2},{3,11},{11,3},{4,12},{12,4},... | collective-permute-start | bytes 417800 | tf_op jit(solution)/shard_map/ppermute | solution.py:167
  13.8 1.0 %collective-permute-done.1 = bf16[2,272,128]{2,1,0:T(8,128)(2,1)S(1)} collective-permute-done((bf16[2,272,128]{2,1,0:T(8,128)(2,1)S(1)}, bf16[2,272,128]{2,1,0:T(8,128)(2,1)S(1)}, u32[]{:S(2)}, u32[]{:S(2)}) %collective-permute-start.1) | collective-permute-done | bytes 139296 | tf_op jit(solution)/shard_map/ppermute | solution.py:167
  14.9 0.2 collective-permute-start.2
  15.1 2.7 %collective-permute-start.7 = (bf16[480,128]{1,0:T(8,128)(2,1)S(1)}, bf16[480,128]{1,0:T(8,128)(2,1)S(1)}, u32[]{:S(2)}, u32[]{:S(2)}) collective-permute-start(bf16[480,128]{1,0:T(8,128)(2,1)S(1)} %copy-done.1), channel_id=1, source_target_pairs={{0,6},{2,0},{4,2},{6,4},{8,56},{10,58},{12,60},{14,62},{16,22},{18... | collective-permute-start | bytes 368648 | tf_op jit(solution)/shard_map/ppermute | solution.py:189
  17.8 0.3 collective-permute-start.6
  18.2 0.7 collective-permute-start.5
  18.9 3.7 %collective-permute-start.3 = (bf16[2,272,128]{2,1,0:T(8,128)(2,1)S(1)}, bf16[2,272,128]{2,1,0:T(8,128)(2,1)S(1)}, u32[]{:S(2)}, u32[]{:S(2)}) collective-permute-start(bf16[2,272,128]{2,1,0:T(8,128)(2,1)S(1)} %pad_maximum_fusion.2), channel_id=1, source_target_pairs={{0,128},{8,137},{64,192},{72,201},{128,1},{136,8},{192,65},{200,72... | collective-permute-start | bytes 417800 | tf_op jit(solution)/shard_map/ppermute | solution.py:179
  22.6 0.0 collective-permute-done.7
  22.6 0.6 collective-permute-done.6
  23.2 1.5 %collective-permute-done.5 = bf16[480,128]{1,0:T(8,128)(2,1)S(1)} collective-permute-done((bf16[480,128]{1,0:T(8,128)(2,1)S(1)}, bf16[480,128]{1,0:T(8,128)(2,1)S(1)}, u32[]{:S(2)}, u32[]{:S(2)}) %collective-permute-start.5) | collective-permute-done | bytes 122912 | tf_op jit(solution)/shard_map/ppermute | solution.py:189
  24.7 0.1 pad_maximum_fusion.refs_3_
  24.7 1.0 %collective-permute-start.10 = (bf16[4,480,128]{2,1,0:T(8,128)(2,1)S(1)}, bf16[4,480,128]{2,1,0:T(8,128)(2,1)S(1)}, u32[]{:S(2)}, u32[]{:S(2)}) collective-permute-start(bf16[4,480,128]{2,1,0:T(8,128)(2,1)S(1)} %pad_maximum_fusion.refs_3_), channel_id=1, source_target_pairs={{0,16},{2,18},{4,20},{6,22},{8,10},{10,12},{12,14},{14,8},{16,32},... | collective-permute-start | bytes 1474568 | tf_op jit(solution)/shard_map/ppermute | solution.py:189
  25.7 0.0 collective-permute-done.2
  25.8 0.4 collective-permute-done.3
  26.2 3.2 %collective-permute-start.4 = (bf16[6,272,128]{2,1,0:T(8,128)(2,1)S(1)}, bf16[6,272,128]{2,1,0:T(8,128)(2,1)S(1)}, u32[]{:S(2)}, u32[]{:S(2)}) collective-permute-start(bf16[6,272,128]{2,1,0:T(8,128)(2,1)S(1)} %constant_dynamic-update-slice_fusion.refs_1_), channel_id=1, source_target_pairs={{0,8},{8,0},{1,9},{9,1},{2,10},{10,2},{3,11},{11,3},{4,12},{12,4},... | collective-permute-start | bytes 1253384 | tf_op jit(solution)/shard_map/ppermute | solution.py:167
  29.4 2.1 %collective-permute-start.9 = (bf16[4,480,128]{2,1,0:T(8,128)(2,1)S(1)}, bf16[4,480,128]{2,1,0:T(8,128)(2,1)S(1)}, u32[]{:S(2)}, u32[]{:S(2)}) collective-permute-start(bf16[4,480,128]{2,1,0:T(8,128)(2,1)S(1)} %pad_maximum_fusion.refs_3_), channel_id=1, source_target_pairs={{0,48},{2,50},{4,52},{6,54},{8,14},{10,8},{12,10},{14,12},{16,0},{... | collective-permute-start | bytes 1474568 | tf_op jit(solution)/shard_map/ppermute | solution.py:189
  31.5 1.2 %collective-permute-start.8 = (bf16[4,480,128]{2,1,0:T(8,128)(2,1)S(1)}, bf16[4,480,128]{2,1,0:T(8,128)(2,1)S(1)}, u32[]{:S(2)}, u32[]{:S(2)}) collective-permute-start(bf16[4,480,128]{2,1,0:T(8,128)(2,1)S(1)} %pad_maximum_fusion.refs_3_), channel_id=1, source_target_pairs={{0,32},{2,34},{4,36},{6,38},{8,12},{10,14},{12,8},{14,10},{16,48},... | collective-permute-start | bytes 1474568 | tf_op jit(solution)/shard_map/ppermute | solution.py:189
  32.7 1.3 %collective-permute-done.10.refs_3_ = bf16[4,480,128]{2,1,0:T(8,128)(2,1)S(1)} collective-permute-done((bf16[4,480,128]{2,1,0:T(8,128)(2,1)S(1)}, bf16[4,480,128]{2,1,0:T(8,128)(2,1)S(1)}, u32[]{:S(2)}, u32[]{:S(2)}) %collective-permute-start.10) | collective-permute-done | bytes 491552 | tf_op jit(solution)/shard_map/ppermute | solution.py:189
  34.0 0.0 collective-permute-done.4.refs_2_
  34.0 4.8 %chunk1.1 = (bf16[4,480,128]{2,1,0:T(8,128)(2,1)S(1)}, f32[4,128,128]{2,1,0:T(8,128)S(1)}, f32[6,128,128]{2,1,0:T(8,128)S(1)}, f32[6,128,128]{2,1,0:T(8,128)S(1)}) custom-call(bf16[4,272,128]{2,1,0:T(8,128)(2,1)S(1)} %pad_maximum_fusion.1.refs_0_, bf16[6,272,128]{2,1,0:T(8,128)(2,1)S(1)} %constant_dynamic-update-slice_fusion.refs_1_, ...), custom_call_target="tpu_custom_call" | custom-call | flops 2516582400 | bytes 3145728 | tf_op jit(solution)/shard_map/chunk1/pallas_call | solution.py:29
  38.8 1.4 %collective-permute-start.11 = (bf16[4,480,128]{2,1,0:T(8,128)(2,1)S(1)}, bf16[4,480,128]{2,1,0:T(8,128)(2,1)S(1)}, u32[]{:S(2)}, u32[]{:S(2)}) collective-permute-start(bf16[4,480,128]{2,1,0:T(8,128)(2,1)S(1)} %get-tuple-element.39), channel_id=1, source_target_pairs={{0,48},{2,50},{4,52},{6,54},{8,14},{10,8},{12,10},{14,12},{16,0},{... | collective-permute-start | bytes 1474568 | tf_op jit(solution)/shard_map/ppermute | solution.py:189
  40.2 2.3 %collective-permute-done.9.refs_3_ = bf16[4,480,128]{2,1,0:T(8,128)(2,1)S(1)} collective-permute-done((bf16[4,480,128]{2,1,0:T(8,128)(2,1)S(1)}, bf16[4,480,128]{2,1,0:T(8,128)(2,1)S(1)}, u32[]{:S(2)}, u32[]{:S(2)}) %collective-permute-start.9) | collective-permute-done | bytes 491552 | tf_op jit(solution)/shard_map/ppermute | solution.py:189
  42.5 4.9 %chunk3.1 = (bf16[4,480,128]{2,1,0:T(8,128)(2,1)S(1)}, f32[4,128,128]{2,1,0:T(8,128)S(1)}, f32[6,128,128]{2,1,0:T(8,128)S(1)}, f32[6,128,128]{2,1,0:T(8,128)S(1)}) custom-call(bf16[4,272,128]{2,1,0:T(8,128)(2,1)S(1)} %pad_maximum_fusion.1.refs_0_, ...), custom_call_target="tpu_custom_call", output_to_operand_aliasing={{1}: (4, {}), {2}: (5, {}), {3}: (6, {})} | custom-call | flops 2516582400 | bytes 4194304 | tf_op jit(solution)/shard_map/chunk3/pallas_call | solution.py:29
  47.4 1.5 %collective-permute-start.12 = (bf16[4,480,128]{2,1,0:T(8,128)(2,1)S(1)}, bf16[4,480,128]{2,1,0:T(8,128)(2,1)S(1)}, u32[]{:S(2)}, u32[]{:S(2)}) collective-permute-start(bf16[4,480,128]{2,1,0:T(8,128)(2,1)S(1)} %get-tuple-element.43), channel_id=1, source_target_pairs={{0,16},{2,18},{4,20},{6,22},{8,10},{10,12},{12,14},{14,8},{16,32},... | collective-permute-start | bytes 1474568 | tf_op jit(solution)/shard_map/ppermute | solution.py:189
  49.0 4.9 %chunk2.1 = (bf16[4,480,128]{2,1,0:T(8,128)(2,1)S(1)}, f32[4,128,128]{2,1,0:T(8,128)S(1)}, f32[6,128,128]{2,1,0:T(8,128)S(1)}, f32[6,128,128]{2,1,0:T(8,128)S(1)}) custom-call(bf16[4,272,128]{2,1,0:T(8,128)(2,1)S(1)} %pad_maximum_fusion.1.refs_0_, ...), custom_call_target="tpu_custom_call", output_to_operand_aliasing={{1}: (4, {}), {2}: (5, {}), {3}: (6, {})} | custom-call | flops 2516582400 | bytes 4685824 | tf_op jit(solution)/shard_map/chunk2/pallas_call | solution.py:29
  53.9 3.1 %collective-permute-start.14 = (bf16[4,480,128]{2,1,0:T(8,128)(2,1)S(1)}, bf16[4,480,128]{2,1,0:T(8,128)(2,1)S(1)}, u32[]{:S(2)}, u32[]{:S(2)}) collective-permute-start(bf16[4,480,128]{2,1,0:T(8,128)(2,1)S(1)} %get-tuple-element.48), channel_id=1, source_target_pairs={{0,32},{2,34},{4,36},{6,38},{8,12},{10,14},{12,8},{14,10},{16,48},... | collective-permute-start | bytes 1474568 | tf_op jit(solution)/shard_map/ppermute | solution.py:189
  57.0 0.1 collective-permute-done.12.refs_7_.b3
  57.1 4.9 %chunk0.1 = (f32[4,480,128]{2,1,0:T(8,128)S(1)}, f32[4,128,128]{2,1,0:T(8,128)S(1)}, f32[6,128,128]{2,1,0:T(8,128)S(1)}, f32[6,128,128]{2,1,0:T(8,128)S(1)}) custom-call(bf16[4,272,128]{2,1,0:T(8,128)(2,1)S(1)} %pad_maximum_fusion.1.refs_0_, ...), custom_call_target="tpu_custom_call", output_to_operand_aliasing={{1}: (4, {}), {2}: (5, {}), {3}: (6, {})} | custom-call | flops 2516582400 | bytes 5177344 | tf_op jit(solution)/shard_map/chunk0/pallas_call | solution.py:29
  62.0 6.0 %collective-permute-start.13 = (f32[6,128,128]{2,1,0:T(8,128)S(1)}, f32[6,128,128]{2,1,0:T(8,128)S(1)}, u32[]{:S(2)}, u32[]{:S(2)}) collective-permute-start(f32[6,128,128]{2,1,0:T(8,128)S(1)} %get-tuple-element.46), channel_id=1, source_target_pairs={{0,8},{8,0},{1,9},{9,1},{2,10},{10,2},{3,11},{11,3},{4,12},{12,4},... | collective-permute-start | bytes 1179656 | tf_op jit(solution)/shard_map/ppermute | solution.py:167
  68.1 0.2 merge.1
  68.3 1.1 %collective-permute-done.13.rs = f32[6,128,128]{2,1,0:T(8,128)S(1)} collective-permute-done((f32[6,128,128]{2,1,0:T(8,128)S(1)}, f32[6,128,128]{2,1,0:T(8,128)S(1)}, u32[]{:S(2)}, u32[]{:S(2)}) %collective-permute-start.13) | collective-permute-done | bytes 393248 | tf_op jit(solution)/shard_map/ppermute | solution.py:167
  69.5 4.9 %collective-permute-start.15 = (bf16[4,128,128]{2,1,0:T(8,128)(2,1)S(1)}, bf16[4,128,128]{2,1,0:T(8,128)(2,1)S(1)}, u32[]{:S(2)}, u32[]{:S(2)}) collective-permute-start(bf16[4,128,128]{2,1,0:T(8,128)(2,1)S(1)} %get-tuple-element.50), channel_id=1, source_target_pairs={{0,193},{8,72},{64,0},{72,136},{128,64},{136,200},{192,128},{200,9... | collective-permute-start | bytes 393224 | tf_op jit(solution)/shard_map/ppermute | solution.py:179
  74.4 0.9 collective-permute-start.16
  75.3 3.2 %collective-permute-done.16.u2 = bf16[2,128,128]{2,1,0:T(8,128)(2,1)S(1)} collective-permute-done((bf16[2,128,128]{2,1,0:T(8,128)(2,1)S(1)}, bf16[2,128,128]{2,1,0:T(8,128)(2,1)S(1)}, u32[]{:S(2)}, u32[]{:S(2)}) %collective-permute-start.16) | collective-permute-done | bytes 65568 | tf_op jit(solution)/shard_map/ppermute | solution.py:179
  78.6 4.0 %collective-permute-start.17 = (f32[2,128,128]{2,1,0:T(8,128)S(1)}, f32[2,128,128]{2,1,0:T(8,128)S(1)}, u32[]{:S(2)}, u32[]{:S(2)}) collective-permute-start(f32[2,128,128]{2,1,0:T(8,128)S(1)} %get-tuple-element.53), channel_id=1, source_target_pairs={{0,8},{8,0},{1,9},{9,1},{2,10},{10,2},{3,11},{11,3},{4,12},{12,4},... | collective-permute-start | bytes 393224 | tf_op jit(solution)/shard_map/ppermute | solution.py:167
  82.5 1.3 %collective-permute-start.19 = (bf16[480,128]{1,0:T(8,128)(2,1)S(1)}, bf16[480,128]{1,0:T(8,128)(2,1)S(1)}, u32[]{:S(2)}, u32[]{:S(2)}) collective-permute-start(bf16[480,128]{1,0:T(8,128)(2,1)S(1)} %get-tuple-element.56), channel_id=1, source_target_pairs={{0,6},{2,0},{4,2},{6,4},{8,56},{10,58},{12,60},{14,62},{16,22},{18... | collective-permute-start | bytes 368648 | tf_op jit(solution)/shard_map/ppermute | solution.py:189
  83.9 1.9 %collective-permute-start.20 = (bf16[480,128]{1,0:T(8,128)(2,1)S(1)}, bf16[480,128]{1,0:T(8,128)(2,1)S(1)}, u32[]{:S(2)}, u32[]{:S(2)}) collective-permute-start(bf16[480,128]{1,0:T(8,128)(2,1)S(1)} %get-tuple-element.57), channel_id=1, source_target_pairs={{0,4},{2,6},{4,0},{6,2},{8,40},{10,42},{12,44},{14,46},{16,20},{18... | collective-permute-start | bytes 368648 | tf_op jit(solution)/shard_map/ppermute | solution.py:189
  85.8 0.9 collective-permute-start.21
  86.7 1.0 %collective-permute-start.18 = (f32[128,128]{1,0:T(8,128)S(1)}, f32[128,128]{1,0:T(8,128)S(1)}, u32[]{:S(2)}, u32[]{:S(2)}) collective-permute-start(f32[128,128]{1,0:T(8,128)S(1)} %get-tuple-element.55), channel_id=1, source_target_pairs={{0,1},{1,0},{2,3},{3,2},{4,5},{5,4},{6,7},{7,6},{8,9},{9,8},{10,11... | collective-permute-start | bytes 196616 | tf_op jit(solution)/shard_map/ppermute | solution.py:171
  87.6 1.7 %collective-permute-done.20.f2 = bf16[480,128]{1,0:T(8,128)(2,1)S(1)} collective-permute-done((bf16[480,128]{1,0:T(8,128)(2,1)S(1)}, bf16[480,128]{1,0:T(8,128)(2,1)S(1)}, u32[]{:S(2)}, u32[]{:S(2)}) %collective-permute-start.20) | collective-permute-done | bytes 122912 | tf_op jit(solution)/shard_map/ppermute | solution.py:189
  89.3 1.4 %collective-permute-done.21.f3 = bf16[480,128]{1,0:T(8,128)(2,1)S(1)} collective-permute-done((bf16[480,128]{1,0:T(8,128)(2,1)S(1)}, bf16[480,128]{1,0:T(8,128)(2,1)S(1)}, u32[]{:S(2)}, u32[]{:S(2)}) %collective-permute-start.21) | collective-permute-done | bytes 122912 | tf_op jit(solution)/shard_map/ppermute | solution.py:189
  90.7 3.0 %collective-permute-done.18.far = f32[128,128]{1,0:T(8,128)S(1)} collective-permute-done((f32[128,128]{1,0:T(8,128)S(1)}, f32[128,128]{1,0:T(8,128)S(1)}, u32[]{:S(2)}, u32[]{:S(2)}) %collective-permute-start.18) | collective-permute-done | bytes 65568 | tf_op jit(solution)/shard_map/ppermute | solution.py:171
  93.8 0.8 last.1
  (15 shorter events, 0.2 us)
Async XLA Ops:
  2.4 8.1 %collective-permute-start = (bf16[272,128]{1,0:T(8,128)(2,1)}, bf16[272,128]{1,0:T(8,128)(2,1)S(1)}, u32[]{:S(2)}, u32[]{:S(2)}) collective-permute-start(bf16[272,128]{1,0:T(8,128)(2,1)} %get-tuple-element.31), channel_id=1, source_target_pairs={{0,1},{1,0},{2,3},{3,2},{4,5},{5,4},{6,7},{7,6},{8,9},{9,8},{10,11... | collective-permute-start | bytes 208904 | tf_op jit(solution)/shard_map/ppermute | solution.py:171
  10.5 4.4 %copy-start = (bf16[272,128]{1,0:T(8,128)(2,1)S(1)}, bf16[272,128]{1,0:T(8,128)(2,1)}, u32[]{:S(2)}) copy-start(bf16[272,128]{1,0:T(8,128)(2,1)} %get-tuple-element.31) | copy-start | bytes 208900
  11.5 3.6 %copy-start.1 = (bf16[480,128]{1,0:T(8,128)(2,1)S(1)}, bf16[480,128]{1,0:T(8,128)(2,1)}, u32[]{:S(2)}) copy-start(bf16[480,128]{1,0:T(8,128)(2,1)} %get-tuple-element.32) | copy-start | bytes 368644
  11.5 3.4 %collective-permute-start.1 = (bf16[2,272,128]{2,1,0:T(8,128)(2,1)S(1)}, bf16[2,272,128]{2,1,0:T(8,128)(2,1)S(1)}, u32[]{:S(2)}, u32[]{:S(2)}) collective-permute-start(bf16[2,272,128]{2,1,0:T(8,128)(2,1)S(1)} %pad_maximum_fusion.2), channel_id=1, source_target_pairs={{0,8},{8,0},{1,9},{9,1},{2,10},{10,2},{3,11},{11,3},{4,12},{12,4},... | collective-permute-start | bytes 417800 | tf_op jit(solution)/shard_map/ppermute | solution.py:167
  14.9 10.9 %collective-permute-start.2 = (bf16[4,272,128]{2,1,0:T(8,128)(2,1)S(1)}, bf16[4,272,128]{2,1,0:T(8,128)(2,1)S(1)}, u32[]{:S(2)}, u32[]{:S(2)}) collective-permute-start(bf16[4,272,128]{2,1,0:T(8,128)(2,1)S(1)} %pad_maximum_fusion.1.refs_0_), channel_id=1, source_target_pairs={{0,64},{8,201},{64,128},{72,8},{128,192},{136,72},{192,1},{200,136... | collective-permute-start | bytes 835592 | tf_op jit(solution)/shard_map/ppermute | solution.py:179
  15.1 7.5 %collective-permute-start.7 = (bf16[480,128]{1,0:T(8,128)(2,1)S(1)}, bf16[480,128]{1,0:T(8,128)(2,1)S(1)}, u32[]{:S(2)}, u32[]{:S(2)}) collective-permute-start(bf16[480,128]{1,0:T(8,128)(2,1)S(1)} %copy-done.1), channel_id=1, source_target_pairs={{0,6},{2,0},{4,2},{6,4},{8,56},{10,58},{12,60},{14,62},{16,22},{18... | collective-permute-start | bytes 368648 | tf_op jit(solution)/shard_map/ppermute | solution.py:189
  17.8 5.3 %collective-permute-start.6 = (bf16[480,128]{1,0:T(8,128)(2,1)S(1)}, bf16[480,128]{1,0:T(8,128)(2,1)S(1)}, u32[]{:S(2)}, u32[]{:S(2)}) collective-permute-start(bf16[480,128]{1,0:T(8,128)(2,1)S(1)} %copy-done.1), channel_id=1, source_target_pairs={{0,4},{2,6},{4,0},{6,2},{8,40},{10,42},{12,44},{14,46},{16,20},{18... | collective-permute-start | bytes 368648 | tf_op jit(solution)/shard_map/ppermute | solution.py:189
  18.2 6.5 %collective-permute-start.5 = (bf16[480,128]{1,0:T(8,128)(2,1)S(1)}, bf16[480,128]{1,0:T(8,128)(2,1)S(1)}, u32[]{:S(2)}, u32[]{:S(2)}) collective-permute-start(bf16[480,128]{1,0:T(8,128)(2,1)S(1)} %copy-done.1), channel_id=1, source_target_pairs={{0,2},{2,4},{4,6},{6,0},{8,24},{10,26},{12,28},{14,30},{16,18},{18... | collective-permute-start | bytes 368648 | tf_op jit(solution)/shard_map/ppermute | solution.py:189
  18.9 7.3 %collective-permute-start.3 = (bf16[2,272,128]{2,1,0:T(8,128)(2,1)S(1)}, bf16[2,272,128]{2,1,0:T(8,128)(2,1)S(1)}, u32[]{:S(2)}, u32[]{:S(2)}) collective-permute-start(bf16[2,272,128]{2,1,0:T(8,128)(2,1)S(1)} %pad_maximum_fusion.2), channel_id=1, source_target_pairs={{0,128},{8,137},{64,192},{72,201},{128,1},{136,8},{192,65},{200,72... | collective-permute-start | bytes 417800 | tf_op jit(solution)/shard_map/ppermute | solution.py:179
  24.7 9.3 %collective-permute-start.10 = (bf16[4,480,128]{2,1,0:T(8,128)(2,1)S(1)}, bf16[4,480,128]{2,1,0:T(8,128)(2,1)S(1)}, u32[]{:S(2)}, u32[]{:S(2)}) collective-permute-start(bf16[4,480,128]{2,1,0:T(8,128)(2,1)S(1)} %pad_maximum_fusion.refs_3_), channel_id=1, source_target_pairs={{0,16},{2,18},{4,20},{6,22},{8,10},{10,12},{12,14},{14,8},{16,32},... | collective-permute-start | bytes 1474568 | tf_op jit(solution)/shard_map/ppermute | solution.py:189
  26.2 7.8 %collective-permute-start.4 = (bf16[6,272,128]{2,1,0:T(8,128)(2,1)S(1)}, bf16[6,272,128]{2,1,0:T(8,128)(2,1)S(1)}, u32[]{:S(2)}, u32[]{:S(2)}) collective-permute-start(bf16[6,272,128]{2,1,0:T(8,128)(2,1)S(1)} %constant_dynamic-update-slice_fusion.refs_1_), channel_id=1, source_target_pairs={{0,8},{8,0},{1,9},{9,1},{2,10},{10,2},{3,11},{11,3},{4,12},{12,4},... | collective-permute-start | bytes 1253384 | tf_op jit(solution)/shard_map/ppermute | solution.py:167
  29.4 13.1 %collective-permute-start.9 = (bf16[4,480,128]{2,1,0:T(8,128)(2,1)S(1)}, bf16[4,480,128]{2,1,0:T(8,128)(2,1)S(1)}, u32[]{:S(2)}, u32[]{:S(2)}) collective-permute-start(bf16[4,480,128]{2,1,0:T(8,128)(2,1)S(1)} %pad_maximum_fusion.refs_3_), channel_id=1, source_target_pairs={{0,48},{2,50},{4,52},{6,54},{8,14},{10,8},{12,10},{14,12},{16,0},{... | collective-permute-start | bytes 1474568 | tf_op jit(solution)/shard_map/ppermute | solution.py:189
  31.5 17.5 %collective-permute-start.8 = (bf16[4,480,128]{2,1,0:T(8,128)(2,1)S(1)}, bf16[4,480,128]{2,1,0:T(8,128)(2,1)S(1)}, u32[]{:S(2)}, u32[]{:S(2)}) collective-permute-start(bf16[4,480,128]{2,1,0:T(8,128)(2,1)S(1)} %pad_maximum_fusion.refs_3_), channel_id=1, source_target_pairs={{0,32},{2,34},{4,36},{6,38},{8,12},{10,14},{12,8},{14,10},{16,48},... | collective-permute-start | bytes 1474568 | tf_op jit(solution)/shard_map/ppermute | solution.py:189
  38.8 10.1 %collective-permute-start.11 = (bf16[4,480,128]{2,1,0:T(8,128)(2,1)S(1)}, bf16[4,480,128]{2,1,0:T(8,128)(2,1)S(1)}, u32[]{:S(2)}, u32[]{:S(2)}) collective-permute-start(bf16[4,480,128]{2,1,0:T(8,128)(2,1)S(1)} %get-tuple-element.39), channel_id=1, source_target_pairs={{0,48},{2,50},{4,52},{6,54},{8,14},{10,8},{12,10},{14,12},{16,0},{... | collective-permute-start | bytes 1474568 | tf_op jit(solution)/shard_map/ppermute | solution.py:189
  47.4 9.7 %collective-permute-start.12 = (bf16[4,480,128]{2,1,0:T(8,128)(2,1)S(1)}, bf16[4,480,128]{2,1,0:T(8,128)(2,1)S(1)}, u32[]{:S(2)}, u32[]{:S(2)}) collective-permute-start(bf16[4,480,128]{2,1,0:T(8,128)(2,1)S(1)} %get-tuple-element.43), channel_id=1, source_target_pairs={{0,16},{2,18},{4,20},{6,22},{8,10},{10,12},{12,14},{14,8},{16,32},... | collective-permute-start | bytes 1474568 | tf_op jit(solution)/shard_map/ppermute | solution.py:189
  53.9 14.2 %collective-permute-start.14 = (bf16[4,480,128]{2,1,0:T(8,128)(2,1)S(1)}, bf16[4,480,128]{2,1,0:T(8,128)(2,1)S(1)}, u32[]{:S(2)}, u32[]{:S(2)}) collective-permute-start(bf16[4,480,128]{2,1,0:T(8,128)(2,1)S(1)} %get-tuple-element.48), channel_id=1, source_target_pairs={{0,32},{2,34},{4,36},{6,38},{8,12},{10,14},{12,8},{14,10},{16,48},... | collective-permute-start | bytes 1474568 | tf_op jit(solution)/shard_map/ppermute | solution.py:189
  62.0 7.4 %collective-permute-start.13 = (f32[6,128,128]{2,1,0:T(8,128)S(1)}, f32[6,128,128]{2,1,0:T(8,128)S(1)}, u32[]{:S(2)}, u32[]{:S(2)}) collective-permute-start(f32[6,128,128]{2,1,0:T(8,128)S(1)} %get-tuple-element.46), channel_id=1, source_target_pairs={{0,8},{8,0},{1,9},{9,1},{2,10},{10,2},{3,11},{11,3},{4,12},{12,4},... | collective-permute-start | bytes 1179656 | tf_op jit(solution)/shard_map/ppermute | solution.py:167
  69.5 9.1 %collective-permute-start.15 = (bf16[4,128,128]{2,1,0:T(8,128)(2,1)S(1)}, bf16[4,128,128]{2,1,0:T(8,128)(2,1)S(1)}, u32[]{:S(2)}, u32[]{:S(2)}) collective-permute-start(bf16[4,128,128]{2,1,0:T(8,128)(2,1)S(1)} %get-tuple-element.50), channel_id=1, source_target_pairs={{0,193},{8,72},{64,0},{72,136},{128,64},{136,200},{192,128},{200,9... | collective-permute-start | bytes 393224 | tf_op jit(solution)/shard_map/ppermute | solution.py:179
  74.4 4.1 %collective-permute-start.16 = (bf16[2,128,128]{2,1,0:T(8,128)(2,1)S(1)}, bf16[2,128,128]{2,1,0:T(8,128)(2,1)S(1)}, u32[]{:S(2)}, u32[]{:S(2)}) collective-permute-start(bf16[2,128,128]{2,1,0:T(8,128)(2,1)S(1)} %get-tuple-element.51), channel_id=1, source_target_pairs={{0,129},{8,136},{64,193},{72,200},{128,0},{136,9},{192,64},{200,73... | collective-permute-start | bytes 196616 | tf_op jit(solution)/shard_map/ppermute | solution.py:179
  78.6 8.1 %collective-permute-start.17 = (f32[2,128,128]{2,1,0:T(8,128)S(1)}, f32[2,128,128]{2,1,0:T(8,128)S(1)}, u32[]{:S(2)}, u32[]{:S(2)}) collective-permute-start(f32[2,128,128]{2,1,0:T(8,128)S(1)} %get-tuple-element.53), channel_id=1, source_target_pairs={{0,8},{8,0},{1,9},{9,1},{2,10},{10,2},{3,11},{11,3},{4,12},{12,4},... | collective-permute-start | bytes 393224 | tf_op jit(solution)/shard_map/ppermute | solution.py:167
  82.5 5.1 %collective-permute-start.19 = (bf16[480,128]{1,0:T(8,128)(2,1)S(1)}, bf16[480,128]{1,0:T(8,128)(2,1)S(1)}, u32[]{:S(2)}, u32[]{:S(2)}) collective-permute-start(bf16[480,128]{1,0:T(8,128)(2,1)S(1)} %get-tuple-element.56), channel_id=1, source_target_pairs={{0,6},{2,0},{4,2},{6,4},{8,56},{10,58},{12,60},{14,62},{16,22},{18... | collective-permute-start | bytes 368648 | tf_op jit(solution)/shard_map/ppermute | solution.py:189
  83.9 5.5 %collective-permute-start.20 = (bf16[480,128]{1,0:T(8,128)(2,1)S(1)}, bf16[480,128]{1,0:T(8,128)(2,1)S(1)}, u32[]{:S(2)}, u32[]{:S(2)}) collective-permute-start(bf16[480,128]{1,0:T(8,128)(2,1)S(1)} %get-tuple-element.57), channel_id=1, source_target_pairs={{0,4},{2,6},{4,0},{6,2},{8,40},{10,42},{12,44},{14,46},{16,20},{18... | collective-permute-start | bytes 368648 | tf_op jit(solution)/shard_map/ppermute | solution.py:189
  85.8 4.9 %collective-permute-start.21 = (bf16[480,128]{1,0:T(8,128)(2,1)S(1)}, bf16[480,128]{1,0:T(8,128)(2,1)S(1)}, u32[]{:S(2)}, u32[]{:S(2)}) collective-permute-start(bf16[480,128]{1,0:T(8,128)(2,1)S(1)} %get-tuple-element.58), channel_id=1, source_target_pairs={{0,2},{2,4},{4,6},{6,0},{8,24},{10,26},{12,28},{14,30},{16,18},{18... | collective-permute-start | bytes 368648 | tf_op jit(solution)/shard_map/ppermute | solution.py:189
  86.7 7.1 %collective-permute-start.18 = (f32[128,128]{1,0:T(8,128)S(1)}, f32[128,128]{1,0:T(8,128)S(1)}, u32[]{:S(2)}, u32[]{:S(2)}) collective-permute-start(f32[128,128]{1,0:T(8,128)S(1)} %get-tuple-element.55), channel_id=1, source_target_pairs={{0,1},{1,0},{2,3},{3,2},{4,5},{5,4},{6,7},{7,6},{8,9},{9,8},{10,11... | collective-permute-start | bytes 196616 | tf_op jit(solution)/shard_map/ppermute | solution.py:171
where the time goes:
time: 94.7 us; the launch traced here: 94.5 us
  starting transfers between devices  49.9 us (53%)
  Pallas kernels  22.3 us (24%)
  waiting for transfers between devices  20.6 us (22%)
  other arithmetic  1.06 us (1%)
    pallas_call x10, Pallas kernels, call(): pl.pallas_call(kernel, name=name, out_shape=outs, in_specs=spaces or [VM]...  22.3 us
    ppermute x12, starting transfers between devices, send_plane(): return lax.ppermute(x, ('y', 'core', 'x'), pairs)  18.2 us
    ppermute x4, starting transfers between devices, swap_cores(): return lax.ppermute(x, 'core', SWAP)  15.6 us
    ppermute x4, starting transfers between devices, send_z(): return lax.ppermute(x, ('zl', 'core', 'zh'), pairs)  9.82 us
    ppermute x12, waiting for transfers between devices, send_plane(): return lax.ppermute(x, ('y', 'core', 'x'), pairs)  8.88 us
    ppermute x2, starting transfers between devices, swap_halves(): return lax.ppermute(x, 'zh', FAR)  6.17 us
    ppermute x2, waiting for transfers between devices, swap_halves(): return lax.ppermute(x, 'zh', FAR)  5.97 us
    ppermute x4, waiting for transfers between devices, send_z(): return lax.ppermute(x, ('zl', 'core', 'zh'), pairs)  3.58 us
  transfers between devices with their start and end apart: 22, of which 13 were waited for; matrix products, arithmetic and copies ran while one was open for 0% of the time, Pallas kernels for 21%

commit v1 on v0

v1 whole, which is shorter than its diff:
```python
import math

import jax
import jax.numpy as jnp
from jax import lax
from jax.experimental import pallas as pl
from jax.experimental.pallas import tpu as pltpu
from jax.sharding import Mesh, PartitionSpec as P

W = 128
T = 240
QP = 2 * W + 16
BF, F32 = jnp.bfloat16, jnp.float32
FACTOR = 1.0 / math.sqrt(W)
LOG2E = math.log2(math.e)
NT = (((1,), (1,)), ((), ()))
NN = (((1,), (0,)), ((), ()))
TN = (((0,), (0,)), ((), ()))
VM = pl.BlockSpec(memory_space=pltpu.VMEM)
ANY = pl.BlockSpec(memory_space=pl.ANY)


def dot(a, b, dims):
    return lax.dot_general(a, b, dims, preferred_element_type=F32)


def call(kernel, name, outs, args, flops=0, aliases=None, spaces=None, scratch=(), vmem=40):
    nbytes = sum(math.prod(a.shape) * a.dtype.itemsize for a in list(outs) + list(args))
    return pl.pallas_call(
        kernel,
        name=name,
        out_shape=outs,
        in_specs=spaces or [VM] * len(args),
        out_specs=tuple([VM] * len(outs)),
        input_output_aliases=aliases or {},
        scratch_shapes=list(scratch),
        compiler_params=pltpu.CompilerParams(vmem_limit_bytes=vmem * 2**20),
        cost_estimate=pl.CostEstimate(flops=flops, bytes_accessed=nbytes, transcendentals=0),
    )(*args)


def sds(shape, dtype):
    return jax.ShapeDtypeStruct(shape, dtype)


def pack_kernel(q, g, o, lse, k, v, qp, kv, qbuf, gbuf, obuf, lbuf, sems):
    moves = (
        (g, gbuf),
        (o, obuf),
        (lse, lbuf),
        (q, qbuf),
        (k, kv.at[pl.ds(0, T), :]),
        (v, kv.at[pl.ds(T, T), :]),
    )
    copies = [pltpu.make_async_copy(src, dst, sems.at[n]) for n, (src, dst) in enumerate(moves)]
    for copy in copies:
        copy.start()
    for copy in copies[:3]:
        copy.wait()
    prod = gbuf[...].astype(F32) * obuf[...].astype(F32)
    delta = jnp.sum(prod.T, axis=0, keepdims=True)
    rows = []
    for x in (lbuf[...] * LOG2E, delta):
        for _ in range(3):
            part = x.astype(BF).astype(F32)
            rows.append(part)
            x = x - part
    rows.append(jnp.zeros((10, W), F32))
    stat = jnp.concatenate(rows, axis=0).astype(BF)
    for copy in copies[3:]:
        copy.wait()
    for z in range(8):
        qp[z, 0:W, :] = qbuf[...]
        qp[z, W : 2 * W, :] = gbuf[...]
        qp[z, 2 * W :, :] = stat


SAME, OTHER = ((0, 0), (0, 4)), ((1, 0), (1, 4))


def chunk_kernel(groups, given, touched, has_part, refs):
    qrefs, kv, refs = refs[:2], refs[2], refs[3:]
    acc_in, refs = dict(zip(given, refs)), refs[len(given) :]
    part = refs[0] if has_part else None
    refs = refs[len(refs) - 1 - len(touched) :]
    out, accs = refs[0], dict(zip(touched, refs[1:]))
    ks = jnp.concatenate([kv[i, 0:T, :] for i in range(4)], axis=0)
    vs = jnp.concatenate([kv[i, T:, :] for i in range(4)], axis=0)
    gk = gv = None
    for r, at in groups:
        mem = range(at, at + 4)
        q = jnp.concatenate([qrefs[r][i, 0:W, :] for i in mem], axis=0)
        g = jnp.concatenate([qrefs[r][i, W : 2 * W, :] for i in mem], axis=0)
        stat = jnp.concatenate([qrefs[r][i, 2 * W :, :].astype(F32) for i in mem], axis=1)
        l2 = stat[0:1] + stat[1:2] + stat[2:3]
        delta = stat[3:4] + stat[4:5] + stat[5:6]
        p = jnp.exp2(dot(ks, q, NT) * (FACTOR * LOG2E) - l2)
        ds = (p * (dot(vs, g, NT) - delta)).astype(BF)
        dv = dot(p.astype(BF), g, NN)
        dk = dot(ds, q, NN)
        gv = dv if gv is None else gv + dv
        gk = dk if gk is None else gk + dk
        u = dot(ks, ds, TN)
        for n, i in enumerate(mem):
            block = u[:, n * W : (n + 1) * W]
            accs[r][i] = acc_in[r][i] + block if r in acc_in else block
    for i in range(4):
        rows = slice(i * T, (i + 1) * T)
        for col, total in ((slice(0, T), gk), (slice(T, 2 * T), gv)):
            block = total[rows]
            if has_part:
                block = part[i, col, :] + block
            out[i, col, :] = block.astype(out.dtype)


def chunk(name, queries, kv, acc, dtype, groups=SAME + OTHER, part=None, after=()):
    touched = sorted({r for r, _ in groups})
    given = [r for r in touched if r in acc]
    outs = (sds((4, 2 * T, W), dtype),) + (sds((8, W, W), F32),) * len(touched)
    args = tuple(queries) + (kv,)
    aliases = {len(args) + n: 1 + touched.index(r) for n, r in enumerate(given)}
    args += tuple(acc[r] for r in given)
    if part is not None:
        aliases[len(args)] = 0
        args += (part,)
    spaces = [VM] * len(args) + [ANY] * len(after)

    def kernel(*refs):
        chunk_kernel(groups, given, touched, part is not None, refs)

    flops = 10 * 960 * 512 * len(groups) * W
    out = call(kernel, name, outs, args + tuple(after), flops, aliases, spaces)
    return out[0], {**acc, **dict(zip(touched, out[1:]))}


def merge_kernel(own, b1, b2, b3, after, *outs):
    for r in range(4):
        total = own[r]
        for other in (b1, b2, b3):
            total = total + other[r].astype(F32)
        outs[r][...] = total.astype(outs[r].dtype)


def halves_kernel(mine, got, out):
    out[...] = (mine[...] + got[...]).astype(BF)


def last_kernel(u, own, f1, f2, f3, gq, gk, gv):
    total = u[0].astype(F32)
    for z in range(1, 8):
        total = total + u[z].astype(F32)
    gq[...] = total.T * FACTOR
    total = own[...] + f1[...].astype(F32) + f2[...].astype(F32) + f3[...].astype(F32)
    gk[...] = total[0:T] * FACTOR
    gv[...] = total[T:]


SWAP = [(0, 1), (1, 0)]


def swap_cores(x):
    return lax.ppermute(x, "core", SWAP)


def exchange_z(x):
    return lax.all_to_all(x, ("zl", "zh"), 0, 0, tiled=True)


def send_plane(x, s, core_on_x):
    pairs = []
    for y in range(4):
        for c in range(2):
            for i in range(4):
                to_y, to_x = (y, (i + s) % 4) if c == core_on_x else ((y + s) % 4, i)
                pairs.append(((y * 2 + c) * 4 + i, (to_y * 2 + c) * 4 + to_x))
    return lax.ppermute(x, ("y", "core", "x"), pairs)


def local(queries, keys, values, outputs, out_grad, lse):
    qp, kv = call(
        pack_kernel,
        "pack",
        (sds((8, QP, W), BF), sds((2 * T, W), BF)),
        (queries, out_grad, outputs, lse.reshape(1, W), keys, values),
        spaces=[ANY] * 6,
        scratch=(
            pltpu.VMEM((W, W), BF),
            pltpu.VMEM((W, W), BF),
            pltpu.VMEM((W, W), BF),
            pltpu.VMEM((1, W), F32),
            pltpu.SemaphoreType.DMA((6,)),
        ),
        vmem=60,
    )
    same = exchange_z(qp)
    other = swap_cores(same)
    kv0 = jnp.stack([kv] + [send_plane(kv, r, 0) for r in (1, 2, 3)])
    kvs = {s: send_plane(kv0, s, 1) for s in (1, 3, 2)}

    qs = (same, other)
    part, acc = chunk("chunk0a", qs, kv0, {}, F32, OTHER)
    out1, acc = chunk("chunk1", qs, kvs[1], acc, BF)
    back1 = send_plane(out1, -1, 1)
    out3, acc = chunk("chunk3", qs, kvs[3], acc, BF)
    back3 = send_plane(out3, -3, 1)
    out2, acc = chunk("chunk2", qs, kvs[2], acc, BF, after=(back1,))
    back2 = send_plane(out2, -2, 1)
    rs = swap_cores(acc[1])
    out0, acc = chunk("chunk0b", qs, kv0, acc, F32, SAME, part, (back3,))

    (halves,) = call(halves_kernel, "halves", (sds((8, W, W), BF),), (acc[0], rs))
    u = exchange_z(halves)
    part0, *parts = call(
        merge_kernel,
        "merge",
        (sds((2 * T, W), F32),) + (sds((2 * T, W), BF),) * 3,
        (out0, back1, back2, back3, halves),
        spaces=[VM] * 4 + [ANY],
    )
    f = [send_plane(parts[r - 1], -r, 0) for r in (1, 2, 3)]
    return call(
        last_kernel,
        "last",
        (sds((W, W), F32), sds((T, W), F32), sds((T, W), F32)),
        (u, part0, *f),
    )


def solution(mesh):
    fine = Mesh(mesh.devices.reshape(4, 4, 2, 4, 2), ("zl", "y", "core", "x", "zh"))
    qs, ks = ("x", "zh", "zl", "y", "core"), ("zl", "y", "core", "x", "zh")
    return jax.shard_map(
        local,
        mesh=fine,
        in_specs=(P(qs, None), P(ks, None), P(ks, None), P(qs, None), P(qs, None), P(qs)),
        out_specs=(P(qs, None), P(ks, None), P(ks, None)),
        check_vma=False,
    )
```

time: 94.7 us -> 83.5 us (0.88)
  the two profiles are of different devices: /device:TPU:65 before, /device:TPU:32 now
where the time goes in v1:
time: 83.5 us; the launch traced here: 83.2 us
  starting transfers between devices  36.7 us (44%)
  Pallas kernels  24 us (29%)
  waiting for transfers between devices  21.7 us (26%)
    pallas_call x9, Pallas kernels, call(): pl.pallas_call(kernel, name=name, out_shape=outs, in_specs=spaces or [VM]...  24 us
    ppermute x12, starting transfers between devices, send_plane(): return lax.ppermute(x, ('y', 'core', 'x'), pairs)  23.9 us
    all_to_all x2, starting transfers between devices, exchange_z(): return lax.all_to_all(x, ('zl', 'zh'), 0, 0, tiled=True)  12.8 us
    all_to_all x2, waiting for transfers between devices, exchange_z(): return lax.all_to_all(x, ('zl', 'zh'), 0, 0, tiled=True)  11.5 us
    ppermute x12, waiting for transfers between devices, send_plane(): return lax.ppermute(x, ('y', 'core', 'x'), pairs)  10.2 us
  transfers between devices with their start and end apart: 16, of which 6 were waited for; matrix products, arithmetic and copies ran while one was open for 0% of the time, Pallas kernels for 26%

profile of v1, /device:TPU:32, one launch (start us, length us, event | category | flops | bytes accessed | tf_op | source)
XLA Modules:
  0.0 83.2 jit_solution(2769863354046761401)
XLA Ops:
  0.6 1.9 %pack.1 = (bf16[8,272,128]{2,1,0:T(8,128)(2,1)}, bf16[480,128]{1,0:T(8,128)(2,1)}) custom-call(bf16[128,128]{1,0:T(8,128)(2,1)} %q.1, bf16[128,128]{1,0:T(8,128)(2,1)} %g.1, bf16[128,128]{1,0:T(8,128)(2,1)} %o.1, f32[1,128]{1,0:T(1,128)} %bitcast.9, bf16[240,128]{1,0:T(8,128)(2,1)} %k.1, bf16[240,128]{1,0:T(8,128)(2,1)} %v.1), custom_call_target="tpu_custom_call" | custom-call | bytes 901632 | tf_op jit(solution)/shard_map/pack/pallas_call | solution.py:29
  2.5 0.0 copy-start
  2.5 8.7 %all-to-all-start = ((bf16[8,272,128]{2,1,0:T(8,128)(2,1)}), bf16[8,272,128]{2,1,0:T(8,128)(2,1)S(1)}, u32[]{:S(2)}, u32[]{:S(2)}) async-start(bf16[8,272,128]{2,1,0:T(8,128)(2,1)} %get-tuple-element.22), calls=%async_computation | async-start | bytes 1114112 | tf_op jit(solution)/shard_map/all_to_all | solution.py:166
  11.2 0.0 copy-done
  11.2 2.8 %collective-permute-start.3 = (bf16[480,128]{1,0:T(8,128)(2,1)S(1)}, bf16[480,128]{1,0:T(8,128)(2,1)S(1)}, u32[]{:S(2)}, u32[]{:S(2)}) collective-permute-start(bf16[480,128]{1,0:T(8,128)(2,1)S(1)} %copy-done), channel_id=1, source_target_pairs={{0,6},{2,0},{4,2},{6,4},{8,56},{10,58},{12,60},{14,62},{16,22},{18... | collective-permute-start | bytes 368648 | tf_op jit(solution)/shard_map/ppermute | solution.py:176
  14.0 0.8 collective-permute-start.2
  14.8 0.9 %collective-permute-start.1 = (bf16[480,128]{1,0:T(8,128)(2,1)S(1)}, bf16[480,128]{1,0:T(8,128)(2,1)S(1)}, u32[]{:S(2)}, u32[]{:S(2)}) collective-permute-start(bf16[480,128]{1,0:T(8,128)(2,1)S(1)} %copy-done), channel_id=1, source_target_pairs={{0,2},{2,4},{4,6},{6,0},{8,24},{10,26},{12,28},{14,30},{16,18},{18... | collective-permute-start | bytes 368648 | tf_op jit(solution)/shard_map/ppermute | solution.py:176
  15.7 11.5 %all-to-all-done.refs_0_ = bf16[8,272,128]{2,1,0:T(8,128)(2,1)S(1)} async-done(((bf16[8,272,128]{2,1,0:T(8,128)(2,1)}), bf16[8,272,128]{2,1,0:T(8,128)(2,1)S(1)}, u32[]{:S(2)}, u32[]{:S(2)}) %all-to-all-start) | async-done | bytes 557088 | tf_op jit(solution)/shard_map/all_to_all | solution.py:166
  27.2 0.0 collective-permute-start
  27.2 0.0 collective-permute-done.3
  27.3 0.0 collective-permute-done.2
  27.3 0.0 collective-permute-done.1
  27.3 0.1 pad_maximum_fusion.refs_2_
  27.3 1.7 %collective-permute-start.6 = (bf16[4,480,128]{2,1,0:T(8,128)(2,1)S(1)}, bf16[4,480,128]{2,1,0:T(8,128)(2,1)S(1)}, u32[]{:S(2)}, u32[]{:S(2)}) collective-permute-start(bf16[4,480,128]{2,1,0:T(8,128)(2,1)S(1)} %pad_maximum_fusion.refs_2_), channel_id=1, source_target_pairs={{0,16},{2,18},{4,20},{6,22},{8,10},{10,12},{12,14},{14,8},{16,32},... | collective-permute-start | bytes 1474568 | tf_op jit(solution)/shard_map/ppermute | solution.py:176
  29.0 1.7 %collective-permute-start.5 = (bf16[4,480,128]{2,1,0:T(8,128)(2,1)S(1)}, bf16[4,480,128]{2,1,0:T(8,128)(2,1)S(1)}, u32[]{:S(2)}, u32[]{:S(2)}) collective-permute-start(bf16[4,480,128]{2,1,0:T(8,128)(2,1)S(1)} %pad_maximum_fusion.refs_2_), channel_id=1, source_target_pairs={{0,48},{2,50},{4,52},{6,54},{8,14},{10,8},{12,10},{14,12},{16,0},{... | collective-permute-start | bytes 1474568 | tf_op jit(solution)/shard_map/ppermute | solution.py:176
  30.6 2.0 %collective-permute-start.4 = (bf16[4,480,128]{2,1,0:T(8,128)(2,1)S(1)}, bf16[4,480,128]{2,1,0:T(8,128)(2,1)S(1)}, u32[]{:S(2)}, u32[]{:S(2)}) collective-permute-start(bf16[4,480,128]{2,1,0:T(8,128)(2,1)S(1)} %pad_maximum_fusion.refs_2_), channel_id=1, source_target_pairs={{0,32},{2,34},{4,36},{6,38},{8,12},{10,14},{12,8},{14,10},{16,48},... | collective-permute-start | bytes 1474568 | tf_op jit(solution)/shard_map/ppermute | solution.py:176
  32.6 0.0 collective-permute-done.refs_1_
  32.6 2.5 %chunk0a.1 = (f32[4,480,128]{2,1,0:T(8,128)S(1)}, f32[8,128,128]{2,1,0:T(8,128)S(1)}) custom-call(bf16[8,272,128]{2,1,0:T(8,128)(2,1)S(1)} %all-to-all-done.refs_0_, bf16[8,272,128]{2,1,0:T(8,128)(2,1)S(1)} %collective-permute-done.refs_1_, bf16[4,480,128]{2,1,0:T(8,128)(2,1)S(1)} %pad_maximum_fusion.refs_2_), custom_call_target="tpu_custom_call" | custom-call | flops 1258291200 | bytes 3112960 | tf_op jit(solution)/shard_map/chunk0a/pallas_call | solution.py:29
  35.1 2.3 %collective-permute-done.6.refs_2_ = bf16[4,480,128]{2,1,0:T(8,128)(2,1)S(1)} collective-permute-done((bf16[4,480,128]{2,1,0:T(8,128)(2,1)S(1)}, bf16[4,480,128]{2,1,0:T(8,128)(2,1)S(1)}, u32[]{:S(2)}, u32[]{:S(2)}) %collective-permute-start.6) | collective-permute-done | bytes 491552 | tf_op jit(solution)/shard_map/ppermute | solution.py:176
  37.5 4.8 %chunk1.1 = (bf16[4,480,128]{2,1,0:T(8,128)(2,1)S(1)}, f32[8,128,128]{2,1,0:T(8,128)S(1)}, f32[8,128,128]{2,1,0:T(8,128)S(1)}) custom-call(bf16[8,272,128]{2,1,0:T(8,128)(2,1)S(1)} %all-to-all-done.refs_0_, bf16[8,272,128]{2,1,0:T(8,128)(2,1)S(1)} %collective-permute-done.refs_1_, ...), custom_call_target="tpu_custom_call", output_to_operand_aliasing={{2}: (3, {})} | custom-call | flops 2516582400 | bytes 3670016 | tf_op jit(solution)/shard_map/chunk1/pallas_call | solution.py:29
  42.3 2.1 %collective-permute-start.7 = (bf16[4,480,128]{2,1,0:T(8,128)(2,1)S(1)}, bf16[4,480,128]{2,1,0:T(8,128)(2,1)S(1)}, u32[]{:S(2)}, u32[]{:S(2)}) collective-permute-start(bf16[4,480,128]{2,1,0:T(8,128)(2,1)S(1)} %get-tuple-element.29), channel_id=1, source_target_pairs={{0,48},{2,50},{4,52},{6,54},{8,14},{10,8},{12,10},{14,12},{16,0},{... | collective-permute-start | bytes 1474568 | tf_op jit(solution)/shard_map/ppermute | solution.py:176
  44.4 0.0 collective-permute-done.5.refs_2_
  44.4 4.9 %chunk3.1 = (bf16[4,480,128]{2,1,0:T(8,128)(2,1)S(1)}, f32[8,128,128]{2,1,0:T(8,128)S(1)}, f32[8,128,128]{2,1,0:T(8,128)S(1)}) custom-call(bf16[8,272,128]{2,1,0:T(8,128)(2,1)S(1)} %all-to-all-done.refs_0_, bf16[8,272,128]{2,1,0:T(8,128)(2,1)S(1)} %collective-permute-done.refs_1_, ...), custom_call_target="tpu_custom_call", output_to_operand_aliasing={{1}: (3, {}), {2}: (4, {})} | custom-call | flops 2516582400 | bytes 4194304 | tf_op jit(solution)/shard_map/chunk3/pallas_call | solution.py:29
  49.3 0.3 collective-permute-start.8
  49.6 0.0 collective-permute-done.4.refs_2_
  49.6 1.8 %collective-permute-done.7.refs_5_.b1 = bf16[4,480,128]{2,1,0:T(8,128)(2,1)S(1)} collective-permute-done((bf16[4,480,128]{2,1,0:T(8,128)(2,1)S(1)}, bf16[4,480,128]{2,1,0:T(8,128)(2,1)S(1)}, u32[]{:S(2)}, u32[]{:S(2)}) %collective-permute-start.7) | collective-permute-done | bytes 491552 | tf_op jit(solution)/shard_map/ppermute | solution.py:176
  51.4 5.5 %chunk2.1 = (bf16[4,480,128]{2,1,0:T(8,128)(2,1)}, f32[8,128,128]{2,1,0:T(8,128)S(1)}, f32[8,128,128]{2,1,0:T(8,128)S(1)}) custom-call(bf16[8,272,128]{2,1,0:T(8,128)(2,1)S(1)} %all-to-all-done.refs_0_, bf16[8,272,128]{2,1,0:T(8,128)(2,1)S(1)} %collective-permute-done.refs_1_, ...), custom_call_target="tpu_custom_call", output_to_operand_aliasing={{1}: (3, {}), {2}: (4, {})} | custom-call | flops 2516582400 | bytes 4685824 | tf_op jit(solution)/shard_map/chunk2/pallas_call | solution.py:29
  56.9 0.0 collective-permute-start.9
  56.9 7.2 %collective-permute-start.10 = (bf16[4,480,128]{2,1,0:T(8,128)(2,1)}, bf16[4,480,128]{2,1,0:T(8,128)(2,1)S(1)}, u32[]{:S(2)}, u32[]{:S(2)}) collective-permute-start(bf16[4,480,128]{2,1,0:T(8,128)(2,1)} %get-tuple-element.36), channel_id=1, source_target_pairs={{0,32},{2,34},{4,36},{6,38},{8,12},{10,14},{12,8},{14,10},{16,48},... | collective-permute-start | bytes 1474568 | tf_op jit(solution)/shard_map/ppermute | solution.py:176
  64.2 0.0 collective-permute-done.8.refs_5_.b3
  64.2 2.6 %chunk0b.1 = (f32[4,480,128]{2,1,0:T(8,128)S(1)}, f32[8,128,128]{2,1,0:T(8,128)S(1)}) custom-call(bf16[8,272,128]{2,1,0:T(8,128)(2,1)S(1)} %all-to-all-done.refs_0_, bf16[8,272,128]{2,1,0:T(8,128)(2,1)S(1)} %collective-permute-done.refs_1_, bf16[4,480,128]{2,1,0:T(8,128)(2,1)S(1)} %pad_maximum_fusion.refs_2_, ...), custom_call_target="tpu_custom_call", output_to_operand_aliasing={{1}: (3, {}), {0}: (4, {})} | custom-call | flops 1258291200 | bytes 5111808 | tf_op jit(solution)/shard_map/chunk0b/pallas_call | solution.py:29
  66.8 0.0 collective-permute-done.9.got
  66.8 0.7 halves.1.after
  67.6 4.1 %all-to-all-start.1 = ((bf16[8,128,128]{2,1,0:T(8,128)(2,1)}), bf16[8,128,128]{2,1,0:T(8,128)(2,1)S(1)}, u32[]{:S(2)}, u32[]{:S(2)}) async-start(bf16[8,128,128]{2,1,0:T(8,128)(2,1)} %halves.1.after), calls=%async_computation.1 | async-start | bytes 524288 | tf_op jit(solution)/shard_map/all_to_all | solution.py:166
  71.7 0.0 collective-permute-done.10.b2
  71.7 0.2 merge.1
  71.9 2.8 %collective-permute-start.11 = (bf16[480,128]{1,0:T(8,128)(2,1)S(1)}, bf16[480,128]{1,0:T(8,128)(2,1)S(1)}, u32[]{:S(2)}, u32[]{:S(2)}) collective-permute-start(bf16[480,128]{1,0:T(8,128)(2,1)S(1)} %get-tuple-element.38), channel_id=1, source_target_pairs={{0,6},{2,0},{4,2},{6,4},{8,56},{10,58},{12,60},{14,62},{16,22},{18... | collective-permute-start | bytes 368648 | tf_op jit(solution)/shard_map/ppermute | solution.py:176
  74.7 0.8 collective-permute-start.12
  75.5 0.9 %collective-permute-start.13 = (bf16[480,128]{1,0:T(8,128)(2,1)S(1)}, bf16[480,128]{1,0:T(8,128)(2,1)S(1)}, u32[]{:S(2)}, u32[]{:S(2)}) collective-permute-start(bf16[480,128]{1,0:T(8,128)(2,1)S(1)} %get-tuple-element.40), channel_id=1, source_target_pairs={{0,2},{2,4},{4,6},{6,0},{8,24},{10,26},{12,28},{14,30},{16,18},{18... | collective-permute-start | bytes 368648 | tf_op jit(solution)/shard_map/ppermute | solution.py:176
  76.4 0.8 collective-permute-done.11.f1
  77.2 4.0 %collective-permute-done.12.f2 = bf16[480,128]{1,0:T(8,128)(2,1)S(1)} collective-permute-done((bf16[480,128]{1,0:T(8,128)(2,1)S(1)}, bf16[480,128]{1,0:T(8,128)(2,1)S(1)}, u32[]{:S(2)}, u32[]{:S(2)}) %collective-permute-start.12) | collective-permute-done | bytes 122912 | tf_op jit(solution)/shard_map/ppermute | solution.py:176
  81.2 1.2 %collective-permute-done.13.f3 = bf16[480,128]{1,0:T(8,128)(2,1)S(1)} collective-permute-done((bf16[480,128]{1,0:T(8,128)(2,1)S(1)}, bf16[480,128]{1,0:T(8,128)(2,1)S(1)}, u32[]{:S(2)}, u32[]{:S(2)}) %collective-permute-start.13) | collective-permute-done | bytes 122912 | tf_op jit(solution)/shard_map/ppermute | solution.py:176
  82.4 0.0 all-to-all-done.1.u
  82.4 0.8 last.1
Async XLA Ops:
  2.5 8.7 %copy-start = (bf16[480,128]{1,0:T(8,128)(2,1)S(1)}, bf16[480,128]{1,0:T(8,128)(2,1)}, u32[]{:S(2)}) copy-start(bf16[480,128]{1,0:T(8,128)(2,1)} %get-tuple-element.23) | copy-start | bytes 368644
  2.5 24.7 %all-to-all-start = ((bf16[8,272,128]{2,1,0:T(8,128)(2,1)}), bf16[8,272,128]{2,1,0:T(8,128)(2,1)S(1)}, u32[]{:S(2)}, u32[]{:S(2)}) async-start(bf16[8,272,128]{2,1,0:T(8,128)(2,1)} %get-tuple-element.22), calls=%async_computation | async-start | bytes 1114112 | tf_op jit(solution)/shard_map/all_to_all | solution.py:166
  11.2 16.0 %collective-permute-start.3 = (bf16[480,128]{1,0:T(8,128)(2,1)S(1)}, bf16[480,128]{1,0:T(8,128)(2,1)S(1)}, u32[]{:S(2)}, u32[]{:S(2)}) collective-permute-start(bf16[480,128]{1,0:T(8,128)(2,1)S(1)} %copy-done), channel_id=1, source_target_pairs={{0,6},{2,0},{4,2},{6,4},{8,56},{10,58},{12,60},{14,62},{16,22},{18... | collective-permute-start | bytes 368648 | tf_op jit(solution)/shard_map/ppermute | solution.py:176
  14.0 13.2 %collective-permute-start.2 = (bf16[480,128]{1,0:T(8,128)(2,1)S(1)}, bf16[480,128]{1,0:T(8,128)(2,1)S(1)}, u32[]{:S(2)}, u32[]{:S(2)}) collective-permute-start(bf16[480,128]{1,0:T(8,128)(2,1)S(1)} %copy-done), channel_id=1, source_target_pairs={{0,4},{2,6},{4,0},{6,2},{8,40},{10,42},{12,44},{14,46},{16,20},{18... | collective-permute-start | bytes 368648 | tf_op jit(solution)/shard_map/ppermute | solution.py:176
  14.8 12.5 %collective-permute-start.1 = (bf16[480,128]{1,0:T(8,128)(2,1)S(1)}, bf16[480,128]{1,0:T(8,128)(2,1)S(1)}, u32[]{:S(2)}, u32[]{:S(2)}) collective-permute-start(bf16[480,128]{1,0:T(8,128)(2,1)S(1)} %copy-done), channel_id=1, source_target_pairs={{0,2},{2,4},{4,6},{6,0},{8,24},{10,26},{12,28},{14,30},{16,18},{18... | collective-permute-start | bytes 368648 | tf_op jit(solution)/shard_map/ppermute | solution.py:176
  27.2 5.4 %collective-permute-start = (bf16[8,272,128]{2,1,0:T(8,128)(2,1)S(1)}, bf16[8,272,128]{2,1,0:T(8,128)(2,1)S(1)}, u32[]{:S(2)}, u32[]{:S(2)}) collective-permute-start(bf16[8,272,128]{2,1,0:T(8,128)(2,1)S(1)} %all-to-all-done.refs_0_), channel_id=1, source_target_pairs={{0,8},{8,0},{1,9},{9,1},{2,10},{10,2},{3,11},{11,3},{4,12},{12,4},... | collective-permute-start | bytes 1671176 | tf_op jit(solution)/shard_map/ppermute | solution.py:162
  27.3 10.1 %collective-permute-start.6 = (bf16[4,480,128]{2,1,0:T(8,128)(2,1)S(1)}, bf16[4,480,128]{2,1,0:T(8,128)(2,1)S(1)}, u32[]{:S(2)}, u32[]{:S(2)}) collective-permute-start(bf16[4,480,128]{2,1,0:T(8,128)(2,1)S(1)} %pad_maximum_fusion.refs_2_), channel_id=1, source_target_pairs={{0,16},{2,18},{4,20},{6,22},{8,10},{10,12},{12,14},{14,8},{16,32},... | collective-permute-start | bytes 1474568 | tf_op jit(solution)/shard_map/ppermute | solution.py:176
  29.0 15.4 %collective-permute-start.5 = (bf16[4,480,128]{2,1,0:T(8,128)(2,1)S(1)}, bf16[4,480,128]{2,1,0:T(8,128)(2,1)S(1)}, u32[]{:S(2)}, u32[]{:S(2)}) collective-permute-start(bf16[4,480,128]{2,1,0:T(8,128)(2,1)S(1)} %pad_maximum_fusion.refs_2_), channel_id=1, source_target_pairs={{0,48},{2,50},{4,52},{6,54},{8,14},{10,8},{12,10},{14,12},{16,0},{... | collective-permute-start | bytes 1474568 | tf_op jit(solution)/shard_map/ppermute | solution.py:176
  30.6 18.9 %collective-permute-start.4 = (bf16[4,480,128]{2,1,0:T(8,128)(2,1)S(1)}, bf16[4,480,128]{2,1,0:T(8,128)(2,1)S(1)}, u32[]{:S(2)}, u32[]{:S(2)}) collective-permute-start(bf16[4,480,128]{2,1,0:T(8,128)(2,1)S(1)} %pad_maximum_fusion.refs_2_), channel_id=1, source_target_pairs={{0,32},{2,34},{4,36},{6,38},{8,12},{10,14},{12,8},{14,10},{16,48},... | collective-permute-start | bytes 1474568 | tf_op jit(solution)/shard_map/ppermute | solution.py:176
  42.3 9.1 %collective-permute-start.7 = (bf16[4,480,128]{2,1,0:T(8,128)(2,1)S(1)}, bf16[4,480,128]{2,1,0:T(8,128)(2,1)S(1)}, u32[]{:S(2)}, u32[]{:S(2)}) collective-permute-start(bf16[4,480,128]{2,1,0:T(8,128)(2,1)S(1)} %get-tuple-element.29), channel_id=1, source_target_pairs={{0,48},{2,50},{4,52},{6,54},{8,14},{10,8},{12,10},{14,12},{16,0},{... | collective-permute-start | bytes 1474568 | tf_op jit(solution)/shard_map/ppermute | solution.py:176
  49.3 14.9 %collective-permute-start.8 = (bf16[4,480,128]{2,1,0:T(8,128)(2,1)S(1)}, bf16[4,480,128]{2,1,0:T(8,128)(2,1)S(1)}, u32[]{:S(2)}, u32[]{:S(2)}) collective-permute-start(bf16[4,480,128]{2,1,0:T(8,128)(2,1)S(1)} %get-tuple-element.32), channel_id=1, source_target_pairs={{0,16},{2,18},{4,20},{6,22},{8,10},{10,12},{12,14},{14,8},{16,32},... | collective-permute-start | bytes 1474568 | tf_op jit(solution)/shard_map/ppermute | solution.py:176
  56.9 9.9 %collective-permute-start.9 = (f32[8,128,128]{2,1,0:T(8,128)S(1)}, f32[8,128,128]{2,1,0:T(8,128)S(1)}, u32[]{:S(2)}, u32[]{:S(2)}) collective-permute-start(f32[8,128,128]{2,1,0:T(8,128)S(1)} %get-tuple-element.34), channel_id=1, source_target_pairs={{0,8},{8,0},{1,9},{9,1},{2,10},{10,2},{3,11},{11,3},{4,12},{12,4},... | collective-permute-start | bytes 1572872 | tf_op jit(solution)/shard_map/ppermute | solution.py:162
  56.9 14.7 %collective-permute-start.10 = (bf16[4,480,128]{2,1,0:T(8,128)(2,1)}, bf16[4,480,128]{2,1,0:T(8,128)(2,1)S(1)}, u32[]{:S(2)}, u32[]{:S(2)}) collective-permute-start(bf16[4,480,128]{2,1,0:T(8,128)(2,1)} %get-tuple-element.36), channel_id=1, source_target_pairs={{0,32},{2,34},{4,36},{6,38},{8,12},{10,14},{12,8},{14,10},{16,48},... | collective-permute-start | bytes 1474568 | tf_op jit(solution)/shard_map/ppermute | solution.py:176
  67.6 14.8 %all-to-all-start.1 = ((bf16[8,128,128]{2,1,0:T(8,128)(2,1)}), bf16[8,128,128]{2,1,0:T(8,128)(2,1)S(1)}, u32[]{:S(2)}, u32[]{:S(2)}) async-start(bf16[8,128,128]{2,1,0:T(8,128)(2,1)} %halves.1.after), calls=%async_computation.1 | async-start | bytes 524288 | tf_op jit(solution)/shard_map/all_to_all | solution.py:166
  71.9 5.3 %collective-permute-start.11 = (bf16[480,128]{1,0:T(8,128)(2,1)S(1)}, bf16[480,128]{1,0:T(8,128)(2,1)S(1)}, u32[]{:S(2)}, u32[]{:S(2)}) collective-permute-start(bf16[480,128]{1,0:T(8,128)(2,1)S(1)} %get-tuple-element.38), channel_id=1, source_target_pairs={{0,6},{2,0},{4,2},{6,4},{8,56},{10,58},{12,60},{14,62},{16,22},{18... | collective-permute-start | bytes 368648 | tf_op jit(solution)/shard_map/ppermute | solution.py:176
  74.7 6.5 %collective-permute-start.12 = (bf16[480,128]{1,0:T(8,128)(2,1)S(1)}, bf16[480,128]{1,0:T(8,128)(2,1)S(1)}, u32[]{:S(2)}, u32[]{:S(2)}) collective-permute-start(bf16[480,128]{1,0:T(8,128)(2,1)S(1)} %get-tuple-element.39), channel_id=1, source_target_pairs={{0,4},{2,6},{4,0},{6,2},{8,40},{10,42},{12,44},{14,46},{16,20},{18... | collective-permute-start | bytes 368648 | tf_op jit(solution)/shard_map/ppermute | solution.py:176
  75.5 6.9 %collective-permute-start.13 = (bf16[480,128]{1,0:T(8,128)(2,1)S(1)}, bf16[480,128]{1,0:T(8,128)(2,1)S(1)}, u32[]{:S(2)}, u32[]{:S(2)}) collective-permute-start(bf16[480,128]{1,0:T(8,128)(2,1)S(1)} %get-tuple-element.40), channel_id=1, source_target_pairs={{0,2},{2,4},{4,6},{6,0},{8,24},{10,26},{12,28},{14,30},{16,18},{18... | collective-permute-start | bytes 368648 | tf_op jit(solution)/shard_map/ppermute | solution.py:176

commit v2 on v1

--- a/solution.py
+++ b/solution.py
@@ -8,6 +8,7 @@
 from jax.sharding import Mesh, PartitionSpec as P
 
 W = 128
+JOIN_COST = 30_000_000_000
 T = 240
 QP = 2 * W + 16
 BF, F32 = jnp.bfloat16, jnp.float32
@@ -75,62 +76,79 @@
         qp[z, 2 * W :, :] = stat
 
 
-SAME, OTHER = ((0, 0), (0, 4)), ((1, 0), (1, 4))
-
-
-def chunk_kernel(groups, given, touched, has_part, refs):
-    qrefs, kv, refs = refs[:2], refs[2], refs[3:]
-    acc_in, refs = dict(zip(given, refs)), refs[len(given) :]
-    part = refs[0] if has_part else None
-    refs = refs[len(refs) - 1 - len(touched) :]
-    out, accs = refs[0], dict(zip(touched, refs[1:]))
-    ks = jnp.concatenate([kv[i, 0:T, :] for i in range(4)], axis=0)
-    vs = jnp.concatenate([kv[i, T:, :] for i in range(4)], axis=0)
-    gk = gv = None
-    for r, at in groups:
-        mem = range(at, at + 4)
-        q = jnp.concatenate([qrefs[r][i, 0:W, :] for i in mem], axis=0)
-        g = jnp.concatenate([qrefs[r][i, W : 2 * W, :] for i in mem], axis=0)
-        stat = jnp.concatenate([qrefs[r][i, 2 * W :, :].astype(F32) for i in mem], axis=1)
-        l2 = stat[0:1] + stat[1:2] + stat[2:3]
-        delta = stat[3:4] + stat[4:5] + stat[5:6]
-        p = jnp.exp2(dot(ks, q, NT) * (FACTOR * LOG2E) - l2)
-        ds = (p * (dot(vs, g, NT) - delta)).astype(BF)
-        dv = dot(p.astype(BF), g, NN)
-        dk = dot(ds, q, NN)
-        gv = dv if gv is None else gv + dv
-        gk = dk if gk is None else gk + dk
-        u = dot(ks, ds, TN)
-        for n, i in enumerate(mem):
-            block = u[:, n * W : (n + 1) * W]
-            accs[r][i] = acc_in[r][i] + block if r in acc_in else block
-    for i in range(4):
-        rows = slice(i * T, (i + 1) * T)
-        for col, total in ((slice(0, T), gk), (slice(T, 2 * T), gv)):
-            block = total[rows]
-            if has_part:
-                block = part[i, col, :] + block
-            out[i, col, :] = block.astype(out.dtype)
-
-
-def chunk(name, queries, kv, acc, dtype, groups=SAME + OTHER, part=None, after=()):
-    touched = sorted({r for r, _ in groups})
+def join_kernel(k0, k1, k2, k3, out):
+    for n, k in enumerate((k0, k1, k2, k3)):
+        out[n] = k[...]
+
+
+def after_kernel(x, after1, after2, out):
+    out[...] = x[...]
+
+
+def tiles_kernel(nq, jobs, touched, given, refs):
+    qrefs, refs = refs[:nq], refs[nq:]
+    kvs, refs = refs[: len(jobs)], refs[len(jobs) :]
+    accs = dict(zip(given, refs))
+    parts = list(refs[len(given) :])
+    refs = refs[len(refs) - len(jobs) - len(touched) :]
+    outs, sums = refs[: len(jobs)], dict(zip(touched, refs[len(jobs) :]))
+    for kv, out, (sets, has_part) in zip(kvs, outs, jobs):
+        part = parts.pop(0) if has_part else None
+        ks = jnp.concatenate([kv[i, 0:T, :] for i in range(4)], axis=0)
+        vs = jnp.concatenate([kv[i, T:, :] for i in range(4)], axis=0)
+        gk = gv = None
+        for r, at in [(r, at) for r in sets for at in (0, 4)]:
+            mem = range(at, at + 4)
+            q = jnp.concatenate([qrefs[r][i, 0:W, :] for i in mem], axis=0)
+            g = jnp.concatenate([qrefs[r][i, W : 2 * W, :] for i in mem], axis=0)
+            stat = jnp.concatenate([qrefs[r][i, 2 * W :, :].astype(F32) for i in mem], axis=1)
+            l2 = stat[0:1] + stat[1:2] + stat[2:3]
+            delta = stat[3:4] + stat[4:5] + stat[5:6]
+            p = jnp.exp2(dot(ks, q, NT) * (FACTOR * LOG2E) - l2)
+            ds = (p * (dot(vs, g, NT) - delta)).astype(BF)
+            dv = dot(p.astype(BF), g, NN)
+            dk = dot(ds, q, NN)
+            gv = dv if gv is None else gv + dv
+            gk = dk if gk is None else gk + dk
+            u = dot(ks, ds, TN)
+            for n, i in enumerate(mem):
+                block = u[:, n * W : (n + 1) * W]
+                sums[r][i] = accs[r][i] + block if r in accs else block
+        for r in sets:
+            accs[r] = sums[r]
+        for i in range(4):
+            rows = slice(i * T, (i + 1) * T)
+            for col, total in ((slice(0, T), gk), (slice(T, 2 * T), gv)):
+                block = total[rows]
+                if has_part:
+                    block = part[i, col, :] + block
+                out[i, col, :] = block.astype(out.dtype)
+
+
+def tiles(name, queries, jobs, acc, after=()):
+    touched = sorted({r for _, sets, _, _ in jobs for r in sets})
     given = [r for r in touched if r in acc]
-    outs = (sds((4, 2 * T, W), dtype),) + (sds((8, W, W), F32),) * len(touched)
-    args = tuple(queries) + (kv,)
-    aliases = {len(args) + n: 1 + touched.index(r) for n, r in enumerate(given)}
+    outs = tuple(sds((4, 2 * T, W), dtype) for _, _, dtype, _ in jobs)
+    outs += (sds((8, W, W), F32),) * len(touched)
+    args = tuple(queries) + tuple(job[0] for job in jobs)
+    aliases = {len(args) + n: len(jobs) + touched.index(r) for n, r in enumerate(given)}
     args += tuple(acc[r] for r in given)
-    if part is not None:
-        aliases[len(args)] = 0
-        args += (part,)
+    for n, job in enumerate(jobs):
+        if job[3] is not None:
+            if job[2] == F32:
+                aliases[len(args)] = n
+            args += (job[3],)
     spaces = [VM] * len(args) + [ANY] * len(after)
+    args += tuple(after)
+    static = [(sets, part is not None) for _, sets, _, part in jobs]
 
     def kernel(*refs):
-        chunk_kernel(groups, given, touched, part is not None, refs)
-
-    flops = 10 * 960 * 512 * len(groups) * W
-    out = call(kernel, name, outs, args + tuple(after), flops, aliases, spaces)
-    return out[0], {**acc, **dict(zip(touched, out[1:]))}
+        ins = refs[: len(args) - len(after)]
+        tiles_kernel(len(queries), static, touched, given, ins + refs[len(args) :])
+
+    flops = sum(10 * 960 * 1024 * len(sets) * W for sets, _ in static)
+    out = call(kernel, name, outs, args, flops, aliases, spaces)
+    return out[: len(jobs)], {**acc, **dict(zip(touched, out[len(jobs) :]))}
 
 
 def merge_kernel(own, b1, b2, b3, after, *outs):
@@ -193,20 +211,30 @@
         vmem=60,
     )
     same = exchange_z(qp)
-    other = swap_cores(same)
-    kv0 = jnp.stack([kv] + [send_plane(kv, r, 0) for r in (1, 2, 3)])
-    kvs = {s: send_plane(kv0, s, 1) for s in (1, 3, 2)}
-
-    qs = (same, other)
-    part, acc = chunk("chunk0a", qs, kv0, {}, F32, OTHER)
-    out1, acc = chunk("chunk1", qs, kvs[1], acc, BF)
-    back1 = send_plane(out1, -1, 1)
-    out3, acc = chunk("chunk3", qs, kvs[3], acc, BF)
-    back3 = send_plane(out3, -3, 1)
-    out2, acc = chunk("chunk2", qs, kvs[2], acc, BF, after=(back1,))
-    back2 = send_plane(out2, -2, 1)
-    rs = swap_cores(acc[1])
-    out0, acc = chunk("chunk0b", qs, kv0, acc, F32, SAME, part, (back3,))
+    (kv0,) = call(
+        join_kernel,
+        "join",
+        (sds((4, 2 * T, W), BF),),
+        (kv, *(send_plane(kv, r, 0) for r in (1, 2, 3))),
+        flops=JOIN_COST,
+    )
+    kv1, kv3, kv2 = (send_plane(kv0, s, 1) for s in (1, 3, 2))
+    (same,) = call(after_kernel, "same", (sds((8, QP, W), BF),), (same, kv1, kv3), spaces=[VM, ANY, ANY])
+
+    qs = (same, swap_cores(same))
+    (part1, part3), acc = tiles(
+        "tiles13a", qs[:1], ((kv1, (0,), F32, None), (kv3, (0,), F32, None)), {}
+    )
+    (out1, out3, part0), acc = tiles(
+        "tiles130",
+        qs,
+        ((kv1, (1,), BF, part1), (kv3, (1,), BF, part3), (kv0, (1,), F32, None)),
+        acc,
+    )
+    back1, back3 = send_plane(out1, -1, 1), send_plane(out3, -3, 1)
+    (out2,), acc = tiles("tiles2", qs, ((kv2, (0, 1), BF, None),), acc)
+    rs, back2 = swap_cores(acc[1]), send_plane(out2, -2, 1)
+    (out0,), acc = tiles("tiles0", qs, ((kv0, (0,), F32, part0),), acc, (back1, back3))
 
     (halves,) = call(halves_kernel, "halves", (sds((8, W, W), BF),), (acc[0], rs))
     u = exchange_z(halves)

time: 83.5 us -> 77.7 us (0.931)
  starting transfers between devices: 36.7 us -> 32.4 us
  waiting for transfers between devices: 21.7 us -> 20.3 us
    all_to_all x2, waiting for transfers between devices: 11.5 us -> 4.77 us  [exchange_z(): return lax.all_to_all(x, ('zl', 'zh'), 0, 0, tiled=True)]
    ppermute x12, waiting for transfers between devices: 10.2 us -> 15.5 us  [send_plane(): return lax.ppermute(x, ('y', 'core', 'x'), pairs)]
    ppermute x12, starting transfers between devices: 23.9 us -> 19.2 us  [send_plane(): return lax.ppermute(x, ('y', 'core', 'x'), pairs)]
    pallas_call x9 -> x10, Pallas kernels: 24 us -> 24 us  [call(): pl.pallas_call(kernel, name=name, out_shape=outs, in_specs=spaces or [VM]...]
  transfers between devices with their start and end apart: 16 -> 16, of which waited for: 6 -> 7; matrix products, arithmetic and copies ran while one was open for 0% -> 0% of each run, Pallas kernels for 26% -> 28%
where the time goes in v2:
time: 77.7 us; the launch traced here: 77.4 us
  starting transfers between devices  32.4 us (42%)
  Pallas kernels  24 us (31%)
  waiting for transfers between devices  20.3 us (26%)
    pallas_call x10, Pallas kernels, call(): pl.pallas_call(kernel, name=name, out_shape=outs, in_specs=spaces or [VM]...  24 us
    ppermute x12, starting transfers between devices, send_plane(): return lax.ppermute(x, ('y', 'core', 'x'), pairs)  19.2 us
    ppermute x12, waiting for transfers between devices, send_plane(): return lax.ppermute(x, ('y', 'core', 'x'), pairs)  15.5 us
    all_to_all x2, starting transfers between devices, exchange_z(): return lax.all_to_all(x, ('zl', 'zh'), 0, 0, tiled=True)  12.8 us
    all_to_all x2, waiting for transfers between devices, exchange_z(): return lax.all_to_all(x, ('zl', 'zh'), 0, 0, tiled=True)  4.77 us
  transfers between devices with their start and end apart: 16, of which 7 were waited for; matrix products, arithmetic and copies ran while one was open for 0% of the time, Pallas kernels for 28%

profile of v2, /device:TPU:32, one launch (start us, length us, event | category | flops | bytes accessed | tf_op | source)
XLA Modules:
  0.0 77.4 jit_solution(8714115608226714997)
XLA Ops:
  0.6 1.9 %pack.1 = (bf16[8,272,128]{2,1,0:T(8,128)(2,1)}, bf16[480,128]{1,0:T(8,128)(2,1)}) custom-call(bf16[128,128]{1,0:T(8,128)(2,1)} %q.1, bf16[128,128]{1,0:T(8,128)(2,1)} %g.1, bf16[128,128]{1,0:T(8,128)(2,1)} %o.1, f32[1,128]{1,0:T(1,128)} %bitcast.1, bf16[240,128]{1,0:T(8,128)(2,1)} %k.1, bf16[240,128]{1,0:T(8,128)(2,1)} %v.1), custom_call_target="tpu_custom_call" | custom-call | bytes 901632 | tf_op jit(solution)/shard_map/pack/pallas_call | solution.py:30
  2.5 1.6 %collective-permute-start = (bf16[480,128]{1,0:T(8,128)(2,1)}, bf16[480,128]{1,0:T(8,128)(2,1)S(1)}, u32[]{:S(2)}, u32[]{:S(2)}) collective-permute-start(bf16[480,128]{1,0:T(8,128)(2,1)} %get-tuple-element.22.k0), channel_id=1, source_target_pairs={{0,2},{2,4},{4,6},{6,0},{8,24},{10,26},{12,28},{14,30},{16,18},{18... | collective-permute-start | bytes 368648 | tf_op jit(solution)/shard_map/ppermute | solution.py:194
  4.1 2.7 %collective-permute-start.1 = (bf16[480,128]{1,0:T(8,128)(2,1)}, bf16[480,128]{1,0:T(8,128)(2,1)S(1)}, u32[]{:S(2)}, u32[]{:S(2)}) collective-permute-start(bf16[480,128]{1,0:T(8,128)(2,1)} %get-tuple-element.22.k0), channel_id=1, source_target_pairs={{0,4},{2,6},{4,0},{6,2},{8,40},{10,42},{12,44},{14,46},{16,20},{18... | collective-permute-start | bytes 368648 | tf_op jit(solution)/shard_map/ppermute | solution.py:194
  6.8 1.4 %collective-permute-start.2 = (bf16[480,128]{1,0:T(8,128)(2,1)}, bf16[480,128]{1,0:T(8,128)(2,1)S(1)}, u32[]{:S(2)}, u32[]{:S(2)}) collective-permute-start(bf16[480,128]{1,0:T(8,128)(2,1)} %get-tuple-element.22.k0), channel_id=1, source_target_pairs={{0,6},{2,0},{4,2},{6,4},{8,56},{10,58},{12,60},{14,62},{16,22},{18... | collective-permute-start | bytes 368648 | tf_op jit(solution)/shard_map/ppermute | solution.py:194
  8.2 0.0 copy-start
  8.2 8.7 %all-to-all-start = ((bf16[8,272,128]{2,1,0:T(8,128)(2,1)}), bf16[8,272,128]{2,1,0:T(8,128)(2,1)S(1)}, u32[]{:S(2)}, u32[]{:S(2)}) async-start(bf16[8,272,128]{2,1,0:T(8,128)(2,1)} %get-tuple-element.21), calls=%async_computation | async-start | bytes 1114112 | tf_op jit(solution)/shard_map/all_to_all | solution.py:184
  16.9 0.0 collective-permute-done.k1
  16.9 0.0 collective-permute-done.1.k2
  17.0 0.0 collective-permute-done.2.k3
  17.0 0.0 copy-done
  17.0 1.7 %collective-permute-start.3 = (bf16[4,480,128]{2,1,0:T(8,128)(2,1)S(1)}, bf16[4,480,128]{2,1,0:T(8,128)(2,1)S(1)}, u32[]{:S(2)}, u32[]{:S(2)}) collective-permute-start(bf16[4,480,128]{2,1,0:T(8,128)(2,1)S(1)} %join.1.refs_4_.refs_2_), channel_id=1, source_target_pairs={{0,16},{2,18},{4,20},{6,22},{8,10},{10,12},{12,14},{14,8},{16,32},... | collective-permute-start | bytes 1474568 | tf_op jit(solution)/shard_map/ppermute | solution.py:194
  18.7 1.7 %collective-permute-start.4 = (bf16[4,480,128]{2,1,0:T(8,128)(2,1)S(1)}, bf16[4,480,128]{2,1,0:T(8,128)(2,1)S(1)}, u32[]{:S(2)}, u32[]{:S(2)}) collective-permute-start(bf16[4,480,128]{2,1,0:T(8,128)(2,1)S(1)} %join.1.refs_4_.refs_2_), channel_id=1, source_target_pairs={{0,48},{2,50},{4,52},{6,54},{8,14},{10,8},{12,10},{14,12},{16,0},{... | collective-permute-start | bytes 1474568 | tf_op jit(solution)/shard_map/ppermute | solution.py:194
  20.3 6.8 %collective-permute-done.3.after1.refs_1_.refs_2_ = bf16[4,480,128]{2,1,0:T(8,128)(2,1)S(1)} collective-permute-done((bf16[4,480,128]{2,1,0:T(8,128)(2,1)S(1)}, bf16[4,480,128]{2,1,0:T(8,128)(2,1)S(1)}, u32[]{:S(2)}, u32[]{:S(2)}) %collective-permute-start.3) | collective-permute-done | bytes 491552 | tf_op jit(solution)/shard_map/ppermute | solution.py:194
  27.1 0.4 collective-permute-done.4.after2.refs_2_.refs_3_
  27.5 4.8 %all-to-all-done.x = bf16[8,272,128]{2,1,0:T(8,128)(2,1)S(1)} async-done(((bf16[8,272,128]{2,1,0:T(8,128)(2,1)}), bf16[8,272,128]{2,1,0:T(8,128)(2,1)S(1)}, u32[]{:S(2)}, u32[]{:S(2)}) %all-to-all-start) | async-done | bytes 557088 | tf_op jit(solution)/shard_map/all_to_all | solution.py:184
  32.3 0.1 collective-permute-start.5
  32.4 0.8 collective-permute-start.6
  33.2 4.9 %tiles13a.1 = (f32[4,480,128]{2,1,0:T(8,128)S(1)}, f32[4,480,128]{2,1,0:T(8,128)S(1)}, f32[8,128,128]{2,1,0:T(8,128)S(1)}) custom-call(bf16[8,272,128]{2,1,0:T(8,128)(2,1)S(1)} %same.1.refs_0_, bf16[4,480,128]{2,1,0:T(8,128)(2,1)S(1)} %collective-permute-done.3.after1.refs_1_.refs_2_, bf16[4,480,128]{2,1,0:T(8,128)(2,1)S(1)} %collective-permute-done.4.after2.refs_2_.refs_3_), custom_call_target="tpu_custom_call" | custom-call | flops 2516582400 | bytes 4030464 | tf_op jit(solution)/shard_map/tiles13a/pallas_call | solution.py:30
  38.0 0.0 collective-permute-done.5.refs_1_
  38.0 7.3 %tiles130.1 = (bf16[4,480,128]{2,1,0:T(8,128)(2,1)S(1)}, bf16[4,480,128]{2,1,0:T(8,128)(2,1)S(1)}, f32[4,480,128]{2,1,0:T(8,128)S(1)}, f32[8,128,128]{2,1,0:T(8,128)S(1)}) custom-call(bf16[8,272,128]{2,1,0:T(8,128)(2,1)S(1)} %same.1.refs_0_, bf16[8,272,128]{2,1,0:T(8,128)(2,1)S(1)} %collective-permute-done.5.refs_1_, ...), custom_call_target="tpu_custom_call" | custom-call | flops 3774873600 | bytes 7045120 | tf_op jit(solution)/shard_map/tiles130/pallas_call | solution.py:30
  45.3 2.9 %collective-permute-start.7 = (bf16[4,480,128]{2,1,0:T(8,128)(2,1)S(1)}, bf16[4,480,128]{2,1,0:T(8,128)(2,1)S(1)}, u32[]{:S(2)}, u32[]{:S(2)}) collective-permute-start(bf16[4,480,128]{2,1,0:T(8,128)(2,1)S(1)} %get-tuple-element.29), channel_id=1, source_target_pairs={{0,48},{2,50},{4,52},{6,54},{8,14},{10,8},{12,10},{14,12},{16,0},{... | collective-permute-start | bytes 1474568 | tf_op jit(solution)/shard_map/ppermute | solution.py:194
  48.3 0.0 collective-permute-start.8
  48.3 0.0 collective-permute-done.6.refs_2_
  48.3 5.5 %tiles2.1 = (bf16[4,480,128]{2,1,0:T(8,128)(2,1)}, f32[8,128,128]{2,1,0:T(8,128)S(1)}, f32[8,128,128]{2,1,0:T(8,128)S(1)}) custom-call(bf16[8,272,128]{2,1,0:T(8,128)(2,1)S(1)} %same.1.refs_0_, bf16[8,272,128]{2,1,0:T(8,128)(2,1)S(1)} %collective-permute-done.5.refs_1_, ...), custom_call_target="tpu_custom_call", output_to_operand_aliasing={{1}: (3, {}), {2}: (4, {})} | custom-call | flops 2516582400 | bytes 4194304 | tf_op jit(solution)/shard_map/tiles2/pallas_call | solution.py:30
  53.8 0.3 collective-permute-start.9
  54.1 1.9 %collective-permute-start.10 = (bf16[4,480,128]{2,1,0:T(8,128)(2,1)}, bf16[4,480,128]{2,1,0:T(8,128)(2,1)S(1)}, u32[]{:S(2)}, u32[]{:S(2)}) collective-permute-start(bf16[4,480,128]{2,1,0:T(8,128)(2,1)} %get-tuple-element.34), channel_id=1, source_target_pairs={{0,32},{2,34},{4,36},{6,38},{8,12},{10,14},{12,8},{14,10},{16,48},... | collective-permute-start | bytes 1474568 | tf_op jit(solution)/shard_map/ppermute | solution.py:194
  56.0 0.0 collective-permute-done.7.refs_5_.b1
  56.0 2.3 %collective-permute-done.8.refs_6_.b3 = bf16[4,480,128]{2,1,0:T(8,128)(2,1)S(1)} collective-permute-done((bf16[4,480,128]{2,1,0:T(8,128)(2,1)S(1)}, bf16[4,480,128]{2,1,0:T(8,128)(2,1)S(1)}, u32[]{:S(2)}, u32[]{:S(2)}) %collective-permute-start.8) | collective-permute-done | bytes 491552 | tf_op jit(solution)/shard_map/ppermute | solution.py:194
  58.3 2.6 %tiles0.1 = (f32[4,480,128]{2,1,0:T(8,128)S(1)}, f32[8,128,128]{2,1,0:T(8,128)S(1)}) custom-call(bf16[8,272,128]{2,1,0:T(8,128)(2,1)S(1)} %same.1.refs_0_, bf16[8,272,128]{2,1,0:T(8,128)(2,1)S(1)} %collective-permute-done.5.refs_1_, bf16[4,480,128]{2,1,0:T(8,128)(2,1)S(1)} %join.1.refs_4_.refs_2_, ...), custom_call_target="tpu_custom_call", output_to_operand_aliasing={{1}: (3, {}), {0}: (4, {})} | custom-call | flops 1258291200 | bytes 5603328 | tf_op jit(solution)/shard_map/tiles0/pallas_call | solution.py:30
  61.0 0.0 collective-permute-done.9.got
  61.0 0.7 halves.1.after
  61.7 4.1 %all-to-all-start.1 = ((bf16[8,128,128]{2,1,0:T(8,128)(2,1)}), bf16[8,128,128]{2,1,0:T(8,128)(2,1)S(1)}, u32[]{:S(2)}, u32[]{:S(2)}) async-start(bf16[8,128,128]{2,1,0:T(8,128)(2,1)} %halves.1.after), calls=%async_computation.1 | async-start | bytes 524288 | tf_op jit(solution)/shard_map/all_to_all | solution.py:184
  65.8 0.0 collective-permute-done.10.b2
  65.8 0.2 merge.1
  66.0 2.9 %collective-permute-start.11 = (bf16[480,128]{1,0:T(8,128)(2,1)S(1)}, bf16[480,128]{1,0:T(8,128)(2,1)S(1)}, u32[]{:S(2)}, u32[]{:S(2)}) collective-permute-start(bf16[480,128]{1,0:T(8,128)(2,1)S(1)} %get-tuple-element.36), channel_id=1, source_target_pairs={{0,6},{2,0},{4,2},{6,4},{8,56},{10,58},{12,60},{14,62},{16,22},{18... | collective-permute-start | bytes 368648 | tf_op jit(solution)/shard_map/ppermute | solution.py:194
  68.9 0.8 collective-permute-start.12
  69.7 0.9 %collective-permute-start.13 = (bf16[480,128]{1,0:T(8,128)(2,1)S(1)}, bf16[480,128]{1,0:T(8,128)(2,1)S(1)}, u32[]{:S(2)}, u32[]{:S(2)}) collective-permute-start(bf16[480,128]{1,0:T(8,128)(2,1)S(1)} %get-tuple-element.38), channel_id=1, source_target_pairs={{0,2},{2,4},{4,6},{6,0},{8,24},{10,26},{12,28},{14,30},{16,18},{18... | collective-permute-start | bytes 368648 | tf_op jit(solution)/shard_map/ppermute | solution.py:194
  70.6 0.7 collective-permute-done.11.f1
  71.3 4.0 %collective-permute-done.12.f2 = bf16[480,128]{1,0:T(8,128)(2,1)S(1)} collective-permute-done((bf16[480,128]{1,0:T(8,128)(2,1)S(1)}, bf16[480,128]{1,0:T(8,128)(2,1)S(1)}, u32[]{:S(2)}, u32[]{:S(2)}) %collective-permute-start.12) | collective-permute-done | bytes 122912 | tf_op jit(solution)/shard_map/ppermute | solution.py:194
  75.4 1.2 %collective-permute-done.13.f3 = bf16[480,128]{1,0:T(8,128)(2,1)S(1)} collective-permute-done((bf16[480,128]{1,0:T(8,128)(2,1)S(1)}, bf16[480,128]{1,0:T(8,128)(2,1)S(1)}, u32[]{:S(2)}, u32[]{:S(2)}) %collective-permute-start.13) | collective-permute-done | bytes 122912 | tf_op jit(solution)/shard_map/ppermute | solution.py:194
  76.6 0.0 all-to-all-done.1.u
  76.6 0.8 %last.1 = (f32[128,128]{1,0:T(8,128)}, f32[240,128]{1,0:T(8,128)}, f32[240,128]{1,0:T(8,128)}) custom-call(bf16[8,128,128]{2,1,0:T(8,128)(2,1)S(1)} %all-to-all-done.1.u, f32[480,128]{1,0:T(8,128)S(1)} %get-tuple-element.35.own, bf16[480,128]{1,0:T(8,128)(2,1)S(1)} %collective-permute-done.11.f1, bf16[480,128]{1,0:T(8,128)(2,1)S(1)} %collective-permute-done.12.f2, ...), custom_call_target="tpu_custom_call" | custom-call | bytes 1187840 | tf_op jit(solution)/shard_map/last/pallas_call | solution.py:30
  (2 shorter events, 0.1 us)
Async XLA Ops:
  2.5 14.4 %collective-permute-start = (bf16[480,128]{1,0:T(8,128)(2,1)}, bf16[480,128]{1,0:T(8,128)(2,1)S(1)}, u32[]{:S(2)}, u32[]{:S(2)}) collective-permute-start(bf16[480,128]{1,0:T(8,128)(2,1)} %get-tuple-element.22.k0), channel_id=1, source_target_pairs={{0,2},{2,4},{4,6},{6,0},{8,24},{10,26},{12,28},{14,30},{16,18},{18... | collective-permute-start | bytes 368648 | tf_op jit(solution)/shard_map/ppermute | solution.py:194
  4.1 12.9 %collective-permute-start.1 = (bf16[480,128]{1,0:T(8,128)(2,1)}, bf16[480,128]{1,0:T(8,128)(2,1)S(1)}, u32[]{:S(2)}, u32[]{:S(2)}) collective-permute-start(bf16[480,128]{1,0:T(8,128)(2,1)} %get-tuple-element.22.k0), channel_id=1, source_target_pairs={{0,4},{2,6},{4,0},{6,2},{8,40},{10,42},{12,44},{14,46},{16,20},{18... | collective-permute-start | bytes 368648 | tf_op jit(solution)/shard_map/ppermute | solution.py:194
  6.8 10.2 %collective-permute-start.2 = (bf16[480,128]{1,0:T(8,128)(2,1)}, bf16[480,128]{1,0:T(8,128)(2,1)S(1)}, u32[]{:S(2)}, u32[]{:S(2)}) collective-permute-start(bf16[480,128]{1,0:T(8,128)(2,1)} %get-tuple-element.22.k0), channel_id=1, source_target_pairs={{0,6},{2,0},{4,2},{6,4},{8,56},{10,58},{12,60},{14,62},{16,22},{18... | collective-permute-start | bytes 368648 | tf_op jit(solution)/shard_map/ppermute | solution.py:194
  8.2 8.7 %copy-start = (bf16[480,128]{1,0:T(8,128)(2,1)S(1)}, bf16[480,128]{1,0:T(8,128)(2,1)}, u32[]{:S(2)}) copy-start(bf16[480,128]{1,0:T(8,128)(2,1)} %get-tuple-element.22.k0) | copy-start | bytes 368644
  8.2 24.0 %all-to-all-start = ((bf16[8,272,128]{2,1,0:T(8,128)(2,1)}), bf16[8,272,128]{2,1,0:T(8,128)(2,1)S(1)}, u32[]{:S(2)}, u32[]{:S(2)}) async-start(bf16[8,272,128]{2,1,0:T(8,128)(2,1)} %get-tuple-element.21), calls=%async_computation | async-start | bytes 1114112 | tf_op jit(solution)/shard_map/all_to_all | solution.py:184
  17.0 10.1 %collective-permute-start.3 = (bf16[4,480,128]{2,1,0:T(8,128)(2,1)S(1)}, bf16[4,480,128]{2,1,0:T(8,128)(2,1)S(1)}, u32[]{:S(2)}, u32[]{:S(2)}) collective-permute-start(bf16[4,480,128]{2,1,0:T(8,128)(2,1)S(1)} %join.1.refs_4_.refs_2_), channel_id=1, source_target_pairs={{0,16},{2,18},{4,20},{6,22},{8,10},{10,12},{12,14},{14,8},{16,32},... | collective-permute-start | bytes 1474568 | tf_op jit(solution)/shard_map/ppermute | solution.py:194
  18.7 8.8 %collective-permute-start.4 = (bf16[4,480,128]{2,1,0:T(8,128)(2,1)S(1)}, bf16[4,480,128]{2,1,0:T(8,128)(2,1)S(1)}, u32[]{:S(2)}, u32[]{:S(2)}) collective-permute-start(bf16[4,480,128]{2,1,0:T(8,128)(2,1)S(1)} %join.1.refs_4_.refs_2_), channel_id=1, source_target_pairs={{0,48},{2,50},{4,52},{6,54},{8,14},{10,8},{12,10},{14,12},{16,0},{... | collective-permute-start | bytes 1474568 | tf_op jit(solution)/shard_map/ppermute | solution.py:194
  32.3 5.7 %collective-permute-start.5 = (bf16[8,272,128]{2,1,0:T(8,128)(2,1)S(1)}, bf16[8,272,128]{2,1,0:T(8,128)(2,1)S(1)}, u32[]{:S(2)}, u32[]{:S(2)}) collective-permute-start(bf16[8,272,128]{2,1,0:T(8,128)(2,1)S(1)} %same.1.refs_0_), channel_id=1, source_target_pairs={{0,8},{8,0},{1,9},{9,1},{2,10},{10,2},{3,11},{11,3},{4,12},{12,4},... | collective-permute-start | bytes 1671176 | tf_op jit(solution)/shard_map/ppermute | solution.py:180
  32.4 15.9 %collective-permute-start.6 = (bf16[4,480,128]{2,1,0:T(8,128)(2,1)S(1)}, bf16[4,480,128]{2,1,0:T(8,128)(2,1)S(1)}, u32[]{:S(2)}, u32[]{:S(2)}) collective-permute-start(bf16[4,480,128]{2,1,0:T(8,128)(2,1)S(1)} %join.1.refs_4_.refs_2_), channel_id=1, source_target_pairs={{0,32},{2,34},{4,36},{6,38},{8,12},{10,14},{12,8},{14,10},{16,48},... | collective-permute-start | bytes 1474568 | tf_op jit(solution)/shard_map/ppermute | solution.py:194
  45.3 10.7 %collective-permute-start.7 = (bf16[4,480,128]{2,1,0:T(8,128)(2,1)S(1)}, bf16[4,480,128]{2,1,0:T(8,128)(2,1)S(1)}, u32[]{:S(2)}, u32[]{:S(2)}) collective-permute-start(bf16[4,480,128]{2,1,0:T(8,128)(2,1)S(1)} %get-tuple-element.29), channel_id=1, source_target_pairs={{0,48},{2,50},{4,52},{6,54},{8,14},{10,8},{12,10},{14,12},{16,0},{... | collective-permute-start | bytes 1474568 | tf_op jit(solution)/shard_map/ppermute | solution.py:194
  48.3 10.0 %collective-permute-start.8 = (bf16[4,480,128]{2,1,0:T(8,128)(2,1)S(1)}, bf16[4,480,128]{2,1,0:T(8,128)(2,1)S(1)}, u32[]{:S(2)}, u32[]{:S(2)}) collective-permute-start(bf16[4,480,128]{2,1,0:T(8,128)(2,1)S(1)} %get-tuple-element.30), channel_id=1, source_target_pairs={{0,16},{2,18},{4,20},{6,22},{8,10},{10,12},{12,14},{14,8},{16,32},... | collective-permute-start | bytes 1474568 | tf_op jit(solution)/shard_map/ppermute | solution.py:194
  53.8 7.2 %collective-permute-start.9 = (f32[8,128,128]{2,1,0:T(8,128)S(1)}, f32[8,128,128]{2,1,0:T(8,128)S(1)}, u32[]{:S(2)}, u32[]{:S(2)}) collective-permute-start(f32[8,128,128]{2,1,0:T(8,128)S(1)} %get-tuple-element.32), channel_id=1, source_target_pairs={{0,8},{8,0},{1,9},{9,1},{2,10},{10,2},{3,11},{11,3},{4,12},{12,4},... | collective-permute-start | bytes 1572872 | tf_op jit(solution)/shard_map/ppermute | solution.py:180
  54.1 11.7 %collective-permute-start.10 = (bf16[4,480,128]{2,1,0:T(8,128)(2,1)}, bf16[4,480,128]{2,1,0:T(8,128)(2,1)S(1)}, u32[]{:S(2)}, u32[]{:S(2)}) collective-permute-start(bf16[4,480,128]{2,1,0:T(8,128)(2,1)} %get-tuple-element.34), channel_id=1, source_target_pairs={{0,32},{2,34},{4,36},{6,38},{8,12},{10,14},{12,8},{14,10},{16,48},... | collective-permute-start | bytes 1474568 | tf_op jit(solution)/shard_map/ppermute | solution.py:194
  61.7 14.9 %all-to-all-start.1 = ((bf16[8,128,128]{2,1,0:T(8,128)(2,1)}), bf16[8,128,128]{2,1,0:T(8,128)(2,1)S(1)}, u32[]{:S(2)}, u32[]{:S(2)}) async-start(bf16[8,128,128]{2,1,0:T(8,128)(2,1)} %halves.1.after), calls=%async_computation.1 | async-start | bytes 524288 | tf_op jit(solution)/shard_map/all_to_all | solution.py:184
  66.0 5.3 %collective-permute-start.11 = (bf16[480,128]{1,0:T(8,128)(2,1)S(1)}, bf16[480,128]{1,0:T(8,128)(2,1)S(1)}, u32[]{:S(2)}, u32[]{:S(2)}) collective-permute-start(bf16[480,128]{1,0:T(8,128)(2,1)S(1)} %get-tuple-element.36), channel_id=1, source_target_pairs={{0,6},{2,0},{4,2},{6,4},{8,56},{10,58},{12,60},{14,62},{16,22},{18... | collective-permute-start | bytes 368648 | tf_op jit(solution)/shard_map/ppermute | solution.py:194
  68.9 6.5 %collective-permute-start.12 = (bf16[480,128]{1,0:T(8,128)(2,1)S(1)}, bf16[480,128]{1,0:T(8,128)(2,1)S(1)}, u32[]{:S(2)}, u32[]{:S(2)}) collective-permute-start(bf16[480,128]{1,0:T(8,128)(2,1)S(1)} %get-tuple-element.37), channel_id=1, source_target_pairs={{0,4},{2,6},{4,0},{6,2},{8,40},{10,42},{12,44},{14,46},{16,20},{18... | collective-permute-start | bytes 368648 | tf_op jit(solution)/shard_map/ppermute | solution.py:194
  69.7 6.9 %collective-permute-start.13 = (bf16[480,128]{1,0:T(8,128)(2,1)S(1)}, bf16[480,128]{1,0:T(8,128)(2,1)S(1)}, u32[]{:S(2)}, u32[]{:S(2)}) collective-permute-start(bf16[480,128]{1,0:T(8,128)(2,1)S(1)} %get-tuple-element.38), channel_id=1, source_target_pairs={{0,2},{2,4},{4,6},{6,0},{8,24},{10,26},{12,28},{14,30},{16,18},{18... | collective-permute-start | bytes 368648 | tf_op jit(solution)/shard_map/ppermute | solution.py:194

commit v3 on v2

--- a/solution.py
+++ b/solution.py
@@ -8,7 +8,9 @@
 from jax.sharding import Mesh, PartitionSpec as P
 
 W = 128
-JOIN_COST = 30_000_000_000
+JOIN_COST = 20_000_000_000
+FIRST_COST = 20_000_000_000
+CHIP_COST = 20_000_000_000
 T = 240
 QP = 2 * W + 16
 BF, F32 = jnp.bfloat16, jnp.float32
@@ -70,10 +72,14 @@
     stat = jnp.concatenate(rows, axis=0).astype(BF)
     for copy in copies[3:]:
         copy.wait()
-    for z in range(8):
-        qp[z, 0:W, :] = qbuf[...]
-        qp[z, W : 2 * W, :] = gbuf[...]
-        qp[z, 2 * W :, :] = stat
+    qp[0:W, :] = qbuf[...]
+    qp[W : 2 * W, :] = gbuf[...]
+    qp[2 * W :, :] = stat
+
+
+def pair_kernel(q0, q1, out):
+    out[0] = q0[...]
+    out[1] = q1[...]
 
 
 def join_kernel(k0, k1, k2, k3, out):
@@ -81,8 +87,28 @@
         out[n] = k[...]
 
 
-def after_kernel(x, after1, after2, out):
+def after_kernel(x, after, out):
     out[...] = x[...]
+
+
+def first_kernel(q, out):
+    out[...] = q[0:1]
+
+
+def gather_kernel(q1, q2, q3, q4, kv1, kv3, out):
+    for n, q in enumerate((q1, q2, q3)):
+        out[2 * n : 2 * n + 2] = q[...]
+    out[6:7] = q4[...]
+
+
+GROUPS = (
+    ((0, 0), (1, 0), (1, 2), (1, 4)),
+    ((1, 6), (2, 1), (2, 3), (2, 5)),
+    ((0, 1), (1, 1), (1, 3), (1, 5)),
+    ((2, 0), (2, 2), (2, 4), (2, 6)),
+)
+UP = (0, -1, -2, -3, -4, 1, 2, 3)
+TWIN = (0, 4, 5, 6, 7, 1, 2, 3)
 
 
 def tiles_kernel(nq, jobs, touched, given, refs):
@@ -97,11 +123,11 @@
         ks = jnp.concatenate([kv[i, 0:T, :] for i in range(4)], axis=0)
         vs = jnp.concatenate([kv[i, T:, :] for i in range(4)], axis=0)
         gk = gv = None
-        for r, at in [(r, at) for r in sets for at in (0, 4)]:
-            mem = range(at, at + 4)
-            q = jnp.concatenate([qrefs[r][i, 0:W, :] for i in mem], axis=0)
-            g = jnp.concatenate([qrefs[r][i, W : 2 * W, :] for i in mem], axis=0)
-            stat = jnp.concatenate([qrefs[r][i, 2 * W :, :].astype(F32) for i in mem], axis=1)
+        for c in sets:
+            mem = GROUPS[c]
+            q = jnp.concatenate([qrefs[r][i, 0:W, :] for r, i in mem], axis=0)
+            g = jnp.concatenate([qrefs[r][i, W : 2 * W, :] for r, i in mem], axis=0)
+            stat = jnp.concatenate([qrefs[r][i, 2 * W :, :].astype(F32) for r, i in mem], axis=1)
             l2 = stat[0:1] + stat[1:2] + stat[2:3]
             delta = stat[3:4] + stat[4:5] + stat[5:6]
             p = jnp.exp2(dot(ks, q, NT) * (FACTOR * LOG2E) - l2)
@@ -111,11 +137,10 @@
             gv = dv if gv is None else gv + dv
             gk = dk if gk is None else gk + dk
             u = dot(ks, ds, TN)
-            for n, i in enumerate(mem):
+            for n in range(4):
                 block = u[:, n * W : (n + 1) * W]
-                sums[r][i] = accs[r][i] + block if r in accs else block
-        for r in sets:
-            accs[r] = sums[r]
+                sums[c][n] = accs[c][n] + block if c in accs else block
+            accs[c] = sums[c]
         for i in range(4):
             rows = slice(i * T, (i + 1) * T)
             for col, total in ((slice(0, T), gk), (slice(T, 2 * T), gv)):
@@ -126,10 +151,10 @@
 
 
 def tiles(name, queries, jobs, acc, after=()):
-    touched = sorted({r for _, sets, _, _ in jobs for r in sets})
+    touched = sorted({c for _, sets, _, _ in jobs for c in sets})
     given = [r for r in touched if r in acc]
     outs = tuple(sds((4, 2 * T, W), dtype) for _, _, dtype, _ in jobs)
-    outs += (sds((8, W, W), F32),) * len(touched)
+    outs += (sds((4, W, W), F32),) * len(touched)
     args = tuple(queries) + tuple(job[0] for job in jobs)
     aliases = {len(args) + n: len(jobs) + touched.index(r) for n, r in enumerate(given)}
     args += tuple(acc[r] for r in given)
@@ -146,9 +171,14 @@
         ins = refs[: len(args) - len(after)]
         tiles_kernel(len(queries), static, touched, given, ins + refs[len(args) :])
 
-    flops = sum(10 * 960 * 1024 * len(sets) * W for sets, _ in static)
+    flops = sum(10 * 960 * 512 * len(sets) * W for sets, _ in static)
     out = call(kernel, name, outs, args, flops, aliases, spaces)
     return out[: len(jobs)], {**acc, **dict(zip(touched, out[len(jobs) :]))}
+
+
+def stack_kernel(a, b, out):
+    out[0:4] = a[...]
+    out[4:8] = b[...]
 
 
 def merge_kernel(own, b1, b2, b3, after, *outs):
@@ -159,8 +189,13 @@
         outs[r][...] = total.astype(outs[r].dtype)
 
 
-def halves_kernel(mine, got, out):
-    out[...] = (mine[...] + got[...]).astype(BF)
+def halves_kernel(near, far, got, out):
+    up = 1 - 2 * lax.axis_index("core")
+    here = 4 * lax.axis_index("zh") + lax.axis_index("zl") + 8
+    for n in range(8):
+        z = lax.rem(here + up * UP[n], 8)
+        mine = near[n] if n < 4 else far[n - 4]
+        out[2 * lax.rem(z, 4) + z // 4] = (mine + got[TWIN[n]]).astype(BF)
 
 
 def last_kernel(u, own, f1, f2, f3, gq, gk, gv):
@@ -180,6 +215,14 @@
     return lax.ppermute(x, "core", SWAP)
 
 
+def send_z(x, s):
+    index = lambda z, c: (z % 4) * 4 + c * 2 + z // 4
+    pairs = [
+        (index(z, c), index((z + (s if c == 0 else -s)) % 8, c)) for z in range(8) for c in range(2)
+    ]
+    return lax.ppermute(x, ("zl", "core", "zh"), pairs)
+
+
 def exchange_z(x):
     return lax.all_to_all(x, ("zl", "zh"), 0, 0, tiled=True)
 
@@ -198,7 +241,7 @@
     qp, kv = call(
         pack_kernel,
         "pack",
-        (sds((8, QP, W), BF), sds((2 * T, W), BF)),
+        (sds((QP, W), BF), sds((2 * T, W), BF)),
         (queries, out_grad, outputs, lse.reshape(1, W), keys, values),
         spaces=[ANY] * 6,
         scratch=(
@@ -210,33 +253,42 @@
         ),
         vmem=60,
     )
-    same = exchange_z(qp)
-    (kv0,) = call(
-        join_kernel,
-        "join",
-        (sds((4, 2 * T, W), BF),),
-        (kv, *(send_plane(kv, r, 0) for r in (1, 2, 3))),
-        flops=JOIN_COST,
-    )
-    kv1, kv3, kv2 = (send_plane(kv0, s, 1) for s in (1, 3, 2))
-    (same,) = call(after_kernel, "same", (sds((8, QP, W), BF),), (same, kv1, kv3), spaces=[VM, ANY, ANY])
-
-    qs = (same, swap_cores(same))
+    ks = [send_plane(kv, r, 0) for r in (1, 2, 3)]
+    (chip,) = call(pair_kernel, "chip", (sds((2, QP, W), BF),), (qp, swap_cores(qp)), CHIP_COST)
+    (kv0,) = call(join_kernel, "join", (sds((4, 2 * T, W), BF),), (kv, *ks), JOIN_COST)
+    kv1, kv3 = (send_plane(kv0, s, 1) for s in (1, 3))
+    q1, q2 = send_z(chip, 1), send_z(chip, 2)
+    (q2_own,) = call(first_kernel, "first", (sds((1, QP, W), BF),), (q2,), FIRST_COST)
+    q3, q4 = send_z(q2, 1), send_z(q2_own, 2)
+    (mine,) = call(
+        gather_kernel,
+        "gather",
+        (sds((7, QP, W), BF),),
+        (q1, q2, q3, q4, kv1, kv3),
+        spaces=[VM] * 4 + [ANY] * 2,
+    )
+    (kv0_late,) = call(
+        after_kernel, "late", (sds((4, 2 * T, W), BF),), (kv0, mine), spaces=[VM, ANY]
+    )
+    kv2 = send_plane(kv0_late, 2, 1)
+
+    qs = (chip, mine, swap_cores(mine))
     (part1, part3), acc = tiles(
-        "tiles13a", qs[:1], ((kv1, (0,), F32, None), (kv3, (0,), F32, None)), {}
+        "tiles13a", qs[:2], ((kv1, (0, 2), F32, None), (kv3, (0, 2), F32, None)), {}
     )
     (out1, out3, part0), acc = tiles(
         "tiles130",
         qs,
-        ((kv1, (1,), BF, part1), (kv3, (1,), BF, part3), (kv0, (1,), F32, None)),
+        ((kv1, (1, 3), BF, part1), (kv3, (1, 3), BF, part3), (kv0, (2, 3), F32, None)),
         acc,
     )
     back1, back3 = send_plane(out1, -1, 1), send_plane(out3, -3, 1)
-    (out2,), acc = tiles("tiles2", qs, ((kv2, (0, 1), BF, None),), acc)
-    rs, back2 = swap_cores(acc[1]), send_plane(out2, -2, 1)
-    (out0,), acc = tiles("tiles0", qs, ((kv0, (0,), F32, part0),), acc, (back1, back3))
-
-    (halves,) = call(halves_kernel, "halves", (sds((8, W, W), BF),), (acc[0], rs))
+    (out2,), acc = tiles("tiles2", qs, ((kv2, (0, 1, 2, 3), BF, None),), acc)
+    (others,) = call(stack_kernel, "others", (sds((8, W, W), F32),), (acc[2], acc[3]))
+    rs, back2 = swap_cores(others), send_plane(out2, -2, 1)
+    (out0,), acc = tiles("tiles0", qs, ((kv0, (0, 1), F32, part0),), acc, (back1, back3))
+
+    (halves,) = call(halves_kernel, "halves", (sds((8, W, W), BF),), (acc[0], acc[1], rs))
     u = exchange_z(halves)
     part0, *parts = call(
         merge_kernel,

time: 77.7 us -> 75.2 us (0.968)
  waiting for transfers between devices: 20.3 us -> 12.1 us
  starting transfers between devices: 32.4 us -> 37.7 us
  local copies, waits for them, and re-layouts: 0.01 us -> 0.89 us
    ppermute x0 -> x4, starting transfers between devices: none -> 11.1 us  [send_z(): return lax.ppermute(x, ('zl', 'core', 'zh'), pairs)]
    ppermute x12, waiting for transfers between devices: 15.5 us -> 9.23 us  [send_plane(): return lax.ppermute(x, ('y', 'core', 'x'), pairs)]
    all_to_all x2 -> x1, waiting for transfers between devices: 4.77 us -> 0.01 us  [exchange_z(): return lax.all_to_all(x, ('zl', 'zh'), 0, 0, tiled=True)]
    all_to_all x2 -> x1, starting transfers between devices: 12.8 us -> 8.41 us  [exchange_z(): return lax.all_to_all(x, ('zl', 'zh'), 0, 0, tiled=True)]
    ppermute x0 -> x4, waiting for transfers between devices: none -> 2.84 us  [send_z(): return lax.ppermute(x, ('zl', 'core', 'zh'), pairs)]
    ppermute x12, starting transfers between devices: 19.2 us -> 17.9 us  [send_plane(): return lax.ppermute(x, ('y', 'core', 'x'), pairs)]
    unnamed x2 -> x4, local copies, waits for them, and re-layouts: 0.01 us -> 0.89 us
    pallas_call x10 -> x14, Pallas kernels: 24 us -> 23.4 us  [call(): pl.pallas_call(kernel, name=name, out_shape=outs, in_specs=spaces or [VM]...]
  transfers between devices with their start and end apart: 16 -> 20, of which waited for: 7 -> 7; matrix products, arithmetic and copies ran while one was open for 0% -> 0% of each run, Pallas kernels for 28% -> 28%
where the time goes in v3:
time: 75.2 us; the launch traced here: 74.9 us
  starting transfers between devices  37.7 us (50%)
  Pallas kernels  23.4 us (31%)
  waiting for transfers between devices  12.1 us (16%)
  local copies, waits for them, and re-layouts  0.89 us (1%)
  between operations  0.79 us (1%)
    pallas_call x14, Pallas kernels, call(): pl.pallas_call(kernel, name=name, out_shape=outs, in_specs=spaces or [VM]...  23.4 us
    ppermute x12, starting transfers between devices, send_plane(): return lax.ppermute(x, ('y', 'core', 'x'), pairs)  17.9 us
    ppermute x4, starting transfers between devices, send_z(): return lax.ppermute(x, ('zl', 'core', 'zh'), pairs)  11.1 us
    ppermute x12, waiting for transfers between devices, send_plane(): return lax.ppermute(x, ('y', 'core', 'x'), pairs)  9.23 us
    all_to_all x1, starting transfers between devices, exchange_z(): return lax.all_to_all(x, ('zl', 'zh'), 0, 0, tiled=True)  8.41 us
    ppermute x4, waiting for transfers between devices, send_z(): return lax.ppermute(x, ('zl', 'core', 'zh'), pairs)  2.84 us
  transfers between devices with their start and end apart: 20, of which 7 were waited for; matrix products, arithmetic and copies ran while one was open for 0% of the time, Pallas kernels for 28%

profile of v3, /device:TPU:32, one launch (start us, length us, event | category | flops | bytes accessed | tf_op | source)
XLA Modules:
  0.0 74.9 jit_solution(9729120109472605684)
XLA Ops:
  0.6 1.7 %pack.1 = (bf16[272,128]{1,0:T(8,128)(2,1)}, bf16[480,128]{1,0:T(8,128)(2,1)}) custom-call(bf16[128,128]{1,0:T(8,128)(2,1)} %q.1, bf16[128,128]{1,0:T(8,128)(2,1)} %g.1, bf16[128,128]{1,0:T(8,128)(2,1)} %o.1, f32[1,128]{1,0:T(1,128)} %bitcast.1, bf16[240,128]{1,0:T(8,128)(2,1)} %k.1, bf16[240,128]{1,0:T(8,128)(2,1)} %v.1), custom_call_target="tpu_custom_call" | custom-call | bytes 414208 | tf_op jit(solution)/shard_map/pack/pallas_call | solution.py:32
  2.3 0.1 collective-permute-start
  2.4 0.0 copy-start
  2.4 1.6 %collective-permute-start.5 = (bf16[480,128]{1,0:T(8,128)(2,1)}, bf16[480,128]{1,0:T(8,128)(2,1)S(1)}, u32[]{:S(2)}, u32[]{:S(2)}) collective-permute-start(bf16[480,128]{1,0:T(8,128)(2,1)} %get-tuple-element.28.k0), channel_id=1, source_target_pairs={{0,2},{2,4},{4,6},{6,0},{8,24},{10,26},{12,28},{14,30},{16,18},{18... | collective-permute-start | bytes 368648 | tf_op jit(solution)/shard_map/ppermute | solution.py:237
  4.0 2.7 %collective-permute-start.6 = (bf16[480,128]{1,0:T(8,128)(2,1)}, bf16[480,128]{1,0:T(8,128)(2,1)S(1)}, u32[]{:S(2)}, u32[]{:S(2)}) collective-permute-start(bf16[480,128]{1,0:T(8,128)(2,1)} %get-tuple-element.28.k0), channel_id=1, source_target_pairs={{0,4},{2,6},{4,0},{6,2},{8,40},{10,42},{12,44},{14,46},{16,20},{18... | collective-permute-start | bytes 368648 | tf_op jit(solution)/shard_map/ppermute | solution.py:237
  6.7 1.4 %collective-permute-start.7 = (bf16[480,128]{1,0:T(8,128)(2,1)}, bf16[480,128]{1,0:T(8,128)(2,1)S(1)}, u32[]{:S(2)}, u32[]{:S(2)}) collective-permute-start(bf16[480,128]{1,0:T(8,128)(2,1)} %get-tuple-element.28.k0), channel_id=1, source_target_pairs={{0,6},{2,0},{4,2},{6,4},{8,56},{10,58},{12,60},{14,62},{16,22},{18... | collective-permute-start | bytes 368648 | tf_op jit(solution)/shard_map/ppermute | solution.py:237
  8.1 0.0 collective-permute-done.q1
  8.1 0.9 %copy-done.1 = bf16[272,128]{1,0:T(8,128)(2,1)S(1)} copy-done((bf16[272,128]{1,0:T(8,128)(2,1)S(1)}, bf16[272,128]{1,0:T(8,128)(2,1)}, u32[]{:S(2)}) %copy-start.1) | copy-done | bytes 69656
  9.0 3.3 %collective-permute-start.2 = (bf16[2,272,128]{2,1,0:T(8,128)(2,1)S(1)}, bf16[2,272,128]{2,1,0:T(8,128)(2,1)S(1)}, u32[]{:S(2)}, u32[]{:S(2)}) collective-permute-start(bf16[2,272,128]{2,1,0:T(8,128)(2,1)S(1)} %chip.1.refs_0_), channel_id=1, source_target_pairs={{0,128},{8,137},{64,192},{72,201},{128,1},{136,8},{192,65},{200,72... | collective-permute-start | bytes 417800 | tf_op jit(solution)/shard_map/ppermute | solution.py:223
  12.4 3.1 %collective-permute-start.1 = (bf16[2,272,128]{2,1,0:T(8,128)(2,1)S(1)}, bf16[2,272,128]{2,1,0:T(8,128)(2,1)S(1)}, u32[]{:S(2)}, u32[]{:S(2)}) collective-permute-start(bf16[2,272,128]{2,1,0:T(8,128)(2,1)S(1)} %chip.1.refs_0_), channel_id=1, source_target_pairs={{0,64},{8,201},{64,128},{72,8},{128,192},{136,72},{192,1},{200,136... | collective-permute-start | bytes 417800 | tf_op jit(solution)/shard_map/ppermute | solution.py:223
  15.5 0.0 collective-permute-done.5.k1
  15.5 0.0 collective-permute-done.6.k2
  15.5 0.0 collective-permute-done.7.k3
  15.6 1.7 %collective-permute-start.8 = (bf16[4,480,128]{2,1,0:T(8,128)(2,1)S(1)}, bf16[4,480,128]{2,1,0:T(8,128)(2,1)S(1)}, u32[]{:S(2)}, u32[]{:S(2)}) collective-permute-start(bf16[4,480,128]{2,1,0:T(8,128)(2,1)S(1)} %join.1.x.refs_5_.refs_3_), channel_id=1, source_target_pairs={{0,16},{2,18},{4,20},{6,22},{8,10},{10,12},{12,14},{14,8},{16,32},... | collective-permute-start | bytes 1474568 | tf_op jit(solution)/shard_map/ppermute | solution.py:237
  17.2 1.7 %collective-permute-start.9 = (bf16[4,480,128]{2,1,0:T(8,128)(2,1)S(1)}, bf16[4,480,128]{2,1,0:T(8,128)(2,1)S(1)}, u32[]{:S(2)}, u32[]{:S(2)}) collective-permute-start(bf16[4,480,128]{2,1,0:T(8,128)(2,1)S(1)} %join.1.x.refs_5_.refs_3_), channel_id=1, source_target_pairs={{0,48},{2,50},{4,52},{6,54},{8,14},{10,8},{12,10},{14,12},{16,0},{... | collective-permute-start | bytes 1474568 | tf_op jit(solution)/shard_map/ppermute | solution.py:237
  18.9 0.1 collective-permute-done.2.q.q2
  19.0 0.9 %collective-permute-start.3 = (bf16[2,272,128]{2,1,0:T(8,128)(2,1)S(1)}, bf16[2,272,128]{2,1,0:T(8,128)(2,1)S(1)}, u32[]{:S(2)}, u32[]{:S(2)}) collective-permute-start(bf16[2,272,128]{2,1,0:T(8,128)(2,1)S(1)} %collective-permute-done.2.q.q2), channel_id=1, source_target_pairs={{0,64},{8,201},{64,128},{72,8},{128,192},{136,72},{192,1},{200,136... | collective-permute-start | bytes 417800 | tf_op jit(solution)/shard_map/ppermute | solution.py:223
  19.9 3.7 %collective-permute-start.4 = (bf16[1,272,128]{2,1,0:T(8,128)(2,1)S(1)}, bf16[1,272,128]{2,1,0:T(8,128)(2,1)S(1)}, u32[]{:S(2)}, u32[]{:S(2)}) collective-permute-start(bf16[1,272,128]{2,1,0:T(8,128)(2,1)S(1)} %first.1), channel_id=1, source_target_pairs={{0,128},{8,137},{64,192},{72,201},{128,1},{136,8},{192,65},{200,72... | collective-permute-start | bytes 208904 | tf_op jit(solution)/shard_map/ppermute | solution.py:223
  23.7 0.0 collective-permute-done.1.q1
  23.7 2.7 %collective-permute-done.4.q4 = bf16[1,272,128]{2,1,0:T(8,128)(2,1)S(1)} collective-permute-done((bf16[1,272,128]{2,1,0:T(8,128)(2,1)S(1)}, bf16[1,272,128]{2,1,0:T(8,128)(2,1)S(1)}, u32[]{:S(2)}, u32[]{:S(2)}) %collective-permute-start.4) | collective-permute-done | bytes 69664 | tf_op jit(solution)/shard_map/ppermute | solution.py:223
  26.3 0.0 collective-permute-done.3.q3
  26.4 0.0 collective-permute-done.8.kv1.refs_2_.refs_3_
  26.4 0.0 collective-permute-done.9.kv3.refs_3_.refs_4_
  26.4 0.1 collective-permute-start.10
  26.5 2.9 %collective-permute-start.11 = (bf16[4,480,128]{2,1,0:T(8,128)(2,1)S(1)}, bf16[4,480,128]{2,1,0:T(8,128)(2,1)S(1)}, u32[]{:S(2)}, u32[]{:S(2)}) collective-permute-start(bf16[4,480,128]{2,1,0:T(8,128)(2,1)S(1)} %late.1), channel_id=1, source_target_pairs={{0,32},{2,34},{4,36},{6,38},{8,12},{10,14},{12,8},{14,10},{16,48},... | collective-permute-start | bytes 1474568 | tf_op jit(solution)/shard_map/ppermute | solution.py:237
  29.4 4.9 %tiles13a.1 = (f32[4,480,128]{2,1,0:T(8,128)S(1)}, f32[4,480,128]{2,1,0:T(8,128)S(1)}, f32[4,128,128]{2,1,0:T(8,128)S(1)}, f32[4,128,128]{2,1,0:T(8,128)S(1)}) custom-call(bf16[2,272,128]{2,1,0:T(8,128)(2,1)S(1)} %chip.1.refs_0_, bf16[7,272,128]{2,1,0:T(8,128)(2,1)S(1)} %gather.1.after.refs_1_, ...), custom_call_target="tpu_custom_call" | custom-call | flops 2516582400 | bytes 4100096 | tf_op jit(solution)/shard_map/tiles13a/pallas_call | solution.py:32
  34.3 0.0 collective-permute-done.10.refs_2_
  34.3 7.4 %tiles130.1 = (bf16[4,480,128]{2,1,0:T(8,128)(2,1)S(1)}, bf16[4,480,128]{2,1,0:T(8,128)(2,1)S(1)}, f32[4,480,128]{2,1,0:T(8,128)S(1)}, f32[4,128,128]{2,1,0:T(8,...) custom-call(bf16[2,272,128]{2,1,0:T(8,128)(2,1)S(1)} %chip.1.refs_0_, ...), custom_call_target="tpu_custom_call", output_to_operand_aliasing={{4}: (6, {})} | custom-call | flops 3774873600 | bytes 7569408 | tf_op jit(solution)/shard_map/tiles130/pallas_call | solution.py:32
  41.7 1.4 %collective-permute-start.12 = (bf16[4,480,128]{2,1,0:T(8,128)(2,1)S(1)}, bf16[4,480,128]{2,1,0:T(8,128)(2,1)S(1)}, u32[]{:S(2)}, u32[]{:S(2)}) collective-permute-start(bf16[4,480,128]{2,1,0:T(8,128)(2,1)S(1)} %get-tuple-element.39), channel_id=1, source_target_pairs={{0,48},{2,50},{4,52},{6,54},{8,14},{10,8},{12,10},{14,12},{16,0},{... | collective-permute-start | bytes 1474568 | tf_op jit(solution)/shard_map/ppermute | solution.py:237
  43.1 0.7 collective-permute-start.13
  43.8 4.9 %tiles2.1 = (bf16[4,480,128]{2,1,0:T(8,128)(2,1)S(1)}, f32[4,128,128]{2,1,0:T(8,128)S(1)}, f32[4,128,128]{2,1,0:T(8,128)S(1)}, f32[4,128,128]{2,1,0:T(8,128)S(1)}, f32[4,128,128]{2,1,0:T(8,128)S(1)}) custom-call(bf16[2,272,128]{2,1,0:T(8,128)(2,1)S(1)} %chip.1.refs_0_, ...), custom_call_target="tpu_custom_call", output_to_operand_aliasing={{1}: (4, {}), {2}: (5, {}), {3}: (6, {}), {4}: (7, {})} | custom-call | flops 2516582400 | bytes 4194304 | tf_op jit(solution)/shard_map/tiles2/pallas_call | solution.py:32
  48.8 0.1 collective-permute-start.14
  48.9 1.2 %collective-permute-start.15 = (bf16[4,480,128]{2,1,0:T(8,128)(2,1)S(1)}, bf16[4,480,128]{2,1,0:T(8,128)(2,1)S(1)}, u32[]{:S(2)}, u32[]{:S(2)}) collective-permute-start(bf16[4,480,128]{2,1,0:T(8,128)(2,1)S(1)} %get-tuple-element.46), channel_id=1, source_target_pairs={{0,32},{2,34},{4,36},{6,38},{8,12},{10,14},{12,8},{14,10},{16,48},... | collective-permute-start | bytes 1474568 | tf_op jit(solution)/shard_map/ppermute | solution.py:237
  50.0 0.6 collective-permute-done.12.refs_7_.b1
  50.6 2.6 %collective-permute-done.13.refs_8_.b3 = bf16[4,480,128]{2,1,0:T(8,128)(2,1)S(1)} collective-permute-done((bf16[4,480,128]{2,1,0:T(8,128)(2,1)S(1)}, bf16[4,480,128]{2,1,0:T(8,128)(2,1)S(1)}, u32[]{:S(2)}, u32[]{:S(2)}) %collective-permute-start.13) | collective-permute-done | bytes 491552 | tf_op jit(solution)/shard_map/ppermute | solution.py:237
  53.2 2.7 %tiles0.1 = (f32[4,480,128]{2,1,0:T(8,128)S(1)}, f32[4,128,128]{2,1,0:T(8,128)S(1)}, f32[4,128,128]{2,1,0:T(8,128)S(1)}) custom-call(bf16[2,272,128]{2,1,0:T(8,128)(2,1)S(1)} %chip.1.refs_0_, bf16[7,272,128]{2,1,0:T(8,128)(2,1)S(1)} %gather.1.after.refs_1_, ...), custom_call_target="tpu_custom_call", output_to_operand_aliasing={{1}: (4, {}), {2}: (5, {}), {0}: (6, {})} | custom-call | flops 1258291200 | bytes 5603328 | tf_op jit(solution)/shard_map/tiles0/pallas_call | solution.py:32
  55.8 0.0 collective-permute-done.14.got
  55.8 0.8 %halves.1.after = bf16[8,128,128]{2,1,0:T(8,128)(2,1)} custom-call(f32[4,128,128]{2,1,0:T(8,128)S(1)} %get-tuple-element.41.near, f32[4,128,128]{2,1,0:T(8,128)S(1)} %get-tuple-element.42.far, f32[8,128,128]{2,1,0:T(8,128)S(1)} %collective-permute-done.14.got), custom_call_target="tpu_custom_call" | custom-call | bytes 1310720 | tf_op jit(solution)/shard_map/halves/pallas_call | solution.py:32
  56.6 8.4 %all-to-all-start = ((bf16[8,128,128]{2,1,0:T(8,128)(2,1)}), bf16[8,128,128]{2,1,0:T(8,128)(2,1)S(1)}, u32[]{:S(2)}, u32[]{:S(2)}) async-start(bf16[8,128,128]{2,1,0:T(8,128)(2,1)} %halves.1.after), calls=%async_computation | async-start | bytes 524288 | tf_op jit(solution)/shard_map/all_to_all | solution.py:227
  65.1 0.0 collective-permute-done.15.b2
  65.1 0.2 merge.1
  65.3 0.2 collective-permute-start.16
  65.5 2.5 %collective-permute-start.17 = (bf16[480,128]{1,0:T(8,128)(2,1)S(1)}, bf16[480,128]{1,0:T(8,128)(2,1)S(1)}, u32[]{:S(2)}, u32[]{:S(2)}) collective-permute-start(bf16[480,128]{1,0:T(8,128)(2,1)S(1)} %get-tuple-element.49), channel_id=1, source_target_pairs={{0,4},{2,6},{4,0},{6,2},{8,40},{10,42},{12,44},{14,46},{16,20},{18... | collective-permute-start | bytes 368648 | tf_op jit(solution)/shard_map/ppermute | solution.py:237
  68.0 0.0 collective-permute-start.18
  68.0 2.2 %collective-permute-done.16.f1 = bf16[480,128]{1,0:T(8,128)(2,1)S(1)} collective-permute-done((bf16[480,128]{1,0:T(8,128)(2,1)S(1)}, bf16[480,128]{1,0:T(8,128)(2,1)S(1)}, u32[]{:S(2)}, u32[]{:S(2)}) %collective-permute-start.16) | collective-permute-done | bytes 122912 | tf_op jit(solution)/shard_map/ppermute | solution.py:237
  70.2 1.6 %collective-permute-done.17.f2 = bf16[480,128]{1,0:T(8,128)(2,1)S(1)} collective-permute-done((bf16[480,128]{1,0:T(8,128)(2,1)S(1)}, bf16[480,128]{1,0:T(8,128)(2,1)S(1)}, u32[]{:S(2)}, u32[]{:S(2)}) %collective-permute-start.17) | collective-permute-done | bytes 122912 | tf_op jit(solution)/shard_map/ppermute | solution.py:237
  71.8 2.3 %collective-permute-done.18.f3 = bf16[480,128]{1,0:T(8,128)(2,1)S(1)} collective-permute-done((bf16[480,128]{1,0:T(8,128)(2,1)S(1)}, bf16[480,128]{1,0:T(8,128)(2,1)S(1)}, u32[]{:S(2)}, u32[]{:S(2)}) %collective-permute-start.18) | collective-permute-done | bytes 122912 | tf_op jit(solution)/shard_map/ppermute | solution.py:237
  74.1 0.8 %last.1 = (f32[128,128]{1,0:T(8,128)}, f32[240,128]{1,0:T(8,128)}, f32[240,128]{1,0:T(8,128)}) custom-call(bf16[8,128,128]{2,1,0:T(8,128)(2,1)S(1)} %all-to-all-done.u, f32[480,128]{1,0:T(8,128)S(1)} %get-tuple-element.47.own, bf16[480,128]{1,0:T(8,128)(2,1)S(1)} %collective-permute-done.16.f1, bf16[480,128]{1,0:T(8,128)(2,1)S(1)} %collective-permute-done.17.f2, ...), custom_call_target="tpu_custom_call" | custom-call | bytes 1187840 | tf_op jit(solution)/shard_map/last/pallas_call | solution.py:32
  (10 shorter events, 0.2 us)
Async XLA Ops:
  2.3 5.8 %collective-permute-start = (bf16[272,128]{1,0:T(8,128)(2,1)}, bf16[272,128]{1,0:T(8,128)(2,1)S(1)}, u32[]{:S(2)}, u32[]{:S(2)}) collective-permute-start(bf16[272,128]{1,0:T(8,128)(2,1)} %get-tuple-element.27.q0), channel_id=1, source_target_pairs={{0,8},{8,0},{1,9},{9,1},{2,10},{10,2},{3,11},{11,3},{4,12},{12,4},... | collective-permute-start | bytes 208904 | tf_op jit(solution)/shard_map/ppermute | solution.py:215
  2.4 13.1 %copy-start = (bf16[480,128]{1,0:T(8,128)(2,1)S(1)}, bf16[480,128]{1,0:T(8,128)(2,1)}, u32[]{:S(2)}) copy-start(bf16[480,128]{1,0:T(8,128)(2,1)} %get-tuple-element.28.k0) | copy-start | bytes 368644
  2.4 13.1 %collective-permute-start.5 = (bf16[480,128]{1,0:T(8,128)(2,1)}, bf16[480,128]{1,0:T(8,128)(2,1)S(1)}, u32[]{:S(2)}, u32[]{:S(2)}) collective-permute-start(bf16[480,128]{1,0:T(8,128)(2,1)} %get-tuple-element.28.k0), channel_id=1, source_target_pairs={{0,2},{2,4},{4,6},{6,0},{8,24},{10,26},{12,28},{14,30},{16,18},{18... | collective-permute-start | bytes 368648 | tf_op jit(solution)/shard_map/ppermute | solution.py:237
  4.0 11.6 %collective-permute-start.6 = (bf16[480,128]{1,0:T(8,128)(2,1)}, bf16[480,128]{1,0:T(8,128)(2,1)S(1)}, u32[]{:S(2)}, u32[]{:S(2)}) collective-permute-start(bf16[480,128]{1,0:T(8,128)(2,1)} %get-tuple-element.28.k0), channel_id=1, source_target_pairs={{0,4},{2,6},{4,0},{6,2},{8,40},{10,42},{12,44},{14,46},{16,20},{18... | collective-permute-start | bytes 368648 | tf_op jit(solution)/shard_map/ppermute | solution.py:237
  6.7 8.8 %collective-permute-start.7 = (bf16[480,128]{1,0:T(8,128)(2,1)}, bf16[480,128]{1,0:T(8,128)(2,1)S(1)}, u32[]{:S(2)}, u32[]{:S(2)}) collective-permute-start(bf16[480,128]{1,0:T(8,128)(2,1)} %get-tuple-element.28.k0), channel_id=1, source_target_pairs={{0,6},{2,0},{4,2},{6,4},{8,56},{10,58},{12,60},{14,62},{16,22},{18... | collective-permute-start | bytes 368648 | tf_op jit(solution)/shard_map/ppermute | solution.py:237
  8.1 0.9 %copy-start.1 = (bf16[272,128]{1,0:T(8,128)(2,1)S(1)}, bf16[272,128]{1,0:T(8,128)(2,1)}, u32[]{:S(2)}) copy-start(bf16[272,128]{1,0:T(8,128)(2,1)} %get-tuple-element.27.q0) | copy-start | bytes 208900
  9.0 10.0 %collective-permute-start.2 = (bf16[2,272,128]{2,1,0:T(8,128)(2,1)S(1)}, bf16[2,272,128]{2,1,0:T(8,128)(2,1)S(1)}, u32[]{:S(2)}, u32[]{:S(2)}) collective-permute-start(bf16[2,272,128]{2,1,0:T(8,128)(2,1)S(1)} %chip.1.refs_0_), channel_id=1, source_target_pairs={{0,128},{8,137},{64,192},{72,201},{128,1},{136,8},{192,65},{200,72... | collective-permute-start | bytes 417800 | tf_op jit(solution)/shard_map/ppermute | solution.py:223
  12.4 11.3 %collective-permute-start.1 = (bf16[2,272,128]{2,1,0:T(8,128)(2,1)S(1)}, bf16[2,272,128]{2,1,0:T(8,128)(2,1)S(1)}, u32[]{:S(2)}, u32[]{:S(2)}) collective-permute-start(bf16[2,272,128]{2,1,0:T(8,128)(2,1)S(1)} %chip.1.refs_0_), channel_id=1, source_target_pairs={{0,64},{8,201},{64,128},{72,8},{128,192},{136,72},{192,1},{200,136... | collective-permute-start | bytes 417800 | tf_op jit(solution)/shard_map/ppermute | solution.py:223
  15.6 10.8 %collective-permute-start.8 = (bf16[4,480,128]{2,1,0:T(8,128)(2,1)S(1)}, bf16[4,480,128]{2,1,0:T(8,128)(2,1)S(1)}, u32[]{:S(2)}, u32[]{:S(2)}) collective-permute-start(bf16[4,480,128]{2,1,0:T(8,128)(2,1)S(1)} %join.1.x.refs_5_.refs_3_), channel_id=1, source_target_pairs={{0,16},{2,18},{4,20},{6,22},{8,10},{10,12},{12,14},{14,8},{16,32},... | collective-permute-start | bytes 1474568 | tf_op jit(solution)/shard_map/ppermute | solution.py:237
  17.2 9.1 %collective-permute-start.9 = (bf16[4,480,128]{2,1,0:T(8,128)(2,1)S(1)}, bf16[4,480,128]{2,1,0:T(8,128)(2,1)S(1)}, u32[]{:S(2)}, u32[]{:S(2)}) collective-permute-start(bf16[4,480,128]{2,1,0:T(8,128)(2,1)S(1)} %join.1.x.refs_5_.refs_3_), channel_id=1, source_target_pairs={{0,48},{2,50},{4,52},{6,54},{8,14},{10,8},{12,10},{14,12},{16,0},{... | collective-permute-start | bytes 1474568 | tf_op jit(solution)/shard_map/ppermute | solution.py:237
  19.0 7.3 %collective-permute-start.3 = (bf16[2,272,128]{2,1,0:T(8,128)(2,1)S(1)}, bf16[2,272,128]{2,1,0:T(8,128)(2,1)S(1)}, u32[]{:S(2)}, u32[]{:S(2)}) collective-permute-start(bf16[2,272,128]{2,1,0:T(8,128)(2,1)S(1)} %collective-permute-done.2.q.q2), channel_id=1, source_target_pairs={{0,64},{8,201},{64,128},{72,8},{128,192},{136,72},{192,1},{200,136... | collective-permute-start | bytes 417800 | tf_op jit(solution)/shard_map/ppermute | solution.py:223
  19.9 6.4 %collective-permute-start.4 = (bf16[1,272,128]{2,1,0:T(8,128)(2,1)S(1)}, bf16[1,272,128]{2,1,0:T(8,128)(2,1)S(1)}, u32[]{:S(2)}, u32[]{:S(2)}) collective-permute-start(bf16[1,272,128]{2,1,0:T(8,128)(2,1)S(1)} %first.1), channel_id=1, source_target_pairs={{0,128},{8,137},{64,192},{72,201},{128,1},{136,8},{192,65},{200,72... | collective-permute-start | bytes 208904 | tf_op jit(solution)/shard_map/ppermute | solution.py:223
  26.4 7.9 %collective-permute-start.10 = (bf16[7,272,128]{2,1,0:T(8,128)(2,1)S(1)}, bf16[7,272,128]{2,1,0:T(8,128)(2,1)S(1)}, u32[]{:S(2)}, u32[]{:S(2)}) collective-permute-start(bf16[7,272,128]{2,1,0:T(8,128)(2,1)S(1)} %gather.1.after.refs_1_), channel_id=1, source_target_pairs={{0,8},{8,0},{1,9},{9,1},{2,10},{10,2},{3,11},{11,3},{4,12},{12,4},... | collective-permute-start | bytes 1462280 | tf_op jit(solution)/shard_map/ppermute | solution.py:215
  26.5 17.3 %collective-permute-start.11 = (bf16[4,480,128]{2,1,0:T(8,128)(2,1)S(1)}, bf16[4,480,128]{2,1,0:T(8,128)(2,1)S(1)}, u32[]{:S(2)}, u32[]{:S(2)}) collective-permute-start(bf16[4,480,128]{2,1,0:T(8,128)(2,1)S(1)} %late.1), channel_id=1, source_target_pairs={{0,32},{2,34},{4,36},{6,38},{8,12},{10,14},{12,8},{14,10},{16,48},... | collective-permute-start | bytes 1474568 | tf_op jit(solution)/shard_map/ppermute | solution.py:237
  41.7 8.9 %collective-permute-start.12 = (bf16[4,480,128]{2,1,0:T(8,128)(2,1)S(1)}, bf16[4,480,128]{2,1,0:T(8,128)(2,1)S(1)}, u32[]{:S(2)}, u32[]{:S(2)}) collective-permute-start(bf16[4,480,128]{2,1,0:T(8,128)(2,1)S(1)} %get-tuple-element.39), channel_id=1, source_target_pairs={{0,48},{2,50},{4,52},{6,54},{8,14},{10,8},{12,10},{14,12},{16,0},{... | collective-permute-start | bytes 1474568 | tf_op jit(solution)/shard_map/ppermute | solution.py:237
  43.1 10.0 %collective-permute-start.13 = (bf16[4,480,128]{2,1,0:T(8,128)(2,1)S(1)}, bf16[4,480,128]{2,1,0:T(8,128)(2,1)S(1)}, u32[]{:S(2)}, u32[]{:S(2)}) collective-permute-start(bf16[4,480,128]{2,1,0:T(8,128)(2,1)S(1)} %get-tuple-element.40), channel_id=1, source_target_pairs={{0,16},{2,18},{4,20},{6,22},{8,10},{10,12},{12,14},{14,8},{16,32},... | collective-permute-start | bytes 1474568 | tf_op jit(solution)/shard_map/ppermute | solution.py:237
  48.8 7.1 %collective-permute-start.14 = (f32[8,128,128]{2,1,0:T(8,128)S(1)}, f32[8,128,128]{2,1,0:T(8,128)S(1)}, u32[]{:S(2)}, u32[]{:S(2)}) collective-permute-start(f32[8,128,128]{2,1,0:T(8,128)S(1)} %others.1), channel_id=1, source_target_pairs={{0,8},{8,0},{1,9},{9,1},{2,10},{10,2},{3,11},{11,3},{4,12},{12,4},... | collective-permute-start | bytes 1572872 | tf_op jit(solution)/shard_map/ppermute | solution.py:215
  48.9 16.2 %collective-permute-start.15 = (bf16[4,480,128]{2,1,0:T(8,128)(2,1)S(1)}, bf16[4,480,128]{2,1,0:T(8,128)(2,1)S(1)}, u32[]{:S(2)}, u32[]{:S(2)}) collective-permute-start(bf16[4,480,128]{2,1,0:T(8,128)(2,1)S(1)} %get-tuple-element.46), channel_id=1, source_target_pairs={{0,32},{2,34},{4,36},{6,38},{8,12},{10,14},{12,8},{14,10},{16,48},... | collective-permute-start | bytes 1474568 | tf_op jit(solution)/shard_map/ppermute | solution.py:237
  56.6 17.5 %all-to-all-start = ((bf16[8,128,128]{2,1,0:T(8,128)(2,1)}), bf16[8,128,128]{2,1,0:T(8,128)(2,1)S(1)}, u32[]{:S(2)}, u32[]{:S(2)}) async-start(bf16[8,128,128]{2,1,0:T(8,128)(2,1)} %halves.1.after), calls=%async_computation | async-start | bytes 524288 | tf_op jit(solution)/shard_map/all_to_all | solution.py:227
  65.3 5.0 %collective-permute-start.16 = (bf16[480,128]{1,0:T(8,128)(2,1)S(1)}, bf16[480,128]{1,0:T(8,128)(2,1)S(1)}, u32[]{:S(2)}, u32[]{:S(2)}) collective-permute-start(bf16[480,128]{1,0:T(8,128)(2,1)S(1)} %get-tuple-element.48), channel_id=1, source_target_pairs={{0,6},{2,0},{4,2},{6,4},{8,56},{10,58},{12,60},{14,62},{16,22},{18... | collective-permute-start | bytes 368648 | tf_op jit(solution)/shard_map/ppermute | solution.py:237
  65.5 6.4 %collective-permute-start.17 = (bf16[480,128]{1,0:T(8,128)(2,1)S(1)}, bf16[480,128]{1,0:T(8,128)(2,1)S(1)}, u32[]{:S(2)}, u32[]{:S(2)}) collective-permute-start(bf16[480,128]{1,0:T(8,128)(2,1)S(1)} %get-tuple-element.49), channel_id=1, source_target_pairs={{0,4},{2,6},{4,0},{6,2},{8,40},{10,42},{12,44},{14,46},{16,20},{18... | collective-permute-start | bytes 368648 | tf_op jit(solution)/shard_map/ppermute | solution.py:237
  68.0 6.1 %collective-permute-start.18 = (bf16[480,128]{1,0:T(8,128)(2,1)S(1)}, bf16[480,128]{1,0:T(8,128)(2,1)S(1)}, u32[]{:S(2)}, u32[]{:S(2)}) collective-permute-start(bf16[480,128]{1,0:T(8,128)(2,1)S(1)} %get-tuple-element.50), channel_id=1, source_target_pairs={{0,2},{2,4},{4,6},{6,0},{8,24},{10,26},{12,28},{14,30},{16,18},{18... | collective-permute-start | bytes 368648 | tf_op jit(solution)/shard_map/ppermute | solution.py:237

commit v4 on v3

--- a/solution.py
+++ b/solution.py
@@ -95,24 +95,26 @@
     out[...] = q[0:1]
 
 
-def gather_kernel(q1, q2, q3, q4, kv1, kv3, out):
+def gather_kernel(q1, q2, q3, q4, kv1, kv3, part, out):
     for n, q in enumerate((q1, q2, q3)):
         out[2 * n : 2 * n + 2] = q[...]
     out[6:7] = q4[...]
 
 
 GROUPS = (
-    ((0, 0), (1, 0), (1, 2), (1, 4)),
+    ((0, 1), (1, 1), (1, 3), (0, 0)),
+    ((1, 0), (1, 2), (1, 4), (1, 5)),
     ((1, 6), (2, 1), (2, 3), (2, 5)),
-    ((0, 1), (1, 1), (1, 3), (1, 5)),
     ((2, 0), (2, 2), (2, 4), (2, 6)),
+    ((0, 1), (3, 1), (4, 1), (0, 0)),
 )
+SAME = ((0, 3), (1, 0), (1, 1), (1, 2), (2, 0), (2, 1), (2, 2), (2, 3))
 UP = (0, -1, -2, -3, -4, 1, 2, 3)
 TWIN = (0, 4, 5, 6, 7, 1, 2, 3)
 
 
-def tiles_kernel(nq, jobs, touched, given, refs):
-    qrefs, refs = refs[:nq], refs[nq:]
+def tiles_kernel(ops, jobs, touched, given, refs):
+    qrefs, refs = dict(zip(ops, refs)), refs[len(ops) :]
     kvs, refs = refs[: len(jobs)], refs[len(jobs) :]
     accs = dict(zip(given, refs))
     parts = list(refs[len(given) :])
@@ -137,6 +139,7 @@
             gv = dv if gv is None else gv + dv
             gk = dk if gk is None else gk + dk
             u = dot(ks, ds, TN)
+            c = c % 4
             for n in range(4):
                 block = u[:, n * W : (n + 1) * W]
                 sums[c][n] = accs[c][n] + block if c in accs else block
@@ -151,11 +154,11 @@
 
 
 def tiles(name, queries, jobs, acc, after=()):
-    touched = sorted({c for _, sets, _, _ in jobs for c in sets})
+    touched = sorted({c % 4 for _, sets, _, _ in jobs for c in sets})
     given = [r for r in touched if r in acc]
     outs = tuple(sds((4, 2 * T, W), dtype) for _, _, dtype, _ in jobs)
     outs += (sds((4, W, W), F32),) * len(touched)
-    args = tuple(queries) + tuple(job[0] for job in jobs)
+    args = tuple(queries.values()) + tuple(job[0] for job in jobs)
     aliases = {len(args) + n: len(jobs) + touched.index(r) for n, r in enumerate(given)}
     args += tuple(acc[r] for r in given)
     for n, job in enumerate(jobs):
@@ -169,16 +172,17 @@
 
     def kernel(*refs):
         ins = refs[: len(args) - len(after)]
-        tiles_kernel(len(queries), static, touched, given, ins + refs[len(args) :])
+        tiles_kernel(tuple(queries), static, touched, given, ins + refs[len(args) :])
 
     flops = sum(10 * 960 * 512 * len(sets) * W for sets, _ in static)
     out = call(kernel, name, outs, args, flops, aliases, spaces)
     return out[: len(jobs)], {**acc, **dict(zip(touched, out[len(jobs) :]))}
 
 
-def stack_kernel(a, b, out):
-    out[0:4] = a[...]
-    out[4:8] = b[...]
+def stack_kernel(g0, g1, g3, out):
+    out[0:3] = g0[0:3]
+    out[3] = g1[3]
+    out[4:8] = g3[...]
 
 
 def merge_kernel(own, b1, b2, b3, after, *outs):
@@ -189,13 +193,13 @@
         outs[r][...] = total.astype(outs[r].dtype)
 
 
-def halves_kernel(near, far, got, out):
+def halves_kernel(g0, g1, g2, got, out):
+    groups = (g0, g1, g2)
     up = 1 - 2 * lax.axis_index("core")
     here = 4 * lax.axis_index("zh") + lax.axis_index("zl") + 8
-    for n in range(8):
+    for n, (group, place) in enumerate(SAME):
         z = lax.rem(here + up * UP[n], 8)
-        mine = near[n] if n < 4 else far[n - 4]
-        out[2 * lax.rem(z, 4) + z // 4] = (mine + got[TWIN[n]]).astype(BF)
+        out[2 * lax.rem(z, 4) + z // 4] = (groups[group][place] + got[TWIN[n]]).astype(BF)
 
 
 def last_kernel(u, own, f1, f2, f3, gq, gk, gv):
@@ -260,35 +264,40 @@
     q1, q2 = send_z(chip, 1), send_z(chip, 2)
     (q2_own,) = call(first_kernel, "first", (sds((1, QP, W), BF),), (q2,), FIRST_COST)
     q3, q4 = send_z(q2, 1), send_z(q2_own, 2)
+    (part0,), acc = tiles("tiles0e", {0: chip, 3: q1, 4: q2}, ((kv0, (4,), F32, None),), {})
     (mine,) = call(
         gather_kernel,
         "gather",
         (sds((7, QP, W), BF),),
-        (q1, q2, q3, q4, kv1, kv3),
-        spaces=[VM] * 4 + [ANY] * 2,
+        (q1, q2, q3, q4, kv1, kv3, part0),
+        spaces=[VM] * 4 + [ANY] * 3,
     )
     (kv0_late,) = call(
         after_kernel, "late", (sds((4, 2 * T, W), BF),), (kv0, mine), spaces=[VM, ANY]
     )
     kv2 = send_plane(kv0_late, 2, 1)
 
-    qs = (chip, mine, swap_cores(mine))
+    sib = swap_cores(mine)
     (part1, part3), acc = tiles(
-        "tiles13a", qs[:2], ((kv1, (0, 2), F32, None), (kv3, (0, 2), F32, None)), {}
-    )
+        "tiles13a",
+        {0: chip, 1: mine},
+        ((kv1, (0, 1), F32, None), (kv3, (0, 1), F32, None)),
+        acc,
+    )
+    qs = {0: chip, 1: mine, 2: sib}
     (out1, out3, part0), acc = tiles(
         "tiles130",
         qs,
-        ((kv1, (1, 3), BF, part1), (kv3, (1, 3), BF, part3), (kv0, (2, 3), F32, None)),
+        ((kv1, (2, 3), BF, part1), (kv3, (2, 3), BF, part3), (kv0, (1, 3), F32, part0)),
         acc,
     )
     back1, back3 = send_plane(out1, -1, 1), send_plane(out3, -3, 1)
     (out2,), acc = tiles("tiles2", qs, ((kv2, (0, 1, 2, 3), BF, None),), acc)
-    (others,) = call(stack_kernel, "others", (sds((8, W, W), F32),), (acc[2], acc[3]))
+    (others,) = call(stack_kernel, "others", (sds((8, W, W), F32),), (acc[0], acc[1], acc[3]))
     rs, back2 = swap_cores(others), send_plane(out2, -2, 1)
-    (out0,), acc = tiles("tiles0", qs, ((kv0, (0, 1), F32, part0),), acc, (back1, back3))
-
-    (halves,) = call(halves_kernel, "halves", (sds((8, W, W), BF),), (acc[0], acc[1], rs))
+    (out0,), acc = tiles("tiles0", qs, ((kv0, (2,), F32, part0),), acc, (back1, back3))
+
+    (halves,) = call(halves_kernel, "halves", (sds((8, W, W), BF),), (acc[0], acc[1], acc[2], rs))
     u = exchange_z(halves)
     part0, *parts = call(
         merge_kernel,

time: 75.2 us -> 74.1 us (0.985)
  waiting for transfers between devices: 12.1 us -> 10.8 us
    ppermute x4, waiting for transfers between devices: 2.84 us -> 1.51 us  [send_z(): return lax.ppermute(x, ('zl', 'core', 'zh'), pairs)]
    pallas_call x14 -> x15, Pallas kernels: 23.4 us -> 23.7 us  [call(): pl.pallas_call(kernel, name=name, out_shape=outs, in_specs=spaces or [VM]...]
  transfers between devices with their start and end apart: 20 -> 20, of which waited for: 7 -> 7; matrix products, arithmetic and copies ran while one was open for 0% -> 0% of each run, Pallas kernels for 28% -> 29%
where the time goes in v4:
time: 74.1 us; the launch traced here: 73.8 us
  starting transfers between devices  37.7 us (51%)
  Pallas kernels  23.7 us (32%)
  waiting for transfers between devices  10.8 us (15%)
  local copies, waits for them, and re-layouts  0.89 us (1%)
  between operations  0.8 us (1%)
    pallas_call x15, Pallas kernels, call(): pl.pallas_call(kernel, name=name, out_shape=outs, in_specs=spaces or [VM]...  23.7 us
    ppermute x12, starting transfers between devices, send_plane(): return lax.ppermute(x, ('y', 'core', 'x'), pairs)  17.9 us
    ppermute x4, starting transfers between devices, send_z(): return lax.ppermute(x, ('zl', 'core', 'zh'), pairs)  11.1 us
    ppermute x12, waiting for transfers between devices, send_plane(): return lax.ppermute(x, ('y', 'core', 'x'), pairs)  9.24 us
    all_to_all x1, starting transfers between devices, exchange_z(): return lax.all_to_all(x, ('zl', 'zh'), 0, 0, tiled=True)  8.41 us
    ppermute x4, waiting for transfers between devices, send_z(): return lax.ppermute(x, ('zl', 'core', 'zh'), pairs)  1.51 us
  transfers between devices with their start and end apart: 20, of which 7 were waited for; matrix products, arithmetic and copies ran while one was open for 0% of the time, Pallas kernels for 29%

profile of v4, /device:TPU:32, one launch (start us, length us, event | category | flops | bytes accessed | tf_op | source)
XLA Modules:
  0.0 73.8 jit_solution(13286758180916900450)
XLA Ops:
  0.6 1.7 %pack.1 = (bf16[272,128]{1,0:T(8,128)(2,1)}, bf16[480,128]{1,0:T(8,128)(2,1)}) custom-call(bf16[128,128]{1,0:T(8,128)(2,1)} %q.1, bf16[128,128]{1,0:T(8,128)(2,1)} %g.1, bf16[128,128]{1,0:T(8,128)(2,1)} %o.1, f32[1,128]{1,0:T(1,128)} %bitcast.1, bf16[240,128]{1,0:T(8,128)(2,1)} %k.1, bf16[240,128]{1,0:T(8,128)(2,1)} %v.1), custom_call_target="tpu_custom_call" | custom-call | bytes 414208 | tf_op jit(solution)/shard_map/pack/pallas_call | solution.py:32
  2.3 0.1 collective-permute-start
  2.4 0.0 copy-start
  2.4 1.6 %collective-permute-start.5 = (bf16[480,128]{1,0:T(8,128)(2,1)}, bf16[480,128]{1,0:T(8,128)(2,1)S(1)}, u32[]{:S(2)}, u32[]{:S(2)}) collective-permute-start(bf16[480,128]{1,0:T(8,128)(2,1)} %get-tuple-element.29.k0), channel_id=1, source_target_pairs={{0,2},{2,4},{4,6},{6,0},{8,24},{10,26},{12,28},{14,30},{16,18},{18... | collective-permute-start | bytes 368648 | tf_op jit(solution)/shard_map/ppermute | solution.py:241
  4.0 2.7 %collective-permute-start.6 = (bf16[480,128]{1,0:T(8,128)(2,1)}, bf16[480,128]{1,0:T(8,128)(2,1)S(1)}, u32[]{:S(2)}, u32[]{:S(2)}) collective-permute-start(bf16[480,128]{1,0:T(8,128)(2,1)} %get-tuple-element.29.k0), channel_id=1, source_target_pairs={{0,4},{2,6},{4,0},{6,2},{8,40},{10,42},{12,44},{14,46},{16,20},{18... | collective-permute-start | bytes 368648 | tf_op jit(solution)/shard_map/ppermute | solution.py:241
  6.7 1.4 %collective-permute-start.7 = (bf16[480,128]{1,0:T(8,128)(2,1)}, bf16[480,128]{1,0:T(8,128)(2,1)S(1)}, u32[]{:S(2)}, u32[]{:S(2)}) collective-permute-start(bf16[480,128]{1,0:T(8,128)(2,1)} %get-tuple-element.29.k0), channel_id=1, source_target_pairs={{0,6},{2,0},{4,2},{6,4},{8,56},{10,58},{12,60},{14,62},{16,22},{18... | collective-permute-start | bytes 368648 | tf_op jit(solution)/shard_map/ppermute | solution.py:241
  8.1 0.0 collective-permute-done.q1
  8.1 0.9 %copy-done.1 = bf16[272,128]{1,0:T(8,128)(2,1)S(1)} copy-done((bf16[272,128]{1,0:T(8,128)(2,1)S(1)}, bf16[272,128]{1,0:T(8,128)(2,1)}, u32[]{:S(2)}) %copy-start.1) | copy-done | bytes 69656
  9.0 3.3 %collective-permute-start.2 = (bf16[2,272,128]{2,1,0:T(8,128)(2,1)S(1)}, bf16[2,272,128]{2,1,0:T(8,128)(2,1)S(1)}, u32[]{:S(2)}, u32[]{:S(2)}) collective-permute-start(bf16[2,272,128]{2,1,0:T(8,128)(2,1)S(1)} %chip.1.refs_0_), channel_id=1, source_target_pairs={{0,128},{8,137},{64,192},{72,201},{128,1},{136,8},{192,65},{200,72... | collective-permute-start | bytes 417800 | tf_op jit(solution)/shard_map/ppermute | solution.py:227
  12.4 3.1 %collective-permute-start.1 = (bf16[2,272,128]{2,1,0:T(8,128)(2,1)S(1)}, bf16[2,272,128]{2,1,0:T(8,128)(2,1)S(1)}, u32[]{:S(2)}, u32[]{:S(2)}) collective-permute-start(bf16[2,272,128]{2,1,0:T(8,128)(2,1)S(1)} %chip.1.refs_0_), channel_id=1, source_target_pairs={{0,64},{8,201},{64,128},{72,8},{128,192},{136,72},{192,1},{200,136... | collective-permute-start | bytes 417800 | tf_op jit(solution)/shard_map/ppermute | solution.py:227
  15.5 0.0 collective-permute-done.5.k1
  15.5 0.0 collective-permute-done.6.k2
  15.5 0.0 collective-permute-done.7.k3
  15.6 1.7 %collective-permute-start.8 = (bf16[4,480,128]{2,1,0:T(8,128)(2,1)S(1)}, bf16[4,480,128]{2,1,0:T(8,128)(2,1)S(1)}, u32[]{:S(2)}, u32[]{:S(2)}) collective-permute-start(bf16[4,480,128]{2,1,0:T(8,128)(2,1)S(1)} %join.1.refs_3_.x.refs_5_), channel_id=1, source_target_pairs={{0,16},{2,18},{4,20},{6,22},{8,10},{10,12},{12,14},{14,8},{16,32},... | collective-permute-start | bytes 1474568 | tf_op jit(solution)/shard_map/ppermute | solution.py:241
  17.2 1.7 %collective-permute-start.9 = (bf16[4,480,128]{2,1,0:T(8,128)(2,1)S(1)}, bf16[4,480,128]{2,1,0:T(8,128)(2,1)S(1)}, u32[]{:S(2)}, u32[]{:S(2)}) collective-permute-start(bf16[4,480,128]{2,1,0:T(8,128)(2,1)S(1)} %join.1.refs_3_.x.refs_5_), channel_id=1, source_target_pairs={{0,48},{2,50},{4,52},{6,54},{8,14},{10,8},{12,10},{14,12},{16,0},{... | collective-permute-start | bytes 1474568 | tf_op jit(solution)/shard_map/ppermute | solution.py:241
  18.9 0.1 collective-permute-done.2.q.refs_2_.q2
  19.0 0.9 %collective-permute-start.3 = (bf16[2,272,128]{2,1,0:T(8,128)(2,1)S(1)}, bf16[2,272,128]{2,1,0:T(8,128)(2,1)S(1)}, u32[]{:S(2)}, u32[]{:S(2)}) collective-permute-start(bf16[2,272,128]{2,1,0:T(8,128)(2,1)S(1)} %collective-permute-done.2.q.refs_2_.q2), channel_id=1, source_target_pairs={{0,64},{8,201},{64,128},{72,8},{128,192},{136,72},{192,1},{200,136... | collective-permute-start | bytes 417800 | tf_op jit(solution)/shard_map/ppermute | solution.py:227
  19.9 3.7 %collective-permute-start.4 = (bf16[1,272,128]{2,1,0:T(8,128)(2,1)S(1)}, bf16[1,272,128]{2,1,0:T(8,128)(2,1)S(1)}, u32[]{:S(2)}, u32[]{:S(2)}) collective-permute-start(bf16[1,272,128]{2,1,0:T(8,128)(2,1)S(1)} %first.1), channel_id=1, source_target_pairs={{0,128},{8,137},{64,192},{72,201},{128,1},{136,8},{192,65},{200,72... | collective-permute-start | bytes 208904 | tf_op jit(solution)/shard_map/ppermute | solution.py:227
  23.7 0.0 collective-permute-done.1.refs_1_.q1
  23.7 1.3 %tiles0e.1 = (f32[4,480,128]{2,1,0:T(8,128)S(1)}, f32[4,128,128]{2,1,0:T(8,128)S(1)}) custom-call(bf16[2,272,128]{2,1,0:T(8,128)(2,1)S(1)} %chip.1.refs_0_, bf16[2,272,128]{2,1,0:T(8,128)(2,1)S(1)} %collective-permute-done.1.refs_1_.q1, bf16[2,272,128]{2,1,0:T(8,128)(2,1)S(1)} %collective-permute-done.2.q.refs_2_.q2, ...), custom_call_target="tpu_custom_call" | custom-call | flops 629145600 | bytes 2154496 | tf_op jit(solution)/shard_map/tiles0e/pallas_call | solution.py:32
  25.0 1.4 %collective-permute-done.4.q4 = bf16[1,272,128]{2,1,0:T(8,128)(2,1)S(1)} collective-permute-done((bf16[1,272,128]{2,1,0:T(8,128)(2,1)S(1)}, bf16[1,272,128]{2,1,0:T(8,128)(2,1)S(1)}, u32[]{:S(2)}, u32[]{:S(2)}) %collective-permute-start.4) | collective-permute-done | bytes 69664 | tf_op jit(solution)/shard_map/ppermute | solution.py:227
  26.3 0.0 collective-permute-done.3.q3
  26.4 0.0 collective-permute-done.8.kv1.refs_2_.refs_3_
  26.4 0.0 collective-permute-done.9.kv3.refs_3_.refs_4_
  26.4 0.1 collective-permute-start.10
  26.5 2.9 %collective-permute-start.11 = (bf16[4,480,128]{2,1,0:T(8,128)(2,1)S(1)}, bf16[4,480,128]{2,1,0:T(8,128)(2,1)S(1)}, u32[]{:S(2)}, u32[]{:S(2)}) collective-permute-start(bf16[4,480,128]{2,1,0:T(8,128)(2,1)S(1)} %late.1), channel_id=1, source_target_pairs={{0,32},{2,34},{4,36},{6,38},{8,12},{10,14},{12,8},{14,10},{16,48},... | collective-permute-start | bytes 1474568 | tf_op jit(solution)/shard_map/ppermute | solution.py:241
  29.4 4.9 %tiles13a.1 = (f32[4,480,128]{2,1,0:T(8,128)S(1)}, f32[4,480,128]{2,1,0:T(8,128)S(1)}, f32[4,128,128]{2,1,0:T(8,128)S(1)}, f32[4,128,128]{2,1,0:T(8,128)S(1)}) custom-call(bf16[2,272,128]{2,1,0:T(8,128)(2,1)S(1)} %chip.1.refs_0_, bf16[7,272,128]{2,1,0:T(8,128)(2,1)S(1)} %gather.1.after.refs_1_, ...), custom_call_target="tpu_custom_call", output_to_operand_aliasing={{2}: (4, {})} | custom-call | flops 2516582400 | bytes 4362240 | tf_op jit(solution)/shard_map/tiles13a/pallas_call | solution.py:32
  34.4 7.5 %tiles130.1 = (bf16[4,480,128]{2,1,0:T(8,128)(2,1)S(1)}, bf16[4,480,128]{2,1,0:T(8,128)(2,1)S(1)}, f32[4,480,128]{2,1,0:T(8,128)S(1)}, f32[4,128,128]{2,1,0:T(8,...) custom-call(bf16[2,272,128]{2,1,0:T(8,128)(2,1)S(1)} %chip.1.refs_0_, ...), custom_call_target="tpu_custom_call", output_to_operand_aliasing={{3}: (6, {}), {2}: (9, {})} | custom-call | flops 3774873600 | bytes 8552448 | tf_op jit(solution)/shard_map/tiles130/pallas_call | solution.py:32
  41.9 1.4 %collective-permute-start.12 = (bf16[4,480,128]{2,1,0:T(8,128)(2,1)S(1)}, bf16[4,480,128]{2,1,0:T(8,128)(2,1)S(1)}, u32[]{:S(2)}, u32[]{:S(2)}) collective-permute-start(bf16[4,480,128]{2,1,0:T(8,128)(2,1)S(1)} %get-tuple-element.43), channel_id=1, source_target_pairs={{0,48},{2,50},{4,52},{6,54},{8,14},{10,8},{12,10},{14,12},{16,0},{... | collective-permute-start | bytes 1474568 | tf_op jit(solution)/shard_map/ppermute | solution.py:241
  43.3 0.7 collective-permute-start.13
  44.0 4.9 %tiles2.1 = (bf16[4,480,128]{2,1,0:T(8,128)(2,1)S(1)}, f32[4,128,128]{2,1,0:T(8,128)S(1)}, f32[4,128,128]{2,1,0:T(8,128)S(1)}, f32[4,128,128]{2,1,0:T(8,128)S(1)}, f32[4,128,128]{2,1,0:T(8,128)S(1)}) custom-call(bf16[2,272,128]{2,1,0:T(8,128)(2,1)S(1)} %chip.1.refs_0_, ...), custom_call_target="tpu_custom_call", output_to_operand_aliasing={{1}: (4, {}), {2}: (5, {}), {3}: (6, {}), {4}: (7, {})} | custom-call | flops 2516582400 | bytes 4194304 | tf_op jit(solution)/shard_map/tiles2/pallas_call | solution.py:32
  48.9 0.1 collective-permute-start.14
  49.0 1.2 %collective-permute-start.15 = (bf16[4,480,128]{2,1,0:T(8,128)(2,1)S(1)}, bf16[4,480,128]{2,1,0:T(8,128)(2,1)S(1)}, u32[]{:S(2)}, u32[]{:S(2)}) collective-permute-start(bf16[4,480,128]{2,1,0:T(8,128)(2,1)S(1)} %get-tuple-element.48), channel_id=1, source_target_pairs={{0,32},{2,34},{4,36},{6,38},{8,12},{10,14},{12,8},{14,10},{16,48},... | collective-permute-start | bytes 1474568 | tf_op jit(solution)/shard_map/ppermute | solution.py:241
  50.2 0.6 collective-permute-done.12.refs_6_.b1
  50.8 2.6 %collective-permute-done.13.refs_7_.b3 = bf16[4,480,128]{2,1,0:T(8,128)(2,1)S(1)} collective-permute-done((bf16[4,480,128]{2,1,0:T(8,128)(2,1)S(1)}, bf16[4,480,128]{2,1,0:T(8,128)(2,1)S(1)}, u32[]{:S(2)}, u32[]{:S(2)}) %collective-permute-start.13) | collective-permute-done | bytes 491552 | tf_op jit(solution)/shard_map/ppermute | solution.py:241
  53.3 1.4 %tiles0.1 = (f32[4,480,128]{2,1,0:T(8,128)S(1)}, f32[4,128,128]{2,1,0:T(8,128)S(1)}) custom-call(bf16[2,272,128]{2,1,0:T(8,128)(2,1)S(1)} %chip.1.refs_0_, bf16[7,272,128]{2,1,0:T(8,128)(2,1)S(1)} %gather.1.after.refs_1_, bf16[7,272,128]{2,1,0:T(8,128)(2,1)S(1)} %collective-permute-done.10.refs_2_, ...), custom_call_target="tpu_custom_call", output_to_operand_aliasing={{1}: (4, {}), {0}: (5, {})} | custom-call | flops 629145600 | bytes 5079040 | tf_op jit(solution)/shard_map/tiles0/pallas_call | solution.py:32
  54.8 0.0 collective-permute-done.14.got
  54.8 0.8 %halves.1.after = bf16[8,128,128]{2,1,0:T(8,128)(2,1)} custom-call(f32[4,128,128]{2,1,0:T(8,128)S(1)} %get-tuple-element.39.g0, f32[4,128,128]{2,1,0:T(8,128)S(1)} %get-tuple-element.40.g1, f32[4,128,128]{2,1,0:T(8,128)S(1)} %get-tuple-element.45.g2, f32[8,128,128]{2,1,0:T(8,128)S(1)} %collective-permute-done.14.got), custom_call_target="tpu_custom_call" | custom-call | bytes 1572864 | tf_op jit(solution)/shard_map/halves/pallas_call | solution.py:32
  55.6 8.4 %all-to-all-start = ((bf16[8,128,128]{2,1,0:T(8,128)(2,1)}), bf16[8,128,128]{2,1,0:T(8,128)(2,1)S(1)}, u32[]{:S(2)}, u32[]{:S(2)}) async-start(bf16[8,128,128]{2,1,0:T(8,128)(2,1)} %halves.1.after), calls=%async_computation | async-start | bytes 524288 | tf_op jit(solution)/shard_map/all_to_all | solution.py:231
  64.0 0.0 collective-permute-done.15.b2
  64.0 0.2 merge.1
  64.2 0.2 collective-permute-start.16
  64.4 2.5 %collective-permute-start.17 = (bf16[480,128]{1,0:T(8,128)(2,1)S(1)}, bf16[480,128]{1,0:T(8,128)(2,1)S(1)}, u32[]{:S(2)}, u32[]{:S(2)}) collective-permute-start(bf16[480,128]{1,0:T(8,128)(2,1)S(1)} %get-tuple-element.51), channel_id=1, source_target_pairs={{0,4},{2,6},{4,0},{6,2},{8,40},{10,42},{12,44},{14,46},{16,20},{18... | collective-permute-start | bytes 368648 | tf_op jit(solution)/shard_map/ppermute | solution.py:241
  66.9 0.0 collective-permute-start.18
  66.9 2.2 %collective-permute-done.16.f1 = bf16[480,128]{1,0:T(8,128)(2,1)S(1)} collective-permute-done((bf16[480,128]{1,0:T(8,128)(2,1)S(1)}, bf16[480,128]{1,0:T(8,128)(2,1)S(1)}, u32[]{:S(2)}, u32[]{:S(2)}) %collective-permute-start.16) | collective-permute-done | bytes 122912 | tf_op jit(solution)/shard_map/ppermute | solution.py:241
  69.2 1.6 %collective-permute-done.17.f2 = bf16[480,128]{1,0:T(8,128)(2,1)S(1)} collective-permute-done((bf16[480,128]{1,0:T(8,128)(2,1)S(1)}, bf16[480,128]{1,0:T(8,128)(2,1)S(1)}, u32[]{:S(2)}, u32[]{:S(2)}) %collective-permute-start.17) | collective-permute-done | bytes 122912 | tf_op jit(solution)/shard_map/ppermute | solution.py:241
  70.8 2.3 %collective-permute-done.18.f3 = bf16[480,128]{1,0:T(8,128)(2,1)S(1)} collective-permute-done((bf16[480,128]{1,0:T(8,128)(2,1)S(1)}, bf16[480,128]{1,0:T(8,128)(2,1)S(1)}, u32[]{:S(2)}, u32[]{:S(2)}) %collective-permute-start.18) | collective-permute-done | bytes 122912 | tf_op jit(solution)/shard_map/ppermute | solution.py:241
  73.0 0.8 %last.1 = (f32[128,128]{1,0:T(8,128)}, f32[240,128]{1,0:T(8,128)}, f32[240,128]{1,0:T(8,128)}) custom-call(bf16[8,128,128]{2,1,0:T(8,128)(2,1)S(1)} %all-to-all-done.u, f32[480,128]{1,0:T(8,128)S(1)} %get-tuple-element.49.own, bf16[480,128]{1,0:T(8,128)(2,1)S(1)} %collective-permute-done.16.f1, bf16[480,128]{1,0:T(8,128)(2,1)S(1)} %collective-permute-done.17.f2, ...), custom_call_target="tpu_custom_call" | custom-call | bytes 1187840 | tf_op jit(solution)/shard_map/last/pallas_call | solution.py:32
  (11 shorter events, 0.2 us)
Async XLA Ops:
  2.3 5.8 %collective-permute-start = (bf16[272,128]{1,0:T(8,128)(2,1)}, bf16[272,128]{1,0:T(8,128)(2,1)S(1)}, u32[]{:S(2)}, u32[]{:S(2)}) collective-permute-start(bf16[272,128]{1,0:T(8,128)(2,1)} %get-tuple-element.28.q0), channel_id=1, source_target_pairs={{0,8},{8,0},{1,9},{9,1},{2,10},{10,2},{3,11},{11,3},{4,12},{12,4},... | collective-permute-start | bytes 208904 | tf_op jit(solution)/shard_map/ppermute | solution.py:219
  2.4 13.1 %copy-start = (bf16[480,128]{1,0:T(8,128)(2,1)S(1)}, bf16[480,128]{1,0:T(8,128)(2,1)}, u32[]{:S(2)}) copy-start(bf16[480,128]{1,0:T(8,128)(2,1)} %get-tuple-element.29.k0) | copy-start | bytes 368644
  2.4 13.1 %collective-permute-start.5 = (bf16[480,128]{1,0:T(8,128)(2,1)}, bf16[480,128]{1,0:T(8,128)(2,1)S(1)}, u32[]{:S(2)}, u32[]{:S(2)}) collective-permute-start(bf16[480,128]{1,0:T(8,128)(2,1)} %get-tuple-element.29.k0), channel_id=1, source_target_pairs={{0,2},{2,4},{4,6},{6,0},{8,24},{10,26},{12,28},{14,30},{16,18},{18... | collective-permute-start | bytes 368648 | tf_op jit(solution)/shard_map/ppermute | solution.py:241
  4.0 11.6 %collective-permute-start.6 = (bf16[480,128]{1,0:T(8,128)(2,1)}, bf16[480,128]{1,0:T(8,128)(2,1)S(1)}, u32[]{:S(2)}, u32[]{:S(2)}) collective-permute-start(bf16[480,128]{1,0:T(8,128)(2,1)} %get-tuple-element.29.k0), channel_id=1, source_target_pairs={{0,4},{2,6},{4,0},{6,2},{8,40},{10,42},{12,44},{14,46},{16,20},{18... | collective-permute-start | bytes 368648 | tf_op jit(solution)/shard_map/ppermute | solution.py:241
  6.7 8.8 %collective-permute-start.7 = (bf16[480,128]{1,0:T(8,128)(2,1)}, bf16[480,128]{1,0:T(8,128)(2,1)S(1)}, u32[]{:S(2)}, u32[]{:S(2)}) collective-permute-start(bf16[480,128]{1,0:T(8,128)(2,1)} %get-tuple-element.29.k0), channel_id=1, source_target_pairs={{0,6},{2,0},{4,2},{6,4},{8,56},{10,58},{12,60},{14,62},{16,22},{18... | collective-permute-start | bytes 368648 | tf_op jit(solution)/shard_map/ppermute | solution.py:241
  8.1 0.9 %copy-start.1 = (bf16[272,128]{1,0:T(8,128)(2,1)S(1)}, bf16[272,128]{1,0:T(8,128)(2,1)}, u32[]{:S(2)}) copy-start(bf16[272,128]{1,0:T(8,128)(2,1)} %get-tuple-element.28.q0) | copy-start | bytes 208900
  9.0 10.0 %collective-permute-start.2 = (bf16[2,272,128]{2,1,0:T(8,128)(2,1)S(1)}, bf16[2,272,128]{2,1,0:T(8,128)(2,1)S(1)}, u32[]{:S(2)}, u32[]{:S(2)}) collective-permute-start(bf16[2,272,128]{2,1,0:T(8,128)(2,1)S(1)} %chip.1.refs_0_), channel_id=1, source_target_pairs={{0,128},{8,137},{64,192},{72,201},{128,1},{136,8},{192,65},{200,72... | collective-permute-start | bytes 417800 | tf_op jit(solution)/shard_map/ppermute | solution.py:227
  12.4 11.3 %collective-permute-start.1 = (bf16[2,272,128]{2,1,0:T(8,128)(2,1)S(1)}, bf16[2,272,128]{2,1,0:T(8,128)(2,1)S(1)}, u32[]{:S(2)}, u32[]{:S(2)}) collective-permute-start(bf16[2,272,128]{2,1,0:T(8,128)(2,1)S(1)} %chip.1.refs_0_), channel_id=1, source_target_pairs={{0,64},{8,201},{64,128},{72,8},{128,192},{136,72},{192,1},{200,136... | collective-permute-start | bytes 417800 | tf_op jit(solution)/shard_map/ppermute | solution.py:227
  15.6 10.8 %collective-permute-start.8 = (bf16[4,480,128]{2,1,0:T(8,128)(2,1)S(1)}, bf16[4,480,128]{2,1,0:T(8,128)(2,1)S(1)}, u32[]{:S(2)}, u32[]{:S(2)}) collective-permute-start(bf16[4,480,128]{2,1,0:T(8,128)(2,1)S(1)} %join.1.refs_3_.x.refs_5_), channel_id=1, source_target_pairs={{0,16},{2,18},{4,20},{6,22},{8,10},{10,12},{12,14},{14,8},{16,32},... | collective-permute-start | bytes 1474568 | tf_op jit(solution)/shard_map/ppermute | solution.py:241
  17.2 9.1 %collective-permute-start.9 = (bf16[4,480,128]{2,1,0:T(8,128)(2,1)S(1)}, bf16[4,480,128]{2,1,0:T(8,128)(2,1)S(1)}, u32[]{:S(2)}, u32[]{:S(2)}) collective-permute-start(bf16[4,480,128]{2,1,0:T(8,128)(2,1)S(1)} %join.1.refs_3_.x.refs_5_), channel_id=1, source_target_pairs={{0,48},{2,50},{4,52},{6,54},{8,14},{10,8},{12,10},{14,12},{16,0},{... | collective-permute-start | bytes 1474568 | tf_op jit(solution)/shard_map/ppermute | solution.py:241
  19.0 7.3 %collective-permute-start.3 = (bf16[2,272,128]{2,1,0:T(8,128)(2,1)S(1)}, bf16[2,272,128]{2,1,0:T(8,128)(2,1)S(1)}, u32[]{:S(2)}, u32[]{:S(2)}) collective-permute-start(bf16[2,272,128]{2,1,0:T(8,128)(2,1)S(1)} %collective-permute-done.2.q.refs_2_.q2), channel_id=1, source_target_pairs={{0,64},{8,201},{64,128},{72,8},{128,192},{136,72},{192,1},{200,136... | collective-permute-start | bytes 417800 | tf_op jit(solution)/shard_map/ppermute | solution.py:227
  19.9 6.4 %collective-permute-start.4 = (bf16[1,272,128]{2,1,0:T(8,128)(2,1)S(1)}, bf16[1,272,128]{2,1,0:T(8,128)(2,1)S(1)}, u32[]{:S(2)}, u32[]{:S(2)}) collective-permute-start(bf16[1,272,128]{2,1,0:T(8,128)(2,1)S(1)} %first.1), channel_id=1, source_target_pairs={{0,128},{8,137},{64,192},{72,201},{128,1},{136,8},{192,65},{200,72... | collective-permute-start | bytes 208904 | tf_op jit(solution)/shard_map/ppermute | solution.py:227
  26.4 8.0 %collective-permute-start.10 = (bf16[7,272,128]{2,1,0:T(8,128)(2,1)S(1)}, bf16[7,272,128]{2,1,0:T(8,128)(2,1)S(1)}, u32[]{:S(2)}, u32[]{:S(2)}) collective-permute-start(bf16[7,272,128]{2,1,0:T(8,128)(2,1)S(1)} %gather.1.after.refs_1_), channel_id=1, source_target_pairs={{0,8},{8,0},{1,9},{9,1},{2,10},{10,2},{3,11},{11,3},{4,12},{12,4},... | collective-permute-start | bytes 1462280 | tf_op jit(solution)/shard_map/ppermute | solution.py:219
  26.5 17.4 %collective-permute-start.11 = (bf16[4,480,128]{2,1,0:T(8,128)(2,1)S(1)}, bf16[4,480,128]{2,1,0:T(8,128)(2,1)S(1)}, u32[]{:S(2)}, u32[]{:S(2)}) collective-permute-start(bf16[4,480,128]{2,1,0:T(8,128)(2,1)S(1)} %late.1), channel_id=1, source_target_pairs={{0,32},{2,34},{4,36},{6,38},{8,12},{10,14},{12,8},{14,10},{16,48},... | collective-permute-start | bytes 1474568 | tf_op jit(solution)/shard_map/ppermute | solution.py:241
  41.9 8.9 %collective-permute-start.12 = (bf16[4,480,128]{2,1,0:T(8,128)(2,1)S(1)}, bf16[4,480,128]{2,1,0:T(8,128)(2,1)S(1)}, u32[]{:S(2)}, u32[]{:S(2)}) collective-permute-start(bf16[4,480,128]{2,1,0:T(8,128)(2,1)S(1)} %get-tuple-element.43), channel_id=1, source_target_pairs={{0,48},{2,50},{4,52},{6,54},{8,14},{10,8},{12,10},{14,12},{16,0},{... | collective-permute-start | bytes 1474568 | tf_op jit(solution)/shard_map/ppermute | solution.py:241
  43.3 10.0 %collective-permute-start.13 = (bf16[4,480,128]{2,1,0:T(8,128)(2,1)S(1)}, bf16[4,480,128]{2,1,0:T(8,128)(2,1)S(1)}, u32[]{:S(2)}, u32[]{:S(2)}) collective-permute-start(bf16[4,480,128]{2,1,0:T(8,128)(2,1)S(1)} %get-tuple-element.44), channel_id=1, source_target_pairs={{0,16},{2,18},{4,20},{6,22},{8,10},{10,12},{12,14},{14,8},{16,32},... | collective-permute-start | bytes 1474568 | tf_op jit(solution)/shard_map/ppermute | solution.py:241
  48.9 5.9 %collective-permute-start.14 = (f32[8,128,128]{2,1,0:T(8,128)S(1)}, f32[8,128,128]{2,1,0:T(8,128)S(1)}, u32[]{:S(2)}, u32[]{:S(2)}) collective-permute-start(f32[8,128,128]{2,1,0:T(8,128)S(1)} %others.1), channel_id=1, source_target_pairs={{0,8},{8,0},{1,9},{9,1},{2,10},{10,2},{3,11},{11,3},{4,12},{12,4},... | collective-permute-start | bytes 1572872 | tf_op jit(solution)/shard_map/ppermute | solution.py:219
  49.0 15.0 %collective-permute-start.15 = (bf16[4,480,128]{2,1,0:T(8,128)(2,1)S(1)}, bf16[4,480,128]{2,1,0:T(8,128)(2,1)S(1)}, u32[]{:S(2)}, u32[]{:S(2)}) collective-permute-start(bf16[4,480,128]{2,1,0:T(8,128)(2,1)S(1)} %get-tuple-element.48), channel_id=1, source_target_pairs={{0,32},{2,34},{4,36},{6,38},{8,12},{10,14},{12,8},{14,10},{16,48},... | collective-permute-start | bytes 1474568 | tf_op jit(solution)/shard_map/ppermute | solution.py:241
  55.6 17.5 %all-to-all-start = ((bf16[8,128,128]{2,1,0:T(8,128)(2,1)}), bf16[8,128,128]{2,1,0:T(8,128)(2,1)S(1)}, u32[]{:S(2)}, u32[]{:S(2)}) async-start(bf16[8,128,128]{2,1,0:T(8,128)(2,1)} %halves.1.after), calls=%async_computation | async-start | bytes 524288 | tf_op jit(solution)/shard_map/all_to_all | solution.py:231
  64.2 5.0 %collective-permute-start.16 = (bf16[480,128]{1,0:T(8,128)(2,1)S(1)}, bf16[480,128]{1,0:T(8,128)(2,1)S(1)}, u32[]{:S(2)}, u32[]{:S(2)}) collective-permute-start(bf16[480,128]{1,0:T(8,128)(2,1)S(1)} %get-tuple-element.50), channel_id=1, source_target_pairs={{0,6},{2,0},{4,2},{6,4},{8,56},{10,58},{12,60},{14,62},{16,22},{18... | collective-permute-start | bytes 368648 | tf_op jit(solution)/shard_map/ppermute | solution.py:241
  64.4 6.4 %collective-permute-start.17 = (bf16[480,128]{1,0:T(8,128)(2,1)S(1)}, bf16[480,128]{1,0:T(8,128)(2,1)S(1)}, u32[]{:S(2)}, u32[]{:S(2)}) collective-permute-start(bf16[480,128]{1,0:T(8,128)(2,1)S(1)} %get-tuple-element.51), channel_id=1, source_target_pairs={{0,4},{2,6},{4,0},{6,2},{8,40},{10,42},{12,44},{14,46},{16,20},{18... | collective-permute-start | bytes 368648 | tf_op jit(solution)/shard_map/ppermute | solution.py:241
  66.9 6.1 %collective-permute-start.18 = (bf16[480,128]{1,0:T(8,128)(2,1)S(1)}, bf16[480,128]{1,0:T(8,128)(2,1)S(1)}, u32[]{:S(2)}, u32[]{:S(2)}) collective-permute-start(bf16[480,128]{1,0:T(8,128)(2,1)S(1)} %get-tuple-element.52), channel_id=1, source_target_pairs={{0,2},{2,4},{4,6},{6,0},{8,24},{10,26},{12,28},{14,30},{16,18},{18... | collective-permute-start | bytes 368648 | tf_op jit(solution)/shard_map/ppermute | solution.py:241

commit v5 on v4

--- a/solution.py
+++ b/solution.py
@@ -285,17 +285,18 @@
         acc,
     )
     qs = {0: chip, 1: mine, 2: sib}
-    (out1, out3, part0), acc = tiles(
-        "tiles130",
-        qs,
-        ((kv1, (2, 3), BF, part1), (kv3, (2, 3), BF, part3), (kv0, (1, 3), F32, part0)),
-        acc,
+    (out1, out3), acc = tiles(
+        "tiles13b", qs, ((kv1, (2, 3), BF, part1), (kv3, (2, 3), BF, part3)), acc
     )
     back1, back3 = send_plane(out1, -1, 1), send_plane(out3, -3, 1)
     (out2,), acc = tiles("tiles2", qs, ((kv2, (0, 1, 2, 3), BF, None),), acc)
-    (others,) = call(stack_kernel, "others", (sds((8, W, W), F32),), (acc[0], acc[1], acc[3]))
-    rs, back2 = swap_cores(others), send_plane(out2, -2, 1)
-    (out0,), acc = tiles("tiles0", qs, ((kv0, (2,), F32, part0),), acc, (back1, back3))
+    back2 = send_plane(out2, -2, 1)
+    (part0,), acc = tiles("tiles0c", qs, ((kv0, (1, 3), F32, part0),), acc, (back1,))
+    (others,) = call(
+        stack_kernel, "others", (sds((8, W, W), F32),), (acc[0], acc[1], acc[3])
+    )
+    rs = swap_cores(others)
+    (out0,), acc = tiles("tiles0", qs, ((kv0, (2,), F32, part0),), acc, (back3,))
 
     (halves,) = call(halves_kernel, "halves", (sds((8, W, W), BF),), (acc[0], acc[1], acc[2], rs))
     u = exchange_z(halves)

time: 74.1 us -> 74.6 us (level)
  waiting for transfers between devices: 10.8 us -> 9.87 us
  starting transfers between devices: 37.7 us -> 38.6 us
    ppermute x12, starting transfers between devices: 17.9 us -> 19 us  [send_plane(): return lax.ppermute(x, ('y', 'core', 'x'), pairs)]
    ppermute x12, waiting for transfers between devices: 9.24 us -> 8.36 us  [send_plane(): return lax.ppermute(x, ('y', 'core', 'x'), pairs)]
    pallas_call x15 -> x16, Pallas kernels: 23.7 us -> 23.9 us  [call(): pl.pallas_call(kernel, name=name, out_shape=outs, in_specs=spaces or [VM]...]
  transfers between devices with their start and end apart: 20 -> 20, of which waited for: 7 -> 6; matrix products, arithmetic and copies ran while one was open for 0% -> 0% of each run, Pallas kernels for 29% -> 29%
where the time goes in v5:
time: 74.6 us; the launch traced here: 74.1 us
  starting transfers between devices  38.6 us (52%)
  Pallas kernels  23.9 us (32%)
  waiting for transfers between devices  9.87 us (13%)
  local copies, waits for them, and re-layouts  0.89 us (1%)
  between operations  0.81 us (1%)
    pallas_call x16, Pallas kernels, call(): pl.pallas_call(kernel, name=name, out_shape=outs, in_specs=spaces or [VM]...  23.9 us
    ppermute x12, starting transfers between devices, send_plane(): return lax.ppermute(x, ('y', 'core', 'x'), pairs)  19 us
    ppermute x4, starting transfers between devices, send_z(): return lax.ppermute(x, ('zl', 'core', 'zh'), pairs)  11.1 us
    ppermute x12, waiting for transfers between devices, send_plane(): return lax.ppermute(x, ('y', 'core', 'x'), pairs)  8.36 us
    all_to_all x1, starting transfers between devices, exchange_z(): return lax.all_to_all(x, ('zl', 'zh'), 0, 0, tiled=True)  8.27 us
    ppermute x4, waiting for transfers between devices, send_z(): return lax.ppermute(x, ('zl', 'core', 'zh'), pairs)  1.5 us
  transfers between devices with their start and end apart: 20, of which 6 were waited for; matrix products, arithmetic and copies ran while one was open for 0% of the time, Pallas kernels for 29%

profile of v5, /device:TPU:32, one launch (start us, length us, event | category | flops | bytes accessed | tf_op | source)
XLA Modules:
  0.0 74.1 jit_solution(10230503425359361320)
XLA Ops:
  0.6 1.7 %pack.1 = (bf16[272,128]{1,0:T(8,128)(2,1)}, bf16[480,128]{1,0:T(8,128)(2,1)}) custom-call(bf16[128,128]{1,0:T(8,128)(2,1)} %q.1, bf16[128,128]{1,0:T(8,128)(2,1)} %g.1, bf16[128,128]{1,0:T(8,128)(2,1)} %o.1, f32[1,128]{1,0:T(1,128)} %bitcast.1, bf16[240,128]{1,0:T(8,128)(2,1)} %k.1, bf16[240,128]{1,0:T(8,128)(2,1)} %v.1), custom_call_target="tpu_custom_call" | custom-call | bytes 414208 | tf_op jit(solution)/shard_map/pack/pallas_call | solution.py:32
  2.3 0.1 collective-permute-start
  2.4 0.0 copy-start
  2.4 1.6 %collective-permute-start.5 = (bf16[480,128]{1,0:T(8,128)(2,1)}, bf16[480,128]{1,0:T(8,128)(2,1)S(1)}, u32[]{:S(2)}, u32[]{:S(2)}) collective-permute-start(bf16[480,128]{1,0:T(8,128)(2,1)} %get-tuple-element.30.k0), channel_id=1, source_target_pairs={{0,2},{2,4},{4,6},{6,0},{8,24},{10,26},{12,28},{14,30},{16,18},{18... | collective-permute-start | bytes 368648 | tf_op jit(solution)/shard_map/ppermute | solution.py:241
  4.0 2.7 %collective-permute-start.6 = (bf16[480,128]{1,0:T(8,128)(2,1)}, bf16[480,128]{1,0:T(8,128)(2,1)S(1)}, u32[]{:S(2)}, u32[]{:S(2)}) collective-permute-start(bf16[480,128]{1,0:T(8,128)(2,1)} %get-tuple-element.30.k0), channel_id=1, source_target_pairs={{0,4},{2,6},{4,0},{6,2},{8,40},{10,42},{12,44},{14,46},{16,20},{18... | collective-permute-start | bytes 368648 | tf_op jit(solution)/shard_map/ppermute | solution.py:241
  6.7 1.4 %collective-permute-start.7 = (bf16[480,128]{1,0:T(8,128)(2,1)}, bf16[480,128]{1,0:T(8,128)(2,1)S(1)}, u32[]{:S(2)}, u32[]{:S(2)}) collective-permute-start(bf16[480,128]{1,0:T(8,128)(2,1)} %get-tuple-element.30.k0), channel_id=1, source_target_pairs={{0,6},{2,0},{4,2},{6,4},{8,56},{10,58},{12,60},{14,62},{16,22},{18... | collective-permute-start | bytes 368648 | tf_op jit(solution)/shard_map/ppermute | solution.py:241
  8.1 0.0 collective-permute-done.q1
  8.1 0.9 %copy-done.1 = bf16[272,128]{1,0:T(8,128)(2,1)S(1)} copy-done((bf16[272,128]{1,0:T(8,128)(2,1)S(1)}, bf16[272,128]{1,0:T(8,128)(2,1)}, u32[]{:S(2)}) %copy-start.1) | copy-done | bytes 69656
  9.0 3.3 %collective-permute-start.2 = (bf16[2,272,128]{2,1,0:T(8,128)(2,1)S(1)}, bf16[2,272,128]{2,1,0:T(8,128)(2,1)S(1)}, u32[]{:S(2)}, u32[]{:S(2)}) collective-permute-start(bf16[2,272,128]{2,1,0:T(8,128)(2,1)S(1)} %chip.1.refs_0_), channel_id=1, source_target_pairs={{0,128},{8,137},{64,192},{72,201},{128,1},{136,8},{192,65},{200,72... | collective-permute-start | bytes 417800 | tf_op jit(solution)/shard_map/ppermute | solution.py:227
  12.4 3.1 %collective-permute-start.1 = (bf16[2,272,128]{2,1,0:T(8,128)(2,1)S(1)}, bf16[2,272,128]{2,1,0:T(8,128)(2,1)S(1)}, u32[]{:S(2)}, u32[]{:S(2)}) collective-permute-start(bf16[2,272,128]{2,1,0:T(8,128)(2,1)S(1)} %chip.1.refs_0_), channel_id=1, source_target_pairs={{0,64},{8,201},{64,128},{72,8},{128,192},{136,72},{192,1},{200,136... | collective-permute-start | bytes 417800 | tf_op jit(solution)/shard_map/ppermute | solution.py:227
  15.5 0.0 collective-permute-done.5.k1
  15.5 0.0 collective-permute-done.6.k2
  15.5 0.0 collective-permute-done.7.k3
  15.6 1.7 %collective-permute-start.8 = (bf16[4,480,128]{2,1,0:T(8,128)(2,1)S(1)}, bf16[4,480,128]{2,1,0:T(8,128)(2,1)S(1)}, u32[]{:S(2)}, u32[]{:S(2)}) collective-permute-start(bf16[4,480,128]{2,1,0:T(8,128)(2,1)S(1)} %join.1.refs_3_.x), channel_id=1, source_target_pairs={{0,16},{2,18},{4,20},{6,22},{8,10},{10,12},{12,14},{14,8},{16,32},... | collective-permute-start | bytes 1474568 | tf_op jit(solution)/shard_map/ppermute | solution.py:241
  17.2 1.7 %collective-permute-start.9 = (bf16[4,480,128]{2,1,0:T(8,128)(2,1)S(1)}, bf16[4,480,128]{2,1,0:T(8,128)(2,1)S(1)}, u32[]{:S(2)}, u32[]{:S(2)}) collective-permute-start(bf16[4,480,128]{2,1,0:T(8,128)(2,1)S(1)} %join.1.refs_3_.x), channel_id=1, source_target_pairs={{0,48},{2,50},{4,52},{6,54},{8,14},{10,8},{12,10},{14,12},{16,0},{... | collective-permute-start | bytes 1474568 | tf_op jit(solution)/shard_map/ppermute | solution.py:241
  18.9 0.1 collective-permute-done.2.q.refs_2_.q2
  19.0 0.9 %collective-permute-start.3 = (bf16[2,272,128]{2,1,0:T(8,128)(2,1)S(1)}, bf16[2,272,128]{2,1,0:T(8,128)(2,1)S(1)}, u32[]{:S(2)}, u32[]{:S(2)}) collective-permute-start(bf16[2,272,128]{2,1,0:T(8,128)(2,1)S(1)} %collective-permute-done.2.q.refs_2_.q2), channel_id=1, source_target_pairs={{0,64},{8,201},{64,128},{72,8},{128,192},{136,72},{192,1},{200,136... | collective-permute-start | bytes 417800 | tf_op jit(solution)/shard_map/ppermute | solution.py:227
  19.9 3.7 %collective-permute-start.4 = (bf16[1,272,128]{2,1,0:T(8,128)(2,1)S(1)}, bf16[1,272,128]{2,1,0:T(8,128)(2,1)S(1)}, u32[]{:S(2)}, u32[]{:S(2)}) collective-permute-start(bf16[1,272,128]{2,1,0:T(8,128)(2,1)S(1)} %first.1), channel_id=1, source_target_pairs={{0,128},{8,137},{64,192},{72,201},{128,1},{136,8},{192,65},{200,72... | collective-permute-start | bytes 208904 | tf_op jit(solution)/shard_map/ppermute | solution.py:227
  23.7 0.0 collective-permute-done.1.refs_1_.q1
  23.7 1.3 %tiles0e.1 = (f32[4,480,128]{2,1,0:T(8,128)S(1)}, f32[4,128,128]{2,1,0:T(8,128)S(1)}) custom-call(bf16[2,272,128]{2,1,0:T(8,128)(2,1)S(1)} %chip.1.refs_0_, bf16[2,272,128]{2,1,0:T(8,128)(2,1)S(1)} %collective-permute-done.1.refs_1_.q1, bf16[2,272,128]{2,1,0:T(8,128)(2,1)S(1)} %collective-permute-done.2.q.refs_2_.q2, bf16[4,480,128]{2,1,0:T(8,128)(2,1)S(1)} %join.1.refs_3_.x), custom_call_target="tpu_custom_call" | custom-call | flops 629145600 | bytes 2154496 | tf_op jit(solution)/shard_map/tiles0e/pallas_call | solution.py:32
  25.0 1.4 %collective-permute-done.4.q4 = bf16[1,272,128]{2,1,0:T(8,128)(2,1)S(1)} collective-permute-done((bf16[1,272,128]{2,1,0:T(8,128)(2,1)S(1)}, bf16[1,272,128]{2,1,0:T(8,128)(2,1)S(1)}, u32[]{:S(2)}, u32[]{:S(2)}) %collective-permute-start.4) | collective-permute-done | bytes 69664 | tf_op jit(solution)/shard_map/ppermute | solution.py:227
  26.3 0.0 collective-permute-done.3.q3
  26.4 0.1 collective-permute-start.10
  26.5 2.9 %collective-permute-start.11 = (bf16[4,480,128]{2,1,0:T(8,128)(2,1)S(1)}, bf16[4,480,128]{2,1,0:T(8,128)(2,1)S(1)}, u32[]{:S(2)}, u32[]{:S(2)}) collective-permute-start(bf16[4,480,128]{2,1,0:T(8,128)(2,1)S(1)} %late.1), channel_id=1, source_target_pairs={{0,32},{2,34},{4,36},{6,38},{8,12},{10,14},{12,8},{14,10},{16,48},... | collective-permute-start | bytes 1474568 | tf_op jit(solution)/shard_map/ppermute | solution.py:241
  29.4 4.9 %tiles13a.1 = (f32[4,480,128]{2,1,0:T(8,128)S(1)}, f32[4,480,128]{2,1,0:T(8,128)S(1)}, f32[4,128,128]{2,1,0:T(8,128)S(1)}, f32[4,128,128]{2,1,0:T(8,128)S(1)}) custom-call(bf16[2,272,128]{2,1,0:T(8,128)(2,1)S(1)} %chip.1.refs_0_, bf16[7,272,128]{2,1,0:T(8,128)(2,1)S(1)} %gather.1.after.refs_1_, ...), custom_call_target="tpu_custom_call", output_to_operand_aliasing={{2}: (4, {})} | custom-call | flops 2516582400 | bytes 4362240 | tf_op jit(solution)/shard_map/tiles13a/pallas_call | solution.py:32
  34.4 0.0 collective-permute-done.10.refs_2_
  34.4 5.0 %tiles13b.1 = (bf16[4,480,128]{2,1,0:T(8,128)(2,1)S(1)}, bf16[4,480,128]{2,1,0:T(8,128)(2,1)S(1)}, f32[4,128,128]{2,1,0:T(8,128)S(1)}, f32[4,128,128]{2,1,0:T(8,128)S(1)}) custom-call(bf16[2,272,128]{2,1,0:T(8,128)(2,1)S(1)} %chip.1.refs_0_, bf16[7,272,128]{2,1,0:T(8,128)(2,1)S(1)} %gather.1.after.refs_1_, ...), custom_call_target="tpu_custom_call" | custom-call | flops 2516582400 | bytes 5570560 | tf_op jit(solution)/shard_map/tiles13b/pallas_call | solution.py:32
  39.4 1.4 %collective-permute-start.12 = (bf16[4,480,128]{2,1,0:T(8,128)(2,1)S(1)}, bf16[4,480,128]{2,1,0:T(8,128)(2,1)S(1)}, u32[]{:S(2)}, u32[]{:S(2)}) collective-permute-start(bf16[4,480,128]{2,1,0:T(8,128)(2,1)S(1)} %get-tuple-element.42), channel_id=1, source_target_pairs={{0,48},{2,50},{4,52},{6,54},{8,14},{10,8},{12,10},{14,12},{16,0},{... | collective-permute-start | bytes 1474568 | tf_op jit(solution)/shard_map/ppermute | solution.py:241
  40.8 0.7 collective-permute-start.13
  41.5 0.0 collective-permute-done.11.refs_3_
  41.5 4.9 %tiles2.1 = (bf16[4,480,128]{2,1,0:T(8,128)(2,1)S(1)}, f32[4,128,128]{2,1,0:T(8,128)S(1)}, f32[4,128,128]{2,1,0:T(8,128)S(1)}, f32[4,128,128]{2,1,0:T(8,128)S(1)}, f32[4,128,128]{2,1,0:T(8,128)S(1)}) custom-call(bf16[2,272,128]{2,1,0:T(8,128)(2,1)S(1)} %chip.1.refs_0_, ...), custom_call_target="tpu_custom_call", output_to_operand_aliasing={{1}: (4, {}), {2}: (5, {}), {3}: (6, {}), {4}: (7, {})} | custom-call | flops 2516582400 | bytes 4194304 | tf_op jit(solution)/shard_map/tiles2/pallas_call | solution.py:32
  46.4 1.9 %collective-permute-done.12.refs_7_.b1 = bf16[4,480,128]{2,1,0:T(8,128)(2,1)S(1)} collective-permute-done((bf16[4,480,128]{2,1,0:T(8,128)(2,1)S(1)}, bf16[4,480,128]{2,1,0:T(8,128)(2,1)S(1)}, u32[]{:S(2)}, u32[]{:S(2)}) %collective-permute-start.12) | collective-permute-done | bytes 491552 | tf_op jit(solution)/shard_map/ppermute | solution.py:241
  48.3 2.7 %tiles0c.1 = (f32[4,480,128]{2,1,0:T(8,128)S(1)}, f32[4,128,128]{2,1,0:T(8,128)S(1)}, f32[4,128,128]{2,1,0:T(8,128)S(1)}) custom-call(bf16[2,272,128]{2,1,0:T(8,128)(2,1)S(1)} %chip.1.refs_0_, bf16[7,272,128]{2,1,0:T(8,128)(2,1)S(1)} %gather.1.after.refs_1_, ...), custom_call_target="tpu_custom_call", output_to_operand_aliasing={{1}: (4, {}), {2}: (5, {}), {0}: (6, {})} | custom-call | flops 1258291200 | bytes 5111808 | tf_op jit(solution)/shard_map/tiles0c/pallas_call | solution.py:32
  51.0 0.1 collective-permute-start.14
  51.1 1.0 %collective-permute-start.15 = (bf16[4,480,128]{2,1,0:T(8,128)(2,1)S(1)}, bf16[4,480,128]{2,1,0:T(8,128)(2,1)S(1)}, u32[]{:S(2)}, u32[]{:S(2)}) collective-permute-start(bf16[4,480,128]{2,1,0:T(8,128)(2,1)S(1)} %get-tuple-element.50), channel_id=1, source_target_pairs={{0,32},{2,34},{4,36},{6,38},{8,12},{10,14},{12,8},{14,10},{16,48},... | collective-permute-start | bytes 1474568 | tf_op jit(solution)/shard_map/ppermute | solution.py:241
  52.1 0.0 collective-permute-done.13.refs_6_.b3
  52.1 1.4 %tiles0.1 = (f32[4,480,128]{2,1,0:T(8,128)S(1)}, f32[4,128,128]{2,1,0:T(8,128)S(1)}) custom-call(bf16[2,272,128]{2,1,0:T(8,128)(2,1)S(1)} %chip.1.refs_0_, bf16[7,272,128]{2,1,0:T(8,128)(2,1)S(1)} %gather.1.after.refs_1_, bf16[7,272,128]{2,1,0:T(8,128)(2,1)S(1)} %collective-permute-done.10.refs_2_, ...), custom_call_target="tpu_custom_call", output_to_operand_aliasing={{1}: (4, {}), {0}: (5, {})} | custom-call | flops 629145600 | bytes 4587520 | tf_op jit(solution)/shard_map/tiles0/pallas_call | solution.py:32
  53.6 0.8 %halves.1.after = bf16[8,128,128]{2,1,0:T(8,128)(2,1)} custom-call(f32[4,128,128]{2,1,0:T(8,128)S(1)} %get-tuple-element.39.g0, f32[4,128,128]{2,1,0:T(8,128)S(1)} %get-tuple-element.43.g1, f32[4,128,128]{2,1,0:T(8,128)S(1)} %get-tuple-element.47.g2, f32[8,128,128]{2,1,0:T(8,128)S(1)} %collective-permute-done.14.got), custom_call_target="tpu_custom_call" | custom-call | bytes 1572864 | tf_op jit(solution)/shard_map/halves/pallas_call | solution.py:32
  54.4 8.3 %all-to-all-start = ((bf16[8,128,128]{2,1,0:T(8,128)(2,1)}), bf16[8,128,128]{2,1,0:T(8,128)(2,1)S(1)}, u32[]{:S(2)}, u32[]{:S(2)}) async-start(bf16[8,128,128]{2,1,0:T(8,128)(2,1)} %halves.1.after), calls=%async_computation | async-start | bytes 524288 | tf_op jit(solution)/shard_map/all_to_all | solution.py:231
  62.7 0.0 collective-permute-done.15.b2
  62.7 0.2 merge.1
  62.9 3.0 %collective-permute-start.16 = (bf16[480,128]{1,0:T(8,128)(2,1)S(1)}, bf16[480,128]{1,0:T(8,128)(2,1)S(1)}, u32[]{:S(2)}, u32[]{:S(2)}) collective-permute-start(bf16[480,128]{1,0:T(8,128)(2,1)S(1)} %get-tuple-element.52), channel_id=1, source_target_pairs={{0,6},{2,0},{4,2},{6,4},{8,56},{10,58},{12,60},{14,62},{16,22},{18... | collective-permute-start | bytes 368648 | tf_op jit(solution)/shard_map/ppermute | solution.py:241
  65.9 1.0 %collective-permute-start.18 = (bf16[480,128]{1,0:T(8,128)(2,1)S(1)}, bf16[480,128]{1,0:T(8,128)(2,1)S(1)}, u32[]{:S(2)}, u32[]{:S(2)}) collective-permute-start(bf16[480,128]{1,0:T(8,128)(2,1)S(1)} %get-tuple-element.54), channel_id=1, source_target_pairs={{0,2},{2,4},{4,6},{6,0},{8,24},{10,26},{12,28},{14,30},{16,18},{18... | collective-permute-start | bytes 368648 | tf_op jit(solution)/shard_map/ppermute | solution.py:241
  66.9 2.8 %collective-permute-done.16.f1 = bf16[480,128]{1,0:T(8,128)(2,1)S(1)} collective-permute-done((bf16[480,128]{1,0:T(8,128)(2,1)S(1)}, bf16[480,128]{1,0:T(8,128)(2,1)S(1)}, u32[]{:S(2)}, u32[]{:S(2)}) %collective-permute-start.16) | collective-permute-done | bytes 122912 | tf_op jit(solution)/shard_map/ppermute | solution.py:241
  69.7 2.7 %collective-permute-done.17.f2 = bf16[480,128]{1,0:T(8,128)(2,1)S(1)} collective-permute-done((bf16[480,128]{1,0:T(8,128)(2,1)S(1)}, bf16[480,128]{1,0:T(8,128)(2,1)S(1)}, u32[]{:S(2)}, u32[]{:S(2)}) %collective-permute-start.17) | collective-permute-done | bytes 122912 | tf_op jit(solution)/shard_map/ppermute | solution.py:241
  72.4 0.9 %collective-permute-done.18.f3 = bf16[480,128]{1,0:T(8,128)(2,1)S(1)} collective-permute-done((bf16[480,128]{1,0:T(8,128)(2,1)S(1)}, bf16[480,128]{1,0:T(8,128)(2,1)S(1)}, u32[]{:S(2)}, u32[]{:S(2)}) %collective-permute-start.18) | collective-permute-done | bytes 122912 | tf_op jit(solution)/shard_map/ppermute | solution.py:241
  73.3 0.0 all-to-all-done.u
  73.3 0.8 %last.1 = (f32[128,128]{1,0:T(8,128)}, f32[240,128]{1,0:T(8,128)}, f32[240,128]{1,0:T(8,128)}) custom-call(bf16[8,128,128]{2,1,0:T(8,128)(2,1)S(1)} %all-to-all-done.u, f32[480,128]{1,0:T(8,128)S(1)} %get-tuple-element.51.own, bf16[480,128]{1,0:T(8,128)(2,1)S(1)} %collective-permute-done.16.f1, bf16[480,128]{1,0:T(8,128)(2,1)S(1)} %collective-permute-done.17.f2, ...), custom_call_target="tpu_custom_call" | custom-call | bytes 1187840 | tf_op jit(solution)/shard_map/last/pallas_call | solution.py:32
  (12 shorter events, 0.2 us)
Async XLA Ops:
  2.3 5.8 %collective-permute-start = (bf16[272,128]{1,0:T(8,128)(2,1)}, bf16[272,128]{1,0:T(8,128)(2,1)S(1)}, u32[]{:S(2)}, u32[]{:S(2)}) collective-permute-start(bf16[272,128]{1,0:T(8,128)(2,1)} %get-tuple-element.29.q0), channel_id=1, source_target_pairs={{0,8},{8,0},{1,9},{9,1},{2,10},{10,2},{3,11},{11,3},{4,12},{12,4},... | collective-permute-start | bytes 208904 | tf_op jit(solution)/shard_map/ppermute | solution.py:219
  2.4 13.1 %copy-start = (bf16[480,128]{1,0:T(8,128)(2,1)S(1)}, bf16[480,128]{1,0:T(8,128)(2,1)}, u32[]{:S(2)}) copy-start(bf16[480,128]{1,0:T(8,128)(2,1)} %get-tuple-element.30.k0) | copy-start | bytes 368644
  2.4 13.1 %collective-permute-start.5 = (bf16[480,128]{1,0:T(8,128)(2,1)}, bf16[480,128]{1,0:T(8,128)(2,1)S(1)}, u32[]{:S(2)}, u32[]{:S(2)}) collective-permute-start(bf16[480,128]{1,0:T(8,128)(2,1)} %get-tuple-element.30.k0), channel_id=1, source_target_pairs={{0,2},{2,4},{4,6},{6,0},{8,24},{10,26},{12,28},{14,30},{16,18},{18... | collective-permute-start | bytes 368648 | tf_op jit(solution)/shard_map/ppermute | solution.py:241
  4.0 11.6 %collective-permute-start.6 = (bf16[480,128]{1,0:T(8,128)(2,1)}, bf16[480,128]{1,0:T(8,128)(2,1)S(1)}, u32[]{:S(2)}, u32[]{:S(2)}) collective-permute-start(bf16[480,128]{1,0:T(8,128)(2,1)} %get-tuple-element.30.k0), channel_id=1, source_target_pairs={{0,4},{2,6},{4,0},{6,2},{8,40},{10,42},{12,44},{14,46},{16,20},{18... | collective-permute-start | bytes 368648 | tf_op jit(solution)/shard_map/ppermute | solution.py:241
  6.7 8.8 %collective-permute-start.7 = (bf16[480,128]{1,0:T(8,128)(2,1)}, bf16[480,128]{1,0:T(8,128)(2,1)S(1)}, u32[]{:S(2)}, u32[]{:S(2)}) collective-permute-start(bf16[480,128]{1,0:T(8,128)(2,1)} %get-tuple-element.30.k0), channel_id=1, source_target_pairs={{0,6},{2,0},{4,2},{6,4},{8,56},{10,58},{12,60},{14,62},{16,22},{18... | collective-permute-start | bytes 368648 | tf_op jit(solution)/shard_map/ppermute | solution.py:241
  8.1 0.9 %copy-start.1 = (bf16[272,128]{1,0:T(8,128)(2,1)S(1)}, bf16[272,128]{1,0:T(8,128)(2,1)}, u32[]{:S(2)}) copy-start(bf16[272,128]{1,0:T(8,128)(2,1)} %get-tuple-element.29.q0) | copy-start | bytes 208900
  9.0 10.0 %collective-permute-start.2 = (bf16[2,272,128]{2,1,0:T(8,128)(2,1)S(1)}, bf16[2,272,128]{2,1,0:T(8,128)(2,1)S(1)}, u32[]{:S(2)}, u32[]{:S(2)}) collective-permute-start(bf16[2,272,128]{2,1,0:T(8,128)(2,1)S(1)} %chip.1.refs_0_), channel_id=1, source_target_pairs={{0,128},{8,137},{64,192},{72,201},{128,1},{136,8},{192,65},{200,72... | collective-permute-start | bytes 417800 | tf_op jit(solution)/shard_map/ppermute | solution.py:227
  12.4 11.3 %collective-permute-start.1 = (bf16[2,272,128]{2,1,0:T(8,128)(2,1)S(1)}, bf16[2,272,128]{2,1,0:T(8,128)(2,1)S(1)}, u32[]{:S(2)}, u32[]{:S(2)}) collective-permute-start(bf16[2,272,128]{2,1,0:T(8,128)(2,1)S(1)} %chip.1.refs_0_), channel_id=1, source_target_pairs={{0,64},{8,201},{64,128},{72,8},{128,192},{136,72},{192,1},{200,136... | collective-permute-start | bytes 417800 | tf_op jit(solution)/shard_map/ppermute | solution.py:227
  15.6 10.8 %collective-permute-start.8 = (bf16[4,480,128]{2,1,0:T(8,128)(2,1)S(1)}, bf16[4,480,128]{2,1,0:T(8,128)(2,1)S(1)}, u32[]{:S(2)}, u32[]{:S(2)}) collective-permute-start(bf16[4,480,128]{2,1,0:T(8,128)(2,1)S(1)} %join.1.refs_3_.x), channel_id=1, source_target_pairs={{0,16},{2,18},{4,20},{6,22},{8,10},{10,12},{12,14},{14,8},{16,32},... | collective-permute-start | bytes 1474568 | tf_op jit(solution)/shard_map/ppermute | solution.py:241
  17.2 9.1 %collective-permute-start.9 = (bf16[4,480,128]{2,1,0:T(8,128)(2,1)S(1)}, bf16[4,480,128]{2,1,0:T(8,128)(2,1)S(1)}, u32[]{:S(2)}, u32[]{:S(2)}) collective-permute-start(bf16[4,480,128]{2,1,0:T(8,128)(2,1)S(1)} %join.1.refs_3_.x), channel_id=1, source_target_pairs={{0,48},{2,50},{4,52},{6,54},{8,14},{10,8},{12,10},{14,12},{16,0},{... | collective-permute-start | bytes 1474568 | tf_op jit(solution)/shard_map/ppermute | solution.py:241
  19.0 7.3 %collective-permute-start.3 = (bf16[2,272,128]{2,1,0:T(8,128)(2,1)S(1)}, bf16[2,272,128]{2,1,0:T(8,128)(2,1)S(1)}, u32[]{:S(2)}, u32[]{:S(2)}) collective-permute-start(bf16[2,272,128]{2,1,0:T(8,128)(2,1)S(1)} %collective-permute-done.2.q.refs_2_.q2), channel_id=1, source_target_pairs={{0,64},{8,201},{64,128},{72,8},{128,192},{136,72},{192,1},{200,136... | collective-permute-start | bytes 417800 | tf_op jit(solution)/shard_map/ppermute | solution.py:227
  19.9 6.4 %collective-permute-start.4 = (bf16[1,272,128]{2,1,0:T(8,128)(2,1)S(1)}, bf16[1,272,128]{2,1,0:T(8,128)(2,1)S(1)}, u32[]{:S(2)}, u32[]{:S(2)}) collective-permute-start(bf16[1,272,128]{2,1,0:T(8,128)(2,1)S(1)} %first.1), channel_id=1, source_target_pairs={{0,128},{8,137},{64,192},{72,201},{128,1},{136,8},{192,65},{200,72... | collective-permute-start | bytes 208904 | tf_op jit(solution)/shard_map/ppermute | solution.py:227
  26.4 8.0 %collective-permute-start.10 = (bf16[7,272,128]{2,1,0:T(8,128)(2,1)S(1)}, bf16[7,272,128]{2,1,0:T(8,128)(2,1)S(1)}, u32[]{:S(2)}, u32[]{:S(2)}) collective-permute-start(bf16[7,272,128]{2,1,0:T(8,128)(2,1)S(1)} %gather.1.after.refs_1_), channel_id=1, source_target_pairs={{0,8},{8,0},{1,9},{9,1},{2,10},{10,2},{3,11},{11,3},{4,12},{12,4},... | collective-permute-start | bytes 1462280 | tf_op jit(solution)/shard_map/ppermute | solution.py:219
  26.5 14.9 %collective-permute-start.11 = (bf16[4,480,128]{2,1,0:T(8,128)(2,1)S(1)}, bf16[4,480,128]{2,1,0:T(8,128)(2,1)S(1)}, u32[]{:S(2)}, u32[]{:S(2)}) collective-permute-start(bf16[4,480,128]{2,1,0:T(8,128)(2,1)S(1)} %late.1), channel_id=1, source_target_pairs={{0,32},{2,34},{4,36},{6,38},{8,12},{10,14},{12,8},{14,10},{16,48},... | collective-permute-start | bytes 1474568 | tf_op jit(solution)/shard_map/ppermute | solution.py:241
  39.4 8.9 %collective-permute-start.12 = (bf16[4,480,128]{2,1,0:T(8,128)(2,1)S(1)}, bf16[4,480,128]{2,1,0:T(8,128)(2,1)S(1)}, u32[]{:S(2)}, u32[]{:S(2)}) collective-permute-start(bf16[4,480,128]{2,1,0:T(8,128)(2,1)S(1)} %get-tuple-element.42), channel_id=1, source_target_pairs={{0,48},{2,50},{4,52},{6,54},{8,14},{10,8},{12,10},{14,12},{16,0},{... | collective-permute-start | bytes 1474568 | tf_op jit(solution)/shard_map/ppermute | solution.py:241
  40.8 11.3 %collective-permute-start.13 = (bf16[4,480,128]{2,1,0:T(8,128)(2,1)S(1)}, bf16[4,480,128]{2,1,0:T(8,128)(2,1)S(1)}, u32[]{:S(2)}, u32[]{:S(2)}) collective-permute-start(bf16[4,480,128]{2,1,0:T(8,128)(2,1)S(1)} %get-tuple-element.46), channel_id=1, source_target_pairs={{0,16},{2,18},{4,20},{6,22},{8,10},{10,12},{12,14},{14,8},{16,32},... | collective-permute-start | bytes 1474568 | tf_op jit(solution)/shard_map/ppermute | solution.py:241
  51.0 2.6 %collective-permute-start.14 = (f32[8,128,128]{2,1,0:T(8,128)S(1)}, f32[8,128,128]{2,1,0:T(8,128)S(1)}, u32[]{:S(2)}, u32[]{:S(2)}) collective-permute-start(f32[8,128,128]{2,1,0:T(8,128)S(1)} %others.1), channel_id=1, source_target_pairs={{0,8},{8,0},{1,9},{9,1},{2,10},{10,2},{3,11},{11,3},{4,12},{12,4},... | collective-permute-start | bytes 1572872 | tf_op jit(solution)/shard_map/ppermute | solution.py:219
  51.1 11.6 %collective-permute-start.15 = (bf16[4,480,128]{2,1,0:T(8,128)(2,1)S(1)}, bf16[4,480,128]{2,1,0:T(8,128)(2,1)S(1)}, u32[]{:S(2)}, u32[]{:S(2)}) collective-permute-start(bf16[4,480,128]{2,1,0:T(8,128)(2,1)S(1)} %get-tuple-element.50), channel_id=1, source_target_pairs={{0,32},{2,34},{4,36},{6,38},{8,12},{10,14},{12,8},{14,10},{16,48},... | collective-permute-start | bytes 1474568 | tf_op jit(solution)/shard_map/ppermute | solution.py:241
  54.4 18.9 %all-to-all-start = ((bf16[8,128,128]{2,1,0:T(8,128)(2,1)}), bf16[8,128,128]{2,1,0:T(8,128)(2,1)S(1)}, u32[]{:S(2)}, u32[]{:S(2)}) async-start(bf16[8,128,128]{2,1,0:T(8,128)(2,1)} %halves.1.after), calls=%async_computation | async-start | bytes 524288 | tf_op jit(solution)/shard_map/all_to_all | solution.py:231
  62.9 6.8 %collective-permute-start.16 = (bf16[480,128]{1,0:T(8,128)(2,1)S(1)}, bf16[480,128]{1,0:T(8,128)(2,1)S(1)}, u32[]{:S(2)}, u32[]{:S(2)}) collective-permute-start(bf16[480,128]{1,0:T(8,128)(2,1)S(1)} %get-tuple-element.52), channel_id=1, source_target_pairs={{0,6},{2,0},{4,2},{6,4},{8,56},{10,58},{12,60},{14,62},{16,22},{18... | collective-permute-start | bytes 368648 | tf_op jit(solution)/shard_map/ppermute | solution.py:241
  65.9 6.5 %collective-permute-start.17 = (bf16[480,128]{1,0:T(8,128)(2,1)S(1)}, bf16[480,128]{1,0:T(8,128)(2,1)S(1)}, u32[]{:S(2)}, u32[]{:S(2)}) collective-permute-start(bf16[480,128]{1,0:T(8,128)(2,1)S(1)} %get-tuple-element.53), channel_id=1, source_target_pairs={{0,4},{2,6},{4,0},{6,2},{8,40},{10,42},{12,44},{14,46},{16,20},{18... | collective-permute-start | bytes 368648 | tf_op jit(solution)/shard_map/ppermute | solution.py:241
  65.9 7.4 %collective-permute-start.18 = (bf16[480,128]{1,0:T(8,128)(2,1)S(1)}, bf16[480,128]{1,0:T(8,128)(2,1)S(1)}, u32[]{:S(2)}, u32[]{:S(2)}) collective-permute-start(bf16[480,128]{1,0:T(8,128)(2,1)S(1)} %get-tuple-element.54), channel_id=1, source_target_pairs={{0,2},{2,4},{4,6},{6,0},{8,24},{10,26},{12,28},{14,30},{16,18},{18... | collective-permute-start | bytes 368648 | tf_op jit(solution)/shard_map/ppermute | solution.py:241

commit v6 on v4

--- a/solution.py
+++ b/solution.py
@@ -272,11 +272,6 @@
         (q1, q2, q3, q4, kv1, kv3, part0),
         spaces=[VM] * 4 + [ANY] * 3,
     )
-    (kv0_late,) = call(
-        after_kernel, "late", (sds((4, 2 * T, W), BF),), (kv0, mine), spaces=[VM, ANY]
-    )
-    kv2 = send_plane(kv0_late, 2, 1)
-
     sib = swap_cores(mine)
     (part1, part3), acc = tiles(
         "tiles13a",
@@ -284,6 +279,10 @@
         ((kv1, (0, 1), F32, None), (kv3, (0, 1), F32, None)),
         acc,
     )
+    (kv0_late,) = call(
+        after_kernel, "late", (sds((4, 2 * T, W), BF),), (kv0, part1), spaces=[VM, ANY]
+    )
+    kv2 = send_plane(kv0_late, 2, 1)
     qs = {0: chip, 1: mine, 2: sib}
     (out1, out3, part0), acc = tiles(
         "tiles130",

time: 74.1 us -> 74.3 us (level)
  no operation moved by 1% of the time
where the time goes in v6:
time: 74.3 us; the launch traced here: 74 us
  starting transfers between devices  37.9 us (51%)
  Pallas kernels  23.7 us (32%)
  waiting for transfers between devices  10.7 us (14%)
  local copies, waits for them, and re-layouts  0.89 us (1%)
  between operations  0.79 us (1%)
    pallas_call x15, Pallas kernels, call(): pl.pallas_call(kernel, name=name, out_shape=outs, in_specs=spaces or [VM]...  23.7 us
    ppermute x12, starting transfers between devices, send_plane(): return lax.ppermute(x, ('y', 'core', 'x'), pairs)  18 us
    ppermute x4, starting transfers between devices, send_z(): return lax.ppermute(x, ('zl', 'core', 'zh'), pairs)  11.1 us
    ppermute x12, waiting for transfers between devices, send_plane(): return lax.ppermute(x, ('y', 'core', 'x'), pairs)  9.23 us
    all_to_all x1, starting transfers between devices, exchange_z(): return lax.all_to_all(x, ('zl', 'zh'), 0, 0, tiled=True)  8.41 us
    ppermute x4, waiting for transfers between devices, send_z(): return lax.ppermute(x, ('zl', 'core', 'zh'), pairs)  1.5 us
  transfers between devices with their start and end apart: 20, of which 7 were waited for; matrix products, arithmetic and copies ran while one was open for 0% of the time, Pallas kernels for 29%

profile of v6, /device:TPU:32, one launch (start us, length us, event | category | flops | bytes accessed | tf_op | source)
XLA Modules:
  0.0 74.0 jit_solution(9620532345466472851)
XLA Ops:
  0.6 1.7 %pack.1 = (bf16[272,128]{1,0:T(8,128)(2,1)}, bf16[480,128]{1,0:T(8,128)(2,1)}) custom-call(bf16[128,128]{1,0:T(8,128)(2,1)} %q.1, bf16[128,128]{1,0:T(8,128)(2,1)} %g.1, bf16[128,128]{1,0:T(8,128)(2,1)} %o.1, f32[1,128]{1,0:T(1,128)} %bitcast.1, bf16[240,128]{1,0:T(8,128)(2,1)} %k.1, bf16[240,128]{1,0:T(8,128)(2,1)} %v.1), custom_call_target="tpu_custom_call" | custom-call | bytes 414208 | tf_op jit(solution)/shard_map/pack/pallas_call | solution.py:32
  2.3 0.1 collective-permute-start
  2.4 0.0 copy-start
  2.4 1.6 %collective-permute-start.5 = (bf16[480,128]{1,0:T(8,128)(2,1)}, bf16[480,128]{1,0:T(8,128)(2,1)S(1)}, u32[]{:S(2)}, u32[]{:S(2)}) collective-permute-start(bf16[480,128]{1,0:T(8,128)(2,1)} %get-tuple-element.29.k0), channel_id=1, source_target_pairs={{0,2},{2,4},{4,6},{6,0},{8,24},{10,26},{12,28},{14,30},{16,18},{18... | collective-permute-start | bytes 368648 | tf_op jit(solution)/shard_map/ppermute | solution.py:241
  4.0 2.7 %collective-permute-start.6 = (bf16[480,128]{1,0:T(8,128)(2,1)}, bf16[480,128]{1,0:T(8,128)(2,1)S(1)}, u32[]{:S(2)}, u32[]{:S(2)}) collective-permute-start(bf16[480,128]{1,0:T(8,128)(2,1)} %get-tuple-element.29.k0), channel_id=1, source_target_pairs={{0,4},{2,6},{4,0},{6,2},{8,40},{10,42},{12,44},{14,46},{16,20},{18... | collective-permute-start | bytes 368648 | tf_op jit(solution)/shard_map/ppermute | solution.py:241
  6.7 1.4 %collective-permute-start.7 = (bf16[480,128]{1,0:T(8,128)(2,1)}, bf16[480,128]{1,0:T(8,128)(2,1)S(1)}, u32[]{:S(2)}, u32[]{:S(2)}) collective-permute-start(bf16[480,128]{1,0:T(8,128)(2,1)} %get-tuple-element.29.k0), channel_id=1, source_target_pairs={{0,6},{2,0},{4,2},{6,4},{8,56},{10,58},{12,60},{14,62},{16,22},{18... | collective-permute-start | bytes 368648 | tf_op jit(solution)/shard_map/ppermute | solution.py:241
  8.1 0.0 collective-permute-done.q1
  8.1 0.9 %copy-done.1 = bf16[272,128]{1,0:T(8,128)(2,1)S(1)} copy-done((bf16[272,128]{1,0:T(8,128)(2,1)S(1)}, bf16[272,128]{1,0:T(8,128)(2,1)}, u32[]{:S(2)}) %copy-start.1) | copy-done | bytes 69656
  9.0 3.3 %collective-permute-start.2 = (bf16[2,272,128]{2,1,0:T(8,128)(2,1)S(1)}, bf16[2,272,128]{2,1,0:T(8,128)(2,1)S(1)}, u32[]{:S(2)}, u32[]{:S(2)}) collective-permute-start(bf16[2,272,128]{2,1,0:T(8,128)(2,1)S(1)} %chip.1.refs_0_), channel_id=1, source_target_pairs={{0,128},{8,137},{64,192},{72,201},{128,1},{136,8},{192,65},{200,72... | collective-permute-start | bytes 417800 | tf_op jit(solution)/shard_map/ppermute | solution.py:227
  12.4 3.1 %collective-permute-start.1 = (bf16[2,272,128]{2,1,0:T(8,128)(2,1)S(1)}, bf16[2,272,128]{2,1,0:T(8,128)(2,1)S(1)}, u32[]{:S(2)}, u32[]{:S(2)}) collective-permute-start(bf16[2,272,128]{2,1,0:T(8,128)(2,1)S(1)} %chip.1.refs_0_), channel_id=1, source_target_pairs={{0,64},{8,201},{64,128},{72,8},{128,192},{136,72},{192,1},{200,136... | collective-permute-start | bytes 417800 | tf_op jit(solution)/shard_map/ppermute | solution.py:227
  15.5 0.0 collective-permute-done.5.k1
  15.5 0.0 collective-permute-done.6.k2
  15.5 0.0 collective-permute-done.7.k3
  15.6 1.7 %collective-permute-start.8 = (bf16[4,480,128]{2,1,0:T(8,128)(2,1)S(1)}, bf16[4,480,128]{2,1,0:T(8,128)(2,1)S(1)}, u32[]{:S(2)}, u32[]{:S(2)}) collective-permute-start(bf16[4,480,128]{2,1,0:T(8,128)(2,1)S(1)} %join.1.refs_3_.x.refs_5_), channel_id=1, source_target_pairs={{0,16},{2,18},{4,20},{6,22},{8,10},{10,12},{12,14},{14,8},{16,32},... | collective-permute-start | bytes 1474568 | tf_op jit(solution)/shard_map/ppermute | solution.py:241
  17.2 1.7 %collective-permute-start.9 = (bf16[4,480,128]{2,1,0:T(8,128)(2,1)S(1)}, bf16[4,480,128]{2,1,0:T(8,128)(2,1)S(1)}, u32[]{:S(2)}, u32[]{:S(2)}) collective-permute-start(bf16[4,480,128]{2,1,0:T(8,128)(2,1)S(1)} %join.1.refs_3_.x.refs_5_), channel_id=1, source_target_pairs={{0,48},{2,50},{4,52},{6,54},{8,14},{10,8},{12,10},{14,12},{16,0},{... | collective-permute-start | bytes 1474568 | tf_op jit(solution)/shard_map/ppermute | solution.py:241
  18.9 0.1 collective-permute-done.2.q.refs_2_.q2
  19.0 0.9 %collective-permute-start.3 = (bf16[2,272,128]{2,1,0:T(8,128)(2,1)S(1)}, bf16[2,272,128]{2,1,0:T(8,128)(2,1)S(1)}, u32[]{:S(2)}, u32[]{:S(2)}) collective-permute-start(bf16[2,272,128]{2,1,0:T(8,128)(2,1)S(1)} %collective-permute-done.2.q.refs_2_.q2), channel_id=1, source_target_pairs={{0,64},{8,201},{64,128},{72,8},{128,192},{136,72},{192,1},{200,136... | collective-permute-start | bytes 417800 | tf_op jit(solution)/shard_map/ppermute | solution.py:227
  19.9 3.7 %collective-permute-start.4 = (bf16[1,272,128]{2,1,0:T(8,128)(2,1)S(1)}, bf16[1,272,128]{2,1,0:T(8,128)(2,1)S(1)}, u32[]{:S(2)}, u32[]{:S(2)}) collective-permute-start(bf16[1,272,128]{2,1,0:T(8,128)(2,1)S(1)} %first.1), channel_id=1, source_target_pairs={{0,128},{8,137},{64,192},{72,201},{128,1},{136,8},{192,65},{200,72... | collective-permute-start | bytes 208904 | tf_op jit(solution)/shard_map/ppermute | solution.py:227
  23.7 0.0 collective-permute-done.1.refs_1_.q1
  23.7 1.3 %tiles0e.1 = (f32[4,480,128]{2,1,0:T(8,128)S(1)}, f32[4,128,128]{2,1,0:T(8,128)S(1)}) custom-call(bf16[2,272,128]{2,1,0:T(8,128)(2,1)S(1)} %chip.1.refs_0_, bf16[2,272,128]{2,1,0:T(8,128)(2,1)S(1)} %collective-permute-done.1.refs_1_.q1, bf16[2,272,128]{2,1,0:T(8,128)(2,1)S(1)} %collective-permute-done.2.q.refs_2_.q2, ...), custom_call_target="tpu_custom_call" | custom-call | flops 629145600 | bytes 2154496 | tf_op jit(solution)/shard_map/tiles0e/pallas_call | solution.py:32
  25.0 1.3 %collective-permute-done.4.q4 = bf16[1,272,128]{2,1,0:T(8,128)(2,1)S(1)} collective-permute-done((bf16[1,272,128]{2,1,0:T(8,128)(2,1)S(1)}, bf16[1,272,128]{2,1,0:T(8,128)(2,1)S(1)}, u32[]{:S(2)}, u32[]{:S(2)}) %collective-permute-start.4) | collective-permute-done | bytes 69664 | tf_op jit(solution)/shard_map/ppermute | solution.py:227
  26.3 0.0 collective-permute-done.3.q3
  26.4 0.0 collective-permute-done.8.kv1.refs_2_.refs_3_
  26.4 0.3 collective-permute-start.10
  26.7 4.9 %tiles13a.1 = (f32[4,480,128]{2,1,0:T(8,128)S(1)}, f32[4,480,128]{2,1,0:T(8,128)S(1)}, f32[4,128,128]{2,1,0:T(8,128)S(1)}, f32[4,128,128]{2,1,0:T(8,128)S(1)}) custom-call(bf16[2,272,128]{2,1,0:T(8,128)(2,1)S(1)} %chip.1.refs_0_, bf16[7,272,128]{2,1,0:T(8,128)(2,1)S(1)} %gather.1.refs_1_, ...), custom_call_target="tpu_custom_call", output_to_operand_aliasing={{2}: (4, {})} | custom-call | flops 2516582400 | bytes 4362240 | tf_op jit(solution)/shard_map/tiles13a/pallas_call | solution.py:32
  31.7 2.7 %collective-permute-start.11 = (bf16[4,480,128]{2,1,0:T(8,128)(2,1)S(1)}, bf16[4,480,128]{2,1,0:T(8,128)(2,1)S(1)}, u32[]{:S(2)}, u32[]{:S(2)}) collective-permute-start(bf16[4,480,128]{2,1,0:T(8,128)(2,1)S(1)} %late.1), channel_id=1, source_target_pairs={{0,32},{2,34},{4,36},{6,38},{8,12},{10,14},{12,8},{14,10},{16,48},... | collective-permute-start | bytes 1474568 | tf_op jit(solution)/shard_map/ppermute | solution.py:241
  34.4 0.0 collective-permute-done.10.refs_2_
  34.4 7.5 %tiles130.1 = (bf16[4,480,128]{2,1,0:T(8,128)(2,1)S(1)}, bf16[4,480,128]{2,1,0:T(8,128)(2,1)S(1)}, f32[4,480,128]{2,1,0:T(8,128)S(1)}, f32[4,128,128]{2,1,0:T(8,...) custom-call(bf16[2,272,128]{2,1,0:T(8,128)(2,1)S(1)} %chip.1.refs_0_, ...), custom_call_target="tpu_custom_call", output_to_operand_aliasing={{3}: (6, {}), {2}: (9, {})} | custom-call | flops 3774873600 | bytes 8552448 | tf_op jit(solution)/shard_map/tiles130/pallas_call | solution.py:32
  41.9 1.6 %collective-permute-start.12 = (bf16[4,480,128]{2,1,0:T(8,128)(2,1)S(1)}, bf16[4,480,128]{2,1,0:T(8,128)(2,1)S(1)}, u32[]{:S(2)}, u32[]{:S(2)}) collective-permute-start(bf16[4,480,128]{2,1,0:T(8,128)(2,1)S(1)} %get-tuple-element.43), channel_id=1, source_target_pairs={{0,48},{2,50},{4,52},{6,54},{8,14},{10,8},{12,10},{14,12},{16,0},{... | collective-permute-start | bytes 1474568 | tf_op jit(solution)/shard_map/ppermute | solution.py:241
  43.5 0.7 collective-permute-start.13
  44.2 0.0 collective-permute-done.11.refs_3_
  44.2 4.9 %tiles2.1 = (bf16[4,480,128]{2,1,0:T(8,128)(2,1)S(1)}, f32[4,128,128]{2,1,0:T(8,128)S(1)}, f32[4,128,128]{2,1,0:T(8,128)S(1)}, f32[4,128,128]{2,1,0:T(8,128)S(1)}, f32[4,128,128]{2,1,0:T(8,128)S(1)}) custom-call(bf16[2,272,128]{2,1,0:T(8,128)(2,1)S(1)} %chip.1.refs_0_, ...), custom_call_target="tpu_custom_call", output_to_operand_aliasing={{1}: (4, {}), {2}: (5, {}), {3}: (6, {}), {4}: (7, {})} | custom-call | flops 2516582400 | bytes 4194304 | tf_op jit(solution)/shard_map/tiles2/pallas_call | solution.py:32
  49.2 0.1 collective-permute-start.14
  49.3 1.2 %collective-permute-start.15 = (bf16[4,480,128]{2,1,0:T(8,128)(2,1)S(1)}, bf16[4,480,128]{2,1,0:T(8,128)(2,1)S(1)}, u32[]{:S(2)}, u32[]{:S(2)}) collective-permute-start(bf16[4,480,128]{2,1,0:T(8,128)(2,1)S(1)} %get-tuple-element.48), channel_id=1, source_target_pairs={{0,32},{2,34},{4,36},{6,38},{8,12},{10,14},{12,8},{14,10},{16,48},... | collective-permute-start | bytes 1474568 | tf_op jit(solution)/shard_map/ppermute | solution.py:241
  50.4 0.6 collective-permute-done.12.refs_6_.b1
  51.0 2.6 %collective-permute-done.13.refs_7_.b3 = bf16[4,480,128]{2,1,0:T(8,128)(2,1)S(1)} collective-permute-done((bf16[4,480,128]{2,1,0:T(8,128)(2,1)S(1)}, bf16[4,480,128]{2,1,0:T(8,128)(2,1)S(1)}, u32[]{:S(2)}, u32[]{:S(2)}) %collective-permute-start.13) | collective-permute-done | bytes 491552 | tf_op jit(solution)/shard_map/ppermute | solution.py:241
  53.6 1.4 %tiles0.1 = (f32[4,480,128]{2,1,0:T(8,128)S(1)}, f32[4,128,128]{2,1,0:T(8,128)S(1)}) custom-call(bf16[2,272,128]{2,1,0:T(8,128)(2,1)S(1)} %chip.1.refs_0_, bf16[7,272,128]{2,1,0:T(8,128)(2,1)S(1)} %gather.1.refs_1_, bf16[7,272,128]{2,1,0:T(8,128)(2,1)S(1)} %collective-permute-done.10.refs_2_, ...), custom_call_target="tpu_custom_call", output_to_operand_aliasing={{1}: (4, {}), {0}: (5, {})} | custom-call | flops 629145600 | bytes 5079040 | tf_op jit(solution)/shard_map/tiles0/pallas_call | solution.py:32
  55.0 0.8 %halves.1.after = bf16[8,128,128]{2,1,0:T(8,128)(2,1)} custom-call(f32[4,128,128]{2,1,0:T(8,128)S(1)} %get-tuple-element.39.g0, f32[4,128,128]{2,1,0:T(8,128)S(1)} %get-tuple-element.40.g1, f32[4,128,128]{2,1,0:T(8,128)S(1)} %get-tuple-element.45.g2, f32[8,128,128]{2,1,0:T(8,128)S(1)} %collective-permute-done.14.got), custom_call_target="tpu_custom_call" | custom-call | bytes 1572864 | tf_op jit(solution)/shard_map/halves/pallas_call | solution.py:32
  55.8 8.4 %all-to-all-start = ((bf16[8,128,128]{2,1,0:T(8,128)(2,1)}), bf16[8,128,128]{2,1,0:T(8,128)(2,1)S(1)}, u32[]{:S(2)}, u32[]{:S(2)}) async-start(bf16[8,128,128]{2,1,0:T(8,128)(2,1)} %halves.1.after), calls=%async_computation | async-start | bytes 524288 | tf_op jit(solution)/shard_map/all_to_all | solution.py:231
  64.2 0.0 collective-permute-done.15.b2
  64.2 0.2 merge.1
  64.4 0.2 collective-permute-start.16
  64.6 2.5 %collective-permute-start.17 = (bf16[480,128]{1,0:T(8,128)(2,1)S(1)}, bf16[480,128]{1,0:T(8,128)(2,1)S(1)}, u32[]{:S(2)}, u32[]{:S(2)}) collective-permute-start(bf16[480,128]{1,0:T(8,128)(2,1)S(1)} %get-tuple-element.51), channel_id=1, source_target_pairs={{0,4},{2,6},{4,0},{6,2},{8,40},{10,42},{12,44},{14,46},{16,20},{18... | collective-permute-start | bytes 368648 | tf_op jit(solution)/shard_map/ppermute | solution.py:241
  67.2 0.0 collective-permute-start.18
  67.2 2.2 %collective-permute-done.16.f1 = bf16[480,128]{1,0:T(8,128)(2,1)S(1)} collective-permute-done((bf16[480,128]{1,0:T(8,128)(2,1)S(1)}, bf16[480,128]{1,0:T(8,128)(2,1)S(1)}, u32[]{:S(2)}, u32[]{:S(2)}) %collective-permute-start.16) | collective-permute-done | bytes 122912 | tf_op jit(solution)/shard_map/ppermute | solution.py:241
  69.4 1.6 %collective-permute-done.17.f2 = bf16[480,128]{1,0:T(8,128)(2,1)S(1)} collective-permute-done((bf16[480,128]{1,0:T(8,128)(2,1)S(1)}, bf16[480,128]{1,0:T(8,128)(2,1)S(1)}, u32[]{:S(2)}, u32[]{:S(2)}) %collective-permute-start.17) | collective-permute-done | bytes 122912 | tf_op jit(solution)/shard_map/ppermute | solution.py:241
  71.0 2.2 %collective-permute-done.18.f3 = bf16[480,128]{1,0:T(8,128)(2,1)S(1)} collective-permute-done((bf16[480,128]{1,0:T(8,128)(2,1)S(1)}, bf16[480,128]{1,0:T(8,128)(2,1)S(1)}, u32[]{:S(2)}, u32[]{:S(2)}) %collective-permute-start.18) | collective-permute-done | bytes 122912 | tf_op jit(solution)/shard_map/ppermute | solution.py:241
  73.3 0.8 %last.1 = (f32[128,128]{1,0:T(8,128)}, f32[240,128]{1,0:T(8,128)}, f32[240,128]{1,0:T(8,128)}) custom-call(bf16[8,128,128]{2,1,0:T(8,128)(2,1)S(1)} %all-to-all-done.u, f32[480,128]{1,0:T(8,128)S(1)} %get-tuple-element.49.own, bf16[480,128]{1,0:T(8,128)(2,1)S(1)} %collective-permute-done.16.f1, bf16[480,128]{1,0:T(8,128)(2,1)S(1)} %collective-permute-done.17.f2, ...), custom_call_target="tpu_custom_call" | custom-call | bytes 1187840 | tf_op jit(solution)/shard_map/last/pallas_call | solution.py:32
  (11 shorter events, 0.2 us)
Async XLA Ops:
  2.3 5.8 %collective-permute-start = (bf16[272,128]{1,0:T(8,128)(2,1)}, bf16[272,128]{1,0:T(8,128)(2,1)S(1)}, u32[]{:S(2)}, u32[]{:S(2)}) collective-permute-start(bf16[272,128]{1,0:T(8,128)(2,1)} %get-tuple-element.28.q0), channel_id=1, source_target_pairs={{0,8},{8,0},{1,9},{9,1},{2,10},{10,2},{3,11},{11,3},{4,12},{12,4},... | collective-permute-start | bytes 208904 | tf_op jit(solution)/shard_map/ppermute | solution.py:219
  2.4 13.1 %copy-start = (bf16[480,128]{1,0:T(8,128)(2,1)S(1)}, bf16[480,128]{1,0:T(8,128)(2,1)}, u32[]{:S(2)}) copy-start(bf16[480,128]{1,0:T(8,128)(2,1)} %get-tuple-element.29.k0) | copy-start | bytes 368644
  2.4 13.1 %collective-permute-start.5 = (bf16[480,128]{1,0:T(8,128)(2,1)}, bf16[480,128]{1,0:T(8,128)(2,1)S(1)}, u32[]{:S(2)}, u32[]{:S(2)}) collective-permute-start(bf16[480,128]{1,0:T(8,128)(2,1)} %get-tuple-element.29.k0), channel_id=1, source_target_pairs={{0,2},{2,4},{4,6},{6,0},{8,24},{10,26},{12,28},{14,30},{16,18},{18... | collective-permute-start | bytes 368648 | tf_op jit(solution)/shard_map/ppermute | solution.py:241
  4.0 11.6 %collective-permute-start.6 = (bf16[480,128]{1,0:T(8,128)(2,1)}, bf16[480,128]{1,0:T(8,128)(2,1)S(1)}, u32[]{:S(2)}, u32[]{:S(2)}) collective-permute-start(bf16[480,128]{1,0:T(8,128)(2,1)} %get-tuple-element.29.k0), channel_id=1, source_target_pairs={{0,4},{2,6},{4,0},{6,2},{8,40},{10,42},{12,44},{14,46},{16,20},{18... | collective-permute-start | bytes 368648 | tf_op jit(solution)/shard_map/ppermute | solution.py:241
  6.7 8.8 %collective-permute-start.7 = (bf16[480,128]{1,0:T(8,128)(2,1)}, bf16[480,128]{1,0:T(8,128)(2,1)S(1)}, u32[]{:S(2)}, u32[]{:S(2)}) collective-permute-start(bf16[480,128]{1,0:T(8,128)(2,1)} %get-tuple-element.29.k0), channel_id=1, source_target_pairs={{0,6},{2,0},{4,2},{6,4},{8,56},{10,58},{12,60},{14,62},{16,22},{18... | collective-permute-start | bytes 368648 | tf_op jit(solution)/shard_map/ppermute | solution.py:241
  8.1 0.9 %copy-start.1 = (bf16[272,128]{1,0:T(8,128)(2,1)S(1)}, bf16[272,128]{1,0:T(8,128)(2,1)}, u32[]{:S(2)}) copy-start(bf16[272,128]{1,0:T(8,128)(2,1)} %get-tuple-element.28.q0) | copy-start | bytes 208900
  9.0 10.0 %collective-permute-start.2 = (bf16[2,272,128]{2,1,0:T(8,128)(2,1)S(1)}, bf16[2,272,128]{2,1,0:T(8,128)(2,1)S(1)}, u32[]{:S(2)}, u32[]{:S(2)}) collective-permute-start(bf16[2,272,128]{2,1,0:T(8,128)(2,1)S(1)} %chip.1.refs_0_), channel_id=1, source_target_pairs={{0,128},{8,137},{64,192},{72,201},{128,1},{136,8},{192,65},{200,72... | collective-permute-start | bytes 417800 | tf_op jit(solution)/shard_map/ppermute | solution.py:227
  12.4 11.3 %collective-permute-start.1 = (bf16[2,272,128]{2,1,0:T(8,128)(2,1)S(1)}, bf16[2,272,128]{2,1,0:T(8,128)(2,1)S(1)}, u32[]{:S(2)}, u32[]{:S(2)}) collective-permute-start(bf16[2,272,128]{2,1,0:T(8,128)(2,1)S(1)} %chip.1.refs_0_), channel_id=1, source_target_pairs={{0,64},{8,201},{64,128},{72,8},{128,192},{136,72},{192,1},{200,136... | collective-permute-start | bytes 417800 | tf_op jit(solution)/shard_map/ppermute | solution.py:227
  15.6 10.8 %collective-permute-start.8 = (bf16[4,480,128]{2,1,0:T(8,128)(2,1)S(1)}, bf16[4,480,128]{2,1,0:T(8,128)(2,1)S(1)}, u32[]{:S(2)}, u32[]{:S(2)}) collective-permute-start(bf16[4,480,128]{2,1,0:T(8,128)(2,1)S(1)} %join.1.refs_3_.x.refs_5_), channel_id=1, source_target_pairs={{0,16},{2,18},{4,20},{6,22},{8,10},{10,12},{12,14},{14,8},{16,32},... | collective-permute-start | bytes 1474568 | tf_op jit(solution)/shard_map/ppermute | solution.py:241
  17.2 9.1 %collective-permute-start.9 = (bf16[4,480,128]{2,1,0:T(8,128)(2,1)S(1)}, bf16[4,480,128]{2,1,0:T(8,128)(2,1)S(1)}, u32[]{:S(2)}, u32[]{:S(2)}) collective-permute-start(bf16[4,480,128]{2,1,0:T(8,128)(2,1)S(1)} %join.1.refs_3_.x.refs_5_), channel_id=1, source_target_pairs={{0,48},{2,50},{4,52},{6,54},{8,14},{10,8},{12,10},{14,12},{16,0},{... | collective-permute-start | bytes 1474568 | tf_op jit(solution)/shard_map/ppermute | solution.py:241
  19.0 7.3 %collective-permute-start.3 = (bf16[2,272,128]{2,1,0:T(8,128)(2,1)S(1)}, bf16[2,272,128]{2,1,0:T(8,128)(2,1)S(1)}, u32[]{:S(2)}, u32[]{:S(2)}) collective-permute-start(bf16[2,272,128]{2,1,0:T(8,128)(2,1)S(1)} %collective-permute-done.2.q.refs_2_.q2), channel_id=1, source_target_pairs={{0,64},{8,201},{64,128},{72,8},{128,192},{136,72},{192,1},{200,136... | collective-permute-start | bytes 417800 | tf_op jit(solution)/shard_map/ppermute | solution.py:227
  19.9 6.4 %collective-permute-start.4 = (bf16[1,272,128]{2,1,0:T(8,128)(2,1)S(1)}, bf16[1,272,128]{2,1,0:T(8,128)(2,1)S(1)}, u32[]{:S(2)}, u32[]{:S(2)}) collective-permute-start(bf16[1,272,128]{2,1,0:T(8,128)(2,1)S(1)} %first.1), channel_id=1, source_target_pairs={{0,128},{8,137},{64,192},{72,201},{128,1},{136,8},{192,65},{200,72... | collective-permute-start | bytes 208904 | tf_op jit(solution)/shard_map/ppermute | solution.py:227
  26.4 8.0 %collective-permute-start.10 = (bf16[7,272,128]{2,1,0:T(8,128)(2,1)S(1)}, bf16[7,272,128]{2,1,0:T(8,128)(2,1)S(1)}, u32[]{:S(2)}, u32[]{:S(2)}) collective-permute-start(bf16[7,272,128]{2,1,0:T(8,128)(2,1)S(1)} %gather.1.refs_1_), channel_id=1, source_target_pairs={{0,8},{8,0},{1,9},{9,1},{2,10},{10,2},{3,11},{11,3},{4,12},{12,4},... | collective-permute-start | bytes 1462280 | tf_op jit(solution)/shard_map/ppermute | solution.py:219
  31.7 12.5 %collective-permute-start.11 = (bf16[4,480,128]{2,1,0:T(8,128)(2,1)S(1)}, bf16[4,480,128]{2,1,0:T(8,128)(2,1)S(1)}, u32[]{:S(2)}, u32[]{:S(2)}) collective-permute-start(bf16[4,480,128]{2,1,0:T(8,128)(2,1)S(1)} %late.1), channel_id=1, source_target_pairs={{0,32},{2,34},{4,36},{6,38},{8,12},{10,14},{12,8},{14,10},{16,48},... | collective-permute-start | bytes 1474568 | tf_op jit(solution)/shard_map/ppermute | solution.py:241
  41.9 9.1 %collective-permute-start.12 = (bf16[4,480,128]{2,1,0:T(8,128)(2,1)S(1)}, bf16[4,480,128]{2,1,0:T(8,128)(2,1)S(1)}, u32[]{:S(2)}, u32[]{:S(2)}) collective-permute-start(bf16[4,480,128]{2,1,0:T(8,128)(2,1)S(1)} %get-tuple-element.43), channel_id=1, source_target_pairs={{0,48},{2,50},{4,52},{6,54},{8,14},{10,8},{12,10},{14,12},{16,0},{... | collective-permute-start | bytes 1474568 | tf_op jit(solution)/shard_map/ppermute | solution.py:241
  43.5 10.0 %collective-permute-start.13 = (bf16[4,480,128]{2,1,0:T(8,128)(2,1)S(1)}, bf16[4,480,128]{2,1,0:T(8,128)(2,1)S(1)}, u32[]{:S(2)}, u32[]{:S(2)}) collective-permute-start(bf16[4,480,128]{2,1,0:T(8,128)(2,1)S(1)} %get-tuple-element.44), channel_id=1, source_target_pairs={{0,16},{2,18},{4,20},{6,22},{8,10},{10,12},{12,14},{14,8},{16,32},... | collective-permute-start | bytes 1474568 | tf_op jit(solution)/shard_map/ppermute | solution.py:241
  49.2 5.9 %collective-permute-start.14 = (f32[8,128,128]{2,1,0:T(8,128)S(1)}, f32[8,128,128]{2,1,0:T(8,128)S(1)}, u32[]{:S(2)}, u32[]{:S(2)}) collective-permute-start(f32[8,128,128]{2,1,0:T(8,128)S(1)} %others.1), channel_id=1, source_target_pairs={{0,8},{8,0},{1,9},{9,1},{2,10},{10,2},{3,11},{11,3},{4,12},{12,4},... | collective-permute-start | bytes 1572872 | tf_op jit(solution)/shard_map/ppermute | solution.py:219
  49.3 15.0 %collective-permute-start.15 = (bf16[4,480,128]{2,1,0:T(8,128)(2,1)S(1)}, bf16[4,480,128]{2,1,0:T(8,128)(2,1)S(1)}, u32[]{:S(2)}, u32[]{:S(2)}) collective-permute-start(bf16[4,480,128]{2,1,0:T(8,128)(2,1)S(1)} %get-tuple-element.48), channel_id=1, source_target_pairs={{0,32},{2,34},{4,36},{6,38},{8,12},{10,14},{12,8},{14,10},{16,48},... | collective-permute-start | bytes 1474568 | tf_op jit(solution)/shard_map/ppermute | solution.py:241
  55.8 17.5 %all-to-all-start = ((bf16[8,128,128]{2,1,0:T(8,128)(2,1)}), bf16[8,128,128]{2,1,0:T(8,128)(2,1)S(1)}, u32[]{:S(2)}, u32[]{:S(2)}) async-start(bf16[8,128,128]{2,1,0:T(8,128)(2,1)} %halves.1.after), calls=%async_computation | async-start | bytes 524288 | tf_op jit(solution)/shard_map/all_to_all | solution.py:231
  64.4 5.0 %collective-permute-start.16 = (bf16[480,128]{1,0:T(8,128)(2,1)S(1)}, bf16[480,128]{1,0:T(8,128)(2,1)S(1)}, u32[]{:S(2)}, u32[]{:S(2)}) collective-permute-start(bf16[480,128]{1,0:T(8,128)(2,1)S(1)} %get-tuple-element.50), channel_id=1, source_target_pairs={{0,6},{2,0},{4,2},{6,4},{8,56},{10,58},{12,60},{14,62},{16,22},{18... | collective-permute-start | bytes 368648 | tf_op jit(solution)/shard_map/ppermute | solution.py:241
  64.6 6.4 %collective-permute-start.17 = (bf16[480,128]{1,0:T(8,128)(2,1)S(1)}, bf16[480,128]{1,0:T(8,128)(2,1)S(1)}, u32[]{:S(2)}, u32[]{:S(2)}) collective-permute-start(bf16[480,128]{1,0:T(8,128)(2,1)S(1)} %get-tuple-element.51), channel_id=1, source_target_pairs={{0,4},{2,6},{4,0},{6,2},{8,40},{10,42},{12,44},{14,46},{16,20},{18... | collective-permute-start | bytes 368648 | tf_op jit(solution)/shard_map/ppermute | solution.py:241
  67.2 6.1 %collective-permute-start.18 = (bf16[480,128]{1,0:T(8,128)(2,1)S(1)}, bf16[480,128]{1,0:T(8,128)(2,1)S(1)}, u32[]{:S(2)}, u32[]{:S(2)}) collective-permute-start(bf16[480,128]{1,0:T(8,128)(2,1)S(1)} %get-tuple-element.52), channel_id=1, source_target_pairs={{0,2},{2,4},{4,6},{6,0},{8,24},{10,26},{12,28},{14,30},{16,18},{18... | collective-permute-start | bytes 368648 | tf_op jit(solution)/shard_map/ppermute | solution.py:241
